TPU v7x, 32 devices: a whole 2x2x4 slice. The times are simulated.
32 devices in a mesh: dp: 8 (over y, x, core), ctx: 4 (over z).
Axes of the slice: x: 2, y: 2, z: 4, core: 2. Of those that a mesh axis runs over, the one named last changes fastest.
Arguments:
- tokens: bfloat16 [8192, 2048], P(('dp', 'ctx')), may hold values from -6 to 6
- cotangent: bfloat16 [8192, 2048], P(('dp', 'ctx')), may hold values from -6 to 6
- segments: int32 [8192], P(('dp', 'ctx')), may hold values from 0 to 1023, as said below
- attn_weight: float32 [2048, 4, 2048], P(('dp', 'ctx'))
- attn_first: float32 [2048, 4, 2048], P(('dp', 'ctx'))
- attn_second: float32 [2048, 4, 2048], P(('dp', 'ctx'))
- mlp_weight: float32 [8192, 3, 2048], P(('dp', 'ctx'))
- mlp_first: float32 [8192, 3, 2048], P(('dp', 'ctx'))
- mlp_second: float32 [8192, 3, 2048], P(('dp', 'ctx'))
- gain_weight: float32 [2, 2048], P(None, ('dp', 'ctx')), may hold values from 0.5 to 1.5
- gain_first: float32 [2, 2048], P(None, ('dp', 'ctx'))
- gain_second: float32 [2, 2048], P(None, ('dp', 'ctx'))
Outputs:
- output: bfloat16 [8192, 2048], P(('dp', 'ctx'))
- grad_input: float32 [8192, 2048], P(('dp', 'ctx'))
- attn_first_new: float32 [2048, 4, 2048], P(('dp', 'ctx'))
- attn_second_new: float32 [2048, 3, 2048], P(('dp', 'ctx'))
- projection_second: float32 [2048, 2048], P(('dp', 'ctx'))
- attn_weight_new: float32 [2048, 4, 2048], P(('dp', 'ctx'))
- mlp_first_new: float32 [8192, 3, 2048], P(('dp', 'ctx'))
- mlp_second_new: float32 [8192, 3, 2048], P(('dp', 'ctx'))
- mlp_weight_new: float32 [8192, 3, 2048], P(('dp', 'ctx'))
- gain_first_new: float32 [2, 2048], P(None, ('dp', 'ctx'))
- gain_second_new: float32 [2, 2048], P(None, ('dp', 'ctx'))
- gain_weight_new: float32 [2, 2048], P(None, ('dp', 'ctx'))
Inputs may be any that keep to these rules, and one draw needn't show every extreme that they name: `segments`: within each sequence of 1024 tokens the numbers start at 0, never fall, and the last document is numbered 1024 - 1; equal numbers mark one document. In every sequence one document begins within the first 256 tokens and ends within the last 256 tokens.
All inputs are finite; a program needn't handle non-finite values.
Results may differ from a plain program's by a relative error of at most 0.014.
Values may be sent and summed in bfloat16 or wider, within the bound.
A program may use at most 1.125 GiB of HBM per device.

v0:
```python
import math

import jax
import jax.numpy as jnp
from jax import lax
from jax.sharding import PartitionSpec as P

D = 2048
HEADS = 32
HD = 64
FF = 8192
STEP = 10


NORM_EPS = 1e-05
ROPE_BASE = 130000.0
BETA_ONE = 0.9
BETA_TWO = 0.95
ADAM_EPS = 1e-08
WEIGHT_DECAY = 0.1
RATE_FACTOR = 1.5
GAIN_RATE = 0.6
OUTPUT_BOOST = 12.0
MASKED = -1e30


def rope_tables(position):
    halved = HD // 2
    frequency = ROPE_BASE ** (-(jnp.arange(halved, dtype=jnp.float32) * 2.0 / HD))
    angle = position.astype(jnp.float32)[:, None] * frequency[None, :]
    return (
        jnp.concatenate([jnp.cos(angle), jnp.cos(angle)], -1),
        jnp.concatenate([jnp.sin(angle), jnp.sin(angle)], -1),
    )


def rotate(values, cosine, sine, direction):
    halved = HD // 2
    turned = jnp.concatenate([-values[..., halved:], values[..., :halved]], -1)
    return values * cosine[:, None, :] + direction * turned * sine[:, None, :]


def norm_scale(values):
    return lax.rsqrt(jnp.mean(values * values, -1, keepdims=True) + NORM_EPS)


def norm_back(grad_normed, values, scale, gain):
    weighted = grad_normed * gain
    grad_values = scale * (
        weighted - values * scale * scale * jnp.mean(weighted * values, -1, keepdims=True)
    )
    return (grad_values, jnp.sum(grad_normed * values * scale, 0))


def adam_update(master, first, second, grad, rate, decay):
    first_new = BETA_ONE * first + (1.0 - BETA_ONE) * grad
    second_new = BETA_TWO * second + (1.0 - BETA_TWO) * grad * grad
    direction = (
        first_new
        / (1.0 - BETA_ONE**STEP)
        / (jnp.sqrt(second_new / (1.0 - BETA_TWO**STEP)) + ADAM_EPS)
    )
    return (first_new, second_new, master - rate * (direction + decay * master))


def masked_scores(query_block, key_block, allowed):
    scores = jnp.einsum(
        "qhe,khe->hqk", query_block, key_block, preferred_element_type=jnp.float32
    ) * HD ** (-0.5)
    return jnp.where(allowed[None], scores, MASKED)


def attention_forward(query, key_all, value_all, allowed):
    group = math.gcd(HEADS, 4)
    length = query.shape[0]

    def head_block(index, state):
        outputs, log_sums = state
        first_head = index * group
        query_block = lax.dynamic_slice_in_dim(query, first_head, group, 1)
        key_block = lax.dynamic_slice_in_dim(key_all, first_head, group, 1)
        value_block = lax.dynamic_slice_in_dim(value_all, first_head, group, 1)
        scores = masked_scores(query_block, key_block, allowed)
        highest = jnp.max(scores, -1, keepdims=True)
        shifted = jnp.exp(scores - highest)
        totals = jnp.sum(shifted, -1, keepdims=True)
        weights = (shifted / totals).astype(jnp.bfloat16)
        result = jnp.einsum(
            "hqk,khe->qhe", weights, value_block, preferred_element_type=jnp.float32
        )
        outputs = lax.dynamic_update_slice_in_dim(outputs, result, first_head, 1)
        log_sums = lax.dynamic_update_slice_in_dim(
            log_sums, highest[..., 0] + jnp.log(totals[..., 0]), first_head, 0
        )
        return (outputs, log_sums)

    start_state = (
        jnp.zeros((length, HEADS, HD), jnp.float32),
        jnp.zeros((HEADS, length), jnp.float32),
    )
    return lax.fori_loop(0, HEADS // group, head_block, start_state)


def attention_backward(query, key_all, value_all, allowed, log_sums, grad_attended):
    group = math.gcd(HEADS, 4)
    length = query.shape[0]
    key_count = key_all.shape[0]
    scale = HD ** (-0.5)

    def head_block(index, state):
        grad_query, grad_key, grad_value = state
        first_head = index * group
        query_block = lax.dynamic_slice_in_dim(query, first_head, group, 1)
        key_block = lax.dynamic_slice_in_dim(key_all, first_head, group, 1)
        value_block = lax.dynamic_slice_in_dim(value_all, first_head, group, 1)
        sums_block = lax.dynamic_slice_in_dim(log_sums, first_head, group, 0)
        grad_block = lax.dynamic_slice_in_dim(grad_attended, first_head, group, 1)
        scores = masked_scores(query_block, key_block, allowed)
        probs = jnp.exp(scores - sums_block[..., None])
        grad_probs = jnp.einsum(
            "qhe,khe->hqk", grad_block, value_block, preferred_element_type=jnp.float32
        )
        inner_sum = jnp.sum(probs * grad_probs, -1, keepdims=True)
        grad_scores = (probs * (grad_probs - inner_sum)).astype(jnp.bfloat16)
        query_part = (
            jnp.einsum("hqk,khe->qhe", grad_scores, key_block, preferred_element_type=jnp.float32)
            * scale
        )
        key_part = (
            jnp.einsum("hqk,qhe->khe", grad_scores, query_block, preferred_element_type=jnp.float32)
            * scale
        )
        value_part = jnp.einsum(
            "hqk,qhe->khe",
            probs.astype(jnp.bfloat16),
            grad_block,
            preferred_element_type=jnp.float32,
        )
        grad_query = lax.dynamic_update_slice_in_dim(grad_query, query_part, first_head, 1)
        grad_key = lax.dynamic_update_slice_in_dim(grad_key, key_part, first_head, 1)
        grad_value = lax.dynamic_update_slice_in_dim(grad_value, value_part, first_head, 1)
        return (grad_query, grad_key, grad_value)

    start_state = (
        jnp.zeros((length, HEADS, HD), jnp.float32),
        jnp.zeros((key_count, HEADS, HD), jnp.float32),
        jnp.zeros((key_count, HEADS, HD), jnp.float32),
    )
    return lax.fori_loop(0, HEADS // group, head_block, start_state)


def column_slices(columns):
    return tuple((values for values in columns))


def reduce_rows(term, columns):
    return lax.psum_scatter(
        term(column_slices(columns)), ("dp", "ctx"), scatter_dimension=0, tiled=True
    )


def local(
    tokens,
    cotangent,
    segments,
    attn_weight,
    attn_first,
    attn_second,
    mlp_weight,
    mlp_first,
    mlp_second,
    gain_weight,
    gain_first,
    gain_second,
):
    local_rows = tokens.shape[0]
    attn_all, gain_all = (
        lax.all_gather(attn_weight.astype(jnp.bfloat16), ("dp", "ctx"), axis=0, tiled=True),
        lax.all_gather(gain_weight.astype(jnp.bfloat16), ("dp", "ctx"), axis=1, tiled=True),
    )
    gain_values = gain_all.astype(jnp.float32)
    mlp_low = mlp_weight.astype(jnp.bfloat16)
    source = tokens.astype(jnp.float32)
    position = lax.axis_index("ctx") * local_rows + jnp.arange(local_rows, dtype=jnp.int32)
    cosine, sine = rope_tables(position)
    scale_one = norm_scale(source)
    normed = (source * scale_one * gain_values[0]).astype(jnp.bfloat16)
    projected = jnp.einsum(
        "td,fkd->tkf", normed, attn_all[:, :3, :], preferred_element_type=jnp.float32
    )
    query = rotate(projected[:, 0].reshape(local_rows, HEADS, HD), cosine, sine, 1.0).astype(
        jnp.bfloat16
    )
    key_own = rotate(projected[:, 1].reshape(local_rows, HEADS, HD), cosine, sine, 1.0).astype(
        jnp.bfloat16
    )
    value_own = projected[:, 2].astype(jnp.bfloat16)
    key_flat, value_flat, segment_all = (
        lax.all_gather(key_own.reshape(local_rows, D), "ctx", axis=0, tiled=True),
        lax.all_gather(value_own, "ctx", axis=0, tiled=True),
        lax.all_gather(segments, "ctx", axis=0, tiled=True),
    )
    key_count = key_flat.shape[0]
    key_all = key_flat.reshape(key_count, HEADS, HD)
    value_all = value_flat.reshape(key_count, HEADS, HD)
    allowed = (jnp.arange(key_count, dtype=jnp.int32)[None, :] <= position[:, None]) & (
        segment_all[None, :] == segments[:, None]
    )
    attended_raw, log_sums = attention_forward(query, key_all, value_all, allowed)
    attended = attended_raw.reshape(local_rows, D).astype(jnp.bfloat16)
    branch = jnp.dot(attended, attn_all[:, 3, :], preferred_element_type=jnp.float32)
    middle = source + branch
    scale_two = norm_scale(middle)
    normed_two = (middle * scale_two * gain_values[1]).astype(jnp.bfloat16)
    piece = lax.all_gather(mlp_low, ("dp", "ctx"), axis=0, tiled=True)
    gate_up = jnp.einsum(
        "td,fkd->tkf", normed_two, piece[:, :2, :], preferred_element_type=jnp.float32
    )
    gate_part = gate_up[:, 0]
    up_part = gate_up[:, 1]
    hidden_part = (jax.nn.silu(gate_part) * up_part).astype(jnp.bfloat16)
    summed = jnp.dot(hidden_part, piece[:, 2, :], preferred_element_type=jnp.float32)
    gate_rows = gate_part
    up_rows = up_part
    hidden_rows = hidden_part
    output = (middle + summed).astype(jnp.bfloat16)
    grad_output = cotangent.astype(jnp.float32)
    piece = lax.all_gather(mlp_low, ("dp", "ctx"), axis=0, tiled=True)
    gate_part = gate_rows
    up_part = up_rows
    grad_hidden = lax.dot_general(
        cotangent, piece[:, 2, :], (((1,), (1,)), ((), ())), preferred_element_type=jnp.float32
    )
    sigmoid_gate = jax.nn.sigmoid(gate_part)
    dgate = (
        grad_hidden * up_part * sigmoid_gate * (1.0 + gate_part * (1.0 - sigmoid_gate))
    ).astype(jnp.bfloat16)
    dup = (grad_hidden * gate_part * sigmoid_gate).astype(jnp.bfloat16)
    stacked = jnp.stack([dgate, dup], 1)
    grad_normed_two = jnp.einsum(
        "tkf,fkd->td", stacked, piece[:, :2, :], preferred_element_type=jnp.float32
    )
    grad_normed_two, dgate_all, dup_all = (grad_normed_two, dgate, dup)

    def mlp_term(pieces):
        dgate_part, dup_part, hidden_part = pieces
        inputs_part = jnp.einsum(
            "tkc,td->ckd",
            jnp.stack([dgate_part, dup_part], 1),
            normed_two,
            preferred_element_type=jnp.float32,
        )
        down_part = lax.dot_general(
            hidden_part, cotangent, (((0,), (0,)), ((), ())), preferred_element_type=jnp.float32
        )
        return jnp.concatenate([inputs_part, down_part[:, None, :]], 1)

    mlp_grad = reduce_rows(mlp_term, (dgate_all, dup_all, hidden_rows))
    middle_part, gain_two_grad = norm_back(grad_normed_two, middle, scale_two, gain_values[1])
    grad_middle = grad_output + middle_part
    grad_branch = grad_middle.astype(jnp.bfloat16)
    grad_attended = lax.dot_general(
        grad_branch, attn_all[:, 3, :], (((1,), (1,)), ((), ())), preferred_element_type=jnp.float32
    ).astype(jnp.bfloat16)
    grad_query, grad_key_all, grad_value_all = attention_backward(
        query, key_all, value_all, allowed, log_sums, grad_attended.reshape(local_rows, HEADS, HD)
    )
    grad_key_own, grad_value_own = (
        lax.psum_scatter(
            grad_key_all.reshape(key_count, D).astype(jnp.bfloat16),
            "ctx",
            scatter_dimension=0,
            tiled=True,
        ).astype(jnp.float32),
        lax.psum_scatter(
            grad_value_all.reshape(key_count, D).astype(jnp.bfloat16),
            "ctx",
            scatter_dimension=0,
            tiled=True,
        ).astype(jnp.float32),
    )
    query_back = rotate(grad_query, cosine, sine, -1.0).reshape(local_rows, D).astype(jnp.bfloat16)
    key_back = (
        rotate(grad_key_own.reshape(local_rows, HEADS, HD), cosine, sine, -1.0)
        .reshape(local_rows, D)
        .astype(jnp.bfloat16)
    )
    value_back = grad_value_own.astype(jnp.bfloat16)
    grad_projected = jnp.stack([query_back, key_back, value_back], 1)
    grad_normed = jnp.einsum(
        "tkf,fkd->td", grad_projected, attn_all[:, :3, :], preferred_element_type=jnp.float32
    )
    source_part, gain_one_grad = norm_back(grad_normed, source, scale_one, gain_values[0])
    grad_input = grad_middle + source_part

    def attn_term(pieces):
        grad_part, attended_part = pieces
        inputs_part = jnp.einsum(
            "tkc,td->ckd", grad_part, normed, preferred_element_type=jnp.float32
        )
        output_part = lax.dot_general(
            attended_part, grad_branch, (((0,), (0,)), ((), ())), preferred_element_type=jnp.float32
        )
        return jnp.concatenate([inputs_part, output_part[:, None, :]], 1)

    attn_grad = reduce_rows(attn_term, (grad_projected, attended))
    gain_grad = lax.psum_scatter(
        jnp.stack([gain_one_grad, gain_two_grad], 0), ("dp", "ctx"), scatter_dimension=1, tiled=True
    )
    attn_rate = (
        RATE_FACTOR
        * D ** (-0.5)
        * jnp.array([1.0, 1.0, 1.0, OUTPUT_BOOST], jnp.float32).reshape(1, 4, 1)
    )
    mlp_rate = RATE_FACTOR * jnp.array(
        [D ** (-0.5), D ** (-0.5), FF ** (-0.5)], jnp.float32
    ).reshape(1, 3, 1)
    attn_new = adam_update(attn_weight, attn_first, attn_second, attn_grad, attn_rate, WEIGHT_DECAY)
    mlp_new = adam_update(mlp_weight, mlp_first, mlp_second, mlp_grad, mlp_rate, WEIGHT_DECAY)
    gain_new = adam_update(gain_weight, gain_first, gain_second, gain_grad, GAIN_RATE, 0.0)
    return (
        output,
        grad_input,
        attn_new[0],
        attn_new[1][:, :3, :],
        attn_new[1][:, 3, :],
        attn_new[2],
        mlp_new[0],
        mlp_new[1],
        mlp_new[2],
        gain_new[0],
        gain_new[1],
        gain_new[2],
    )


def solution(mesh):
    placed = (
        P(("dp", "ctx"), None),
        P(("dp", "ctx"), None),
        P(("dp", "ctx")),
        P(("dp", "ctx"), None, None),
        P(("dp", "ctx"), None, None),
        P(("dp", "ctx"), None, None),
        P(("dp", "ctx"), None, None),
        P(("dp", "ctx"), None, None),
        P(("dp", "ctx"), None, None),
        P(None, ("dp", "ctx")),
        P(None, ("dp", "ctx")),
        P(None, ("dp", "ctx")),
    )
    return jax.shard_map(
        local,
        mesh=mesh,
        in_specs=placed,
        out_specs=(
            P(("dp", "ctx"), None),
            P(("dp", "ctx"), None),
            P(("dp", "ctx"), None, None),
            P(("dp", "ctx"), None, None),
            P(("dp", "ctx"), None),
            P(("dp", "ctx"), None, None),
            P(("dp", "ctx"), None, None),
            P(("dp", "ctx"), None, None),
            P(("dp", "ctx"), None, None),
            P(None, ("dp", "ctx")),
            P(None, ("dp", "ctx")),
            P(None, ("dp", "ctx")),
        ),
        check_vma=False,
    )
```

profile of v0, /device:TPU:24, one launch (start us, length us, event | category | flops | bytes accessed | tf_op | source)
XLA Modules:
  0.0 4063.3 jit_solution(9327552542428114058)
XLA Ops:
  11.1 62.0 %all-gather.1 = bf16[32,64,2]{1,2,0:T(2,128)(2,1)S(1)} all-gather(bf16[1,64,2]{1,2,0:T(2,128)(2,1)S(1)} %convert_bitcast_fusion), channel_id=1, replica_groups=mesh['dp'=8,'ctx'=4] {'dp','ctx'}, dimensions={0}, use_global_device_ids=true | all-gather | bytes 8448 | tf_op jit(solution)/shard_map/all_gather | solution.py:179
  73.6 131.9 %all-gather.8.cloned.1.call-done = bf16[2048,4,2048]{2,0,1:T(8,128)(2,1)} async-done(((bf16[64,4,2048]{2,0,1:T(8,128)(2,1)}), bf16[2048,4,2048]{2,0,1:T(8,128)(2,1)}) %all-gather.8.cloned.1.call-update) | async-done | bytes 33554448 | tf_op jit(solution)/shard_map/all_gather | solution.py:178
  205.5 13.4 fusion.81
  265.8 34.1 all-gather.14.cloned.1.call-done
  306.4 75.1 %all-gather.10.cloned.1.call-done = bf16[1024,2048]{1,0:T(8,128)(2,1)} async-done(((bf16[256,2048]{1,0:T(8,128)(2,1)}), bf16[1024,2048]{1,0:T(8,128)(2,1)}) %all-gather.10.cloned.1.call-update) | async-done | bytes 4194320 | tf_op jit(solution)/shard_map/all_gather | solution.py:199
  387.8 49.2 %while.34 = (s32[]{:T(128)}, bf16[256,32,64]{0,2,1:T(8,128)(2,1)S(1)}, f32[32,256]{1,0:T(8,128)S(1)}, bf16[1024,32,64]{0,2,1:T(8,128)(2,1)}, bf16[256,32,64]{0,2...) while((s32[]{:T(128)}, ...), condition=%wide.region_4.5_spmd.clone, body=%wide.region_1.4_spmd.clone.sunk | while | flops 281803776 | bytes 15114423 | solution.py:101
  444.2 456.9 %all-gather.12.cloned.1.call-done = bf16[8192,3,2048]{2,0,1:T(8,128)(2,1)} async-done(((bf16[256,3,2048]{2,0,1:T(8,128)(2,1)}), bf16[8192,3,2048]{2,0,1:T(8,128)(2,1)}) %all-gather.12.cloned.1.call-update) | async-done | bytes 100663312 | tf_op jit(solution)/shard_map/all_gather | solution.py:215
  901.1 31.2 fusion.59
  932.3 21.8 fusion.80
  954.1 29.6 multiply_reduce_fusion.1
  1002.2 104.2 %while.35 = (s32[]{:T(128)}, f32[256,32,64]{0,2,1:T(8,128)}, bf16[1024,32,64]{0,2,1:T(8,128)(2,1)}, bf16[1024,32,64]{0,2,1:T(8,128)(2,1)}, bf16[1024,32,64]{0,2,...) while((s32[]{:T(128)}, f32[256,32,64]{0,2,1:T(8,128)}, ...), condition=%wide.region_9.10_spmd.clone, body=%wide.region_7.9_spmd.clone.sunk | while | flops 687930368 | bytes 37002448 | solution.py:149
  1131.1 58.0 %reduce-scatter.7.cloned.1.call-done = bf16[256,2048]{1,0:T(8,128)(2,1)} async-done(((bf16[1024,2048]{1,0:T(8,128)(2,1)}), bf16[256,2048]{1,0:T(8,128)(2,1)}) %reduce-scatter.7.cloned.1.call-update) | async-done | bytes 1048592 | tf_op jit(solution)/shard_map/reduce_scatter | solution.py:269
  1205.2 64.1 %reduce-scatter.9.cloned.1.call-done = bf16[256,2048]{1,0:T(8,128)(2,1)} async-done(((bf16[1024,2048]{1,0:T(8,128)(2,1)}), bf16[256,2048]{1,0:T(8,128)(2,1)}) %reduce-scatter.9.cloned.1.call-update) | async-done | bytes 1048592 | tf_op jit(solution)/shard_map/reduce_scatter | solution.py:275
  1269.3 21.5 convolution_bitcast_fusion.2
  1290.8 13.6 fusion.108
  1305.8 44.7 %pad_maximum_fusion.1 = f32[2048,4,2048]{0,2,1:T(8,128)} fusion(f32[2048,1,2048]{0,2,1:T(8,128)} %convolution_bitcast_fusion.3, f32[2048,3,2048]{0,2,1:T(8,128)} %convolution_bitcast_fusion.2), kind=kLoop, calls=%fused_computation.55 | loop fusion | flops 16777216 | bytes 134217728 | tf_op jit(solution)/shard_map/concatenate | solution.py:304
  1350.5 78.8 %copy.143 = f32[2048,4,2048]{2,1,0:T(4,128)} copy(f32[2048,4,2048]{0,2,1:T(8,128)} %pad_maximum_fusion.1) | data formatting | bytes 134217728 | tf_op jit(solution)/shard_map/concatenate | solution.py:304
  1430.5 31.1 convolution_bitcast_fusion.1
  1461.6 51.7 %convolution_bitcast_fusion = f32[8192,2,2048]{0,2,1:T(8,128)} fusion(bf16[256,1,8192]{2,0,1:T(8,128)(2,1)} %get-tuple-element.494, bf16[256,1,8192]{2,0,1:T(8,128)(2,1)} %get-tuple-element.493, f32[256,2048]{1,0:T(8,128)S(1)} %copy-done.10, f32[2048]{0:T(1024)S(1)} %bitcast.205, f32[256]{0:T(256)S(1)} %copy-done.24), kind=kOutput, calls=%fused_computation.60 | convolution fusion | flops 17198219264 | bytes 144712704 | tf_op jit(solution)/shard_map/tkc,td->ckd/dot_general | solution.py:247
  1513.2 134.4 %pad_maximum_fusion = f32[8192,3,2048]{0,2,1:T(8,128)} fusion(f32[8192,1,2048]{0,2,1:T(8,128)} %convolution_bitcast_fusion.1, f32[8192,2,2048]{0,2,1:T(8,128)} %convolution_bitcast_fusion), kind=kLoop, calls=%fused_computation.54 | loop fusion | flops 50331648 | bytes 402653184 | tf_op jit(solution)/shard_map/concatenate | solution.py:256
  1667.6 23.3 fusion.94
  1695.9 721.6 %all-reduce.3.cloned.1.call-done = f32[2048,4,2048]{2,1,0:T(4,128)} async-done(((f32[2048,4,2048]{2,1,0:T(4,128)}), f32[2048,4,2048]{2,1,0:T(4,128)}) %all-reduce.3.cloned.1.call-update) | async-done | bytes 67108880
  2428.3 1593.3 %reduce-scatter.11.cloned.1.call-done = f32[256,3,2048]{0,2,1:T(8,128)} async-done(((f32[8192,3,2048]{0,2,1:T(8,128)}), f32[256,3,2048]{0,2,1:T(8,128)}) %reduce-scatter.11.cloned.1.call-update) | async-done | bytes 6291472 | tf_op jit(solution)/shard_map/reduce_scatter | solution.py:157
  4021.6 14.8 multiply_subtract_fusion
  (266 shorter events, 341.0 us)
Async XLA Ops:
  7.2 66.1 %copy-start.6 = (bf16[256,2048]{1,0:T(8,128)(2,1)S(1)}, bf16[256,2048]{1,0:T(8,128)(2,1)}, u32[]{:S(2)}) copy-start(bf16[256,2048]{1,0:T(8,128)(2,1)} %param.18) | copy-start | bytes 3145732
  7.2 198.3 %all-gather.8.cloned.1.call-start = ((), (), s32[]{:S(2)}) async-start(), calls=%async_computation.4 | async-start | bytes 34603008 | tf_op jit(solution)/shard_map/all_gather | solution.py:178
  11.0 288.9 %all-gather.14.cloned.1.call-start = ((), (), s32[]{:S(2)}) async-start(), calls=%async_computation.10 | async-start | bytes 5242880 | tf_op jit(solution)/shard_map/all_gather | solution.py:200
  73.5 145.3 %copy-start.30 = (f32[256]{0:T(256)}, f32[256]{0:T(256)S(1)}, u32[]{:S(2)}) copy-start(f32[256]{0:T(256)S(1)} %add_rsqrt_fusion.1) | copy-start | bytes 3076
  73.6 145.3 %copy-start.26 = (f32[1,2048]{1,0:T(1,128)}, f32[1,2048]{1,0:T(1,128)S(1)}, u32[]{:S(2)}) copy-start(f32[1,2048]{1,0:T(1,128)S(1)} %get-tuple-element.512) | copy-start | bytes 24580
  73.6 910.1 %copy-start.21 = (f32[1,2048]{1,0:T(1,128)}, f32[1,2048]{1,0:T(1,128)S(1)}, u32[]{:S(2)}) copy-start(f32[1,2048]{1,0:T(1,128)S(1)} %get-tuple-element.511) | copy-start | bytes 24580
  221.6 159.8 %all-gather.10.cloned.1.call-start = ((), (), s32[]{:S(2)}) async-start(), calls=%async_computation.5 | async-start | bytes 5242880 | tf_op jit(solution)/shard_map/all_gather | solution.py:199
  249.5 651.6 %all-gather.12.cloned.1.call-start = ((), (), s32[]{:S(2)}) async-start(), calls=%async_computation.6 | async-start | bytes 103809024 | tf_op jit(solution)/shard_map/all_gather | solution.py:215
  254.6 934.5 %reduce-scatter.7.cloned.1.call-start = ((), (), s32[]{:S(2)}) async-start(), calls=%async_computation.7 | async-start | bytes 5242880 | tf_op jit(solution)/shard_map/reduce_scatter | solution.py:269
  444.2 509.9 %copy-start.9 = (f32[256,2048]{1,0:T(8,128)}, f32[256,2048]{1,0:T(8,128)S(1)}, u32[]{:S(2)}) copy-start(f32[256,2048]{1,0:T(8,128)S(1)} %get-tuple-element.516) | copy-start | bytes 6291460
  444.2 539.5 %copy-start.23 = (f32[256]{0:T(256)}, f32[256]{0:T(256)S(1)}, u32[]{:S(2)}) copy-start(f32[256]{0:T(256)S(1)} %add_rsqrt_fusion) | copy-start | bytes 3076
  986.6 136.4 %copy-start = (f32[256,2048]{1,0:T(8,128)}, f32[256,2048]{1,0:T(8,128)S(1)}, u32[]{:S(2)}) copy-start(f32[256,2048]{1,0:T(8,128)S(1)} %multiply_add_fusion.2) | copy-start | bytes 6291460
  1112.8 156.4 %reduce-scatter.9.cloned.1.call-start = ((), (), s32[]{:S(2)}) async-start(), calls=%async_computation.8 | async-start | bytes 5242880 | tf_op jit(solution)/shard_map/reduce_scatter | solution.py:275
  1119.4 575.2 %reduce-scatter.13.cloned.1.call-start = ((), (), s32[]{:S(2)}) async-start(), calls=%async_computation.11 | async-start | bytes 1081344
  1131.1 62.7 %copy-start.17 = (f32[256,32,32]{0,2,1:T(8,128)S(1)}, f32[256,32,32]{0,2,1:T(8,128)}, u32[]{:S(2)}) copy-start(f32[256,32,32]{0,2,1:T(8,128)} %get-tuple-element.497) | copy-start | bytes 3145732
  1131.1 62.7 %copy-start.20 = (f32[256,64]{0,1:T(8,128)S(1)}, f32[256,64]{0,1:T(8,128)}, u32[]{:S(2)}) copy-start(f32[256,64]{0,1:T(8,128)} %copy-done.19) | copy-start | bytes 196612
  1131.1 62.7 %copy-start.25 = (f32[256,64]{0,1:T(8,128)S(1)}, f32[256,64]{0,1:T(8,128)}, u32[]{:S(2)}) copy-start(f32[256,64]{0,1:T(8,128)} %get-tuple-element.509) | copy-start | bytes 196612
  1199.3 70.0 %copy-start.7 = (bf16[256,2048]{1,0:T(8,128)(2,1)S(1)}, bf16[256,2048]{1,0:T(8,128)(2,1)}, u32[]{:S(2)}) copy-start(bf16[256,2048]{1,0:T(8,128)(2,1)} %param.18) | copy-start | bytes 3145732
  1199.3 70.0 %copy-start.27 = (f32[1,2048]{1,0:T(1,128)S(1)}, f32[1,2048]{1,0:T(1,128)}, u32[]{:S(2)}) copy-start(f32[1,2048]{1,0:T(1,128)} %copy-done.26) | copy-start | bytes 24580
  1199.3 70.0 %copy-start.31 = (f32[256]{0:T(256)S(1)}, f32[256]{0:T(256)}, u32[]{:S(2)}) copy-start(f32[256]{0:T(256)} %copy-done.30) | copy-start | bytes 3076
  1305.8 1111.8 %all-reduce.3.cloned.1.call-start = ((), (), s32[]{:S(2)}) async-start(), calls=%async_computation.12 | async-start | bytes 134217728
  1429.3 2592.3 %reduce-scatter.11.cloned.1.call-start = ((), (), s32[]{:S(2)}) async-start(), calls=%async_computation.9 | async-start | bytes 207618048 | tf_op jit(solution)/shard_map/reduce_scatter | solution.py:157
  1690.9 726.7 %copy-start.39 = (f32[4]{0:T(128)S(1)}, f32[4]{0:T(128)}, u32[]{:S(2)}) copy-start(f32[4]{0:T(128)} %constant.181) | copy-start | bytes 52
  2424.7 1596.9 %copy-start.38 = (f32[3]{0:T(128)S(1)}, f32[3]{0:T(128)}, u32[]{:S(2)}) copy-start(f32[3]{0:T(128)} %constant.182) | copy-start | bytes 40
  (25 other events, 427.1 us)
Sparse Core Ops, SparseCore 0:
  11.6 193.8 all-gather.7
  221.7 78.1 all-gather.13
  302.1 79.2 all-gather.9
  384.8 516.1 all-gather.11
  1113.0 76.1 reduce-scatter.6
  1192.0 77.2 reduce-scatter.8
  1305.9 128.8 reduce-scatter.12
  1442.4 975.1 all-reduce.2
  2425.1 1596.4 reduce-scatter.10
where the time goes:
time: 4080 us; the launch traced here: 4060 us
  waiting for transfers between devices  3140 us (77%)
  matrix products  387 us (9%)
  other arithmetic  259 us (6%)
  local copies, waits for them, and re-layouts  193 us (5%)
  blocking collectives  73.1 us (2%)
    reduce_scatter x1, waiting for transfers between devices, reduce_rows(): lax.psum_scatter(term(column_slices(columns)), ('dp', 'ctx'), scatter_dim...  1590 us
    unnamed x11, waiting for transfers between devices  722 us
    all_gather x1, waiting for transfers between devices, local(): piece = lax.all_gather(mlp_low, ('dp', 'ctx'), axis=0, tiled=True)  457 us
    concatenate x1, other arithmetic, mlp_term(): return jnp.concatenate([inputs_part, down_part[:, None, :]], 1)  134 us
    all_gather x1, waiting for transfers between devices, local(): lax.all_gather(attn_weight.astype(jnp.bfloat16), ('dp', 'ctx'), axis=0, t...  132 us
  transfers between devices with their start and end apart: 9, of which 8 were waited for; matrix products, arithmetic and copies ran while one was open for 13% of the time, Pallas kernels for 0%

commit v1 on v0

v1 whole, which is shorter than its diff:
```python
import functools

import jax
import jax.numpy as jnp
import numpy as np
from jax import lax
from jax.experimental import pallas as pl
from jax.experimental.pallas import tpu as pltpu
from jax.sharding import Mesh
from jax.sharding import PartitionSpec as P

D = 2048
HEADS = 32
HD = 64
FF = 8192
STEP = 10


NORM_EPS = 1e-05
ROPE_BASE = 130000.0
BETA_ONE = 0.9
BETA_TWO = 0.95
ADAM_EPS = 1e-08
WEIGHT_DECAY = 0.1
RATE_FACTOR = 1.5
GAIN_RATE = 0.6
OUTPUT_BOOST = 12.0
MASKED = -1e30
BF = jnp.bfloat16
F32 = jnp.float32
ALL = ("plane", "core", "ctx")
TEAM = ("core", "ctx")


BLOCK = 256
CHUNKS = 2
VMEM_LIMIT = 60 * 1024 * 1024
MESH_ID = pl.DeviceIdType.MESH


def params(semantics=1, **more):
    return pltpu.CompilerParams(
        dimension_semantics=("arbitrary",) * semantics, vmem_limit_bytes=VMEM_LIMIT, **more
    )


def rope_tables(length):
    halved = HD // 2
    frequency = (ROPE_BASE ** (-(np.arange(halved) * 2.0 / HD))).astype(np.float32)
    angle = np.arange(length, dtype=np.float32)[:, None] * frequency[None, :]
    cosine, sine = np.cos(angle).astype(np.float32), np.sin(angle).astype(np.float32)
    zero = np.zeros_like(sine)
    return (
        jnp.asarray(np.concatenate([cosine] * 4, 1)),
        jnp.asarray(np.concatenate([-sine, zero] * 2, 1)),
        jnp.asarray(np.concatenate([zero, sine] * 2, 1)),
    )


def widen(table, feats):
    return jnp.concatenate([table] * (feats // 128), 1) if feats > 128 else table


def rope(values, cosine, low_sine, high_sine):
    width = values.shape[-1]
    ahead = pltpu.roll(values, width - HD // 2, 1)
    behind = pltpu.roll(values, HD // 2, 1)
    return values * cosine + ahead * low_sine + behind * high_sine


def rope_back(values, cosine, low_sine, high_sine):
    width = values.shape[-1]
    ahead = pltpu.roll(values, width - HD // 2, 1)
    behind = pltpu.roll(values, HD // 2, 1)
    return values * cosine - ahead * low_sine - behind * high_sine


def mm(a, b, ca, cb):
    return lax.dot_general(a, b, (((ca,), (cb,)), ((), ())), preferred_element_type=F32)


def norm_scale(values):
    return lax.rsqrt(jnp.mean(values * values, -1, keepdims=True) + NORM_EPS)


def norm_back(grad_normed, values, scale, gain):
    weighted = grad_normed * gain
    grad_values = scale * (
        weighted - values * scale * scale * jnp.mean(weighted * values, -1, keepdims=True)
    )
    return (grad_values, jnp.sum(grad_normed * values * scale, 0))


def adam_update(master, first, second, grad, rate, decay):
    first_new = BETA_ONE * first + (1.0 - BETA_ONE) * grad
    second_new = BETA_TWO * second + (1.0 - BETA_TWO) * grad * grad
    direction = (
        first_new
        / (1.0 - BETA_ONE**STEP)
        / (jnp.sqrt(second_new / (1.0 - BETA_TWO**STEP)) + ADAM_EPS)
    )
    return (first_new, second_new, master - rate * (direction + decay * master))


def greet_all(peers):
    barrier = pltpu.get_barrier_semaphore()
    for peer in peers:
        pl.semaphore_signal(barrier, inc=1, device_id=peer, device_id_type=MESH_ID)
    pl.semaphore_wait(barrier, len(peers))


def neighbours(planes, ctxs):
    plane, core, ctx = lax.axis_index("plane"), lax.axis_index("core"), lax.axis_index("ctx")
    column = [lax.rem(plane + k, planes) for k in range(1, planes)]
    group = [
        (core if dc == 0 else 1 - core, lax.rem(ctx + dz, ctxs))
        for dc in range(2)
        for dz in range(ctxs)
        if dc + dz > 0
    ]
    return plane, core, ctx, column, group


def gather_kernel(planes, ctxs, lines, boards, inputs, refs):
    ins, outs = refs[:inputs], refs[inputs : inputs + len(lines) + len(boards)]
    line_send, line_recv, side_send, side_recv, board_send, board_recv, pass_send, pass_recv, here = refs[
        inputs + len(lines) + len(boards) :
    ]
    plane, core, ctx = lax.axis_index("plane"), lax.axis_index("core"), lax.axis_index("ctx")
    last = ctxs - 1
    column = [lax.rem(plane + k, planes) for k in range(1, planes)]
    greet_all(
        [(p, core, ctx) for p in column]
        + [(plane, core, lax.rem(ctx + k, ctxs)) for k in range(1, ctxs)]
        + [(plane, 1 - core, ctx)]
    )
    other = (plane, 1 - core, ctx)
    pieces = []
    for source, target, chunks in lines:
        rows = ins[source].shape[0] // chunks
        for chunk in range(chunks):
            pieces.append((ins[source], outs[target], pl.ds(chunk * rows, rows)))

    def remote(source, target, send, recv, peer):
        return pltpu.make_async_remote_copy(
            src_ref=source,
            dst_ref=target,
            send_sem=send,
            recv_sem=recv,
            device_id=peer,
            device_id_type=MESH_ID,
        )

    def line(index, way, hop, block, peer_ctx, own):
        value, out, rows = pieces[index]
        slot = out.at[core * ctxs + block, rows]
        return remote(
            value.at[rows] if own else slot,
            slot,
            line_send.at[index, way, hop],
            line_recv.at[index, way, hop],
            (plane, core, peer_ctx),
        )

    def side(index, order, side_core, block, own):
        value, out, rows = pieces[index]
        slot = out.at[side_core * ctxs + block, rows]
        return remote(
            value.at[rows] if own else slot,
            slot,
            side_send.at[index, order],
            side_recv.at[index, order],
            other,
        )

    square = planes == 4
    near_x = plane + 1 - 2 * lax.rem(plane, 2)
    near_y = lax.rem(plane + 2, 4)
    far = 3 - plane

    def board_refs(index, home, half=None, own=True):
        kind, source, target = boards[index]
        value, out = source(ins, outs), outs[target]
        if kind in ("block", "late"):
            size = value.shape[0]
            part = pl.ds(0, size) if half is None else pl.ds(half * (size // 2), size // 2)
            slot = out.at[home, part]
            return (value.at[part] if own else slot), slot
        if kind == "slots":
            size = value.shape[1]
            part = pl.ds(0, size) if half is None else pl.ds(half * (size // 2), size // 2)
            slot = out.at[:, home, part]
            return (value.at[:, part] if own else slot), slot
        size = ctxs if half is None else ctxs // 2
        part = pl.ds(core * ctxs + (0 if half is None else half * size), size)
        slot = out.at[part, home]
        return (value.at[part] if own else slot), slot

    def board(index, k, home, peer):
        value, slot = board_refs(index, home)
        return remote(
            value, slot, board_send.at[index, k], board_recv.at[index, k], (peer, core, ctx)
        )

    sent = [(plane, 0, near_x), (plane, 1, near_x), (plane, 0, near_y), (plane, 1, near_y)]
    sent += [(near_y, 0, near_x), (near_x, 1, near_y)]
    landed = [near_x, near_x, near_y, near_y, far, far]

    def relay(index, k, arriving=False):
        home, half, peer = sent[k]
        value, slot = board_refs(index, landed[k] if arriving else home, half, k < 4)
        return remote(
            value, slot, board_send.at[index, k], board_recv.at[index, k], (peer, core, ctx)
        )

    def relayed(index):
        return square and boards[index][0] != "late"

    def board_start(index):
        if relayed(index):
            for k in (1, 2, 0, 3):
                relay(index, k).start()
            return
        for k, peer in enumerate(column):
            board(index, k, plane, peer).start()

    def board_pass(index):
        if relayed(index):
            relay(index, 2, True).wait_recv()
            relay(index, 4).start()
            relay(index, 1, True).wait_recv()
            relay(index, 5).start()

    def sources(index):
        if relayed(index):
            return [near_x, near_y, far]
        return [lax.rem(plane + planes - 1 - k, planes) for k in range(planes - 1)]

    def share(index, k, home):
        _, slot = board_refs(index, home)
        return remote(slot, slot, pass_send.at[index, k], pass_recv.at[index, k], other)

    def board_finish(index):
        if relayed(index):
            for k in (0, 3, 4, 5):
                relay(index, k, True).wait_recv()
        for k, home in enumerate(sources(index)):
            if not relayed(index):
                board(index, k, home, home).wait_recv()
            if boards[index][0] == "half":
                share(index, k, home).start()

    def board_close(index):
        if relayed(index):
            for k in range(6):
                relay(index, k).wait_send()
        else:
            for k, peer in enumerate(column):
                board(index, k, plane, peer).wait_send()
        if boards[index][0] == "half":
            out = outs[boards[index][2]]
            for k, home in enumerate(sources(index)):
                share(index, k, home).wait_send()
                slot = out.at[pl.ds((1 - core) * ctxs, ctxs), home]
                remote(
                    slot, slot, pass_send.at[index, k], pass_recv.at[index, k], other
                ).wait_recv()

    count = len(pieces)
    late = [i for i in range(len(boards)) if boards[i][0] == "late"]
    early = [i for i in range(len(boards)) if boards[i][0] != "late"]
    board_start(early[0]) if early else None

    @pl.when(ctx < last)
    def _():
        for i in range(count):
            line(i, 0, 1, ctx, ctx + 1, True).start()

    @pl.when(ctx > 0)
    def _():
        for i in range(count):
            line(i, 1, 1, ctx, ctx - 1, True).start()

    for i in range(count):
        side(i, 0, core, ctx, True).start()
    copies = []
    for i, (value, out, rows) in enumerate(pieces):
        copies.append(
            pltpu.make_async_copy(value.at[rows], out.at[core * ctxs + ctx, rows], here.at[i])
        )
    for i in early:
        kind, source, target = boards[i]
        slot = outs[target].at[plane] if kind == "block" else outs[target].at[:, plane]
        copies.append(pltpu.make_async_copy(source(ins, outs), slot, here.at[count + i]))
    for copy in copies:
        copy.start()

    passed = 0
    board_pass(early[0])
    if len(early) > 1:
        board_start(early[1])
    for hop in range(1, ctxs):

        @pl.when(ctx >= hop)
        def _():
            block = ctx - hop
            for i in range(count):
                line(i, 0, hop, block, ctx - 1, False).wait_recv()

                @pl.when(ctx < last)
                def _():
                    line(i, 0, hop + 1, block, ctx + 1, False).start()

                side(i, hop, core, block, False).start()

        @pl.when(ctx + hop <= last)
        def _():
            block = ctx + hop
            for i in range(count):
                line(i, 1, hop, block, ctx + 1, False).wait_recv()

                @pl.when(ctx > 0)
                def _():
                    line(i, 1, hop + 1, block, ctx - 1, False).start()

                side(i, last + hop, core, block, False).start()

        if passed + 1 < len(early):
            passed += 1
            board_pass(early[passed])
            if passed + 1 < len(early):
                board_start(early[passed + 1])
    for i in early:
        board_finish(i)

    for i in range(count):
        side(i, 0, 1 - core, ctx, False).wait_recv()
    for hop in range(1, ctxs):

        @pl.when(ctx >= hop)
        def _():
            for i in range(count):
                side(i, hop, 1 - core, ctx - hop, False).wait_recv()

        @pl.when(ctx + hop <= last)
        def _():
            for i in range(count):
                side(i, last + hop, 1 - core, ctx + hop, False).wait_recv()

    for copy in copies:
        copy.wait()
    for i in late:
        board_start(i)
        kind, source, target = boards[i]
        copy = pltpu.make_async_copy(source(ins, outs), outs[target].at[plane], here.at[count + i])
        copy.start()
        copy.wait()
    for i in late:
        board_finish(i)

    for i in range(len(boards)):
        board_close(i)
    for i in range(count):
        side(i, 0, core, ctx, True).wait_send()
    for hop in range(1, ctxs):

        @pl.when(ctx >= hop)
        def _():
            for i in range(count):
                side(i, hop, core, ctx - hop, False).wait_send()

        @pl.when(ctx + hop <= last)
        def _():
            for i in range(count):
                side(i, last + hop, core, ctx + hop, False).wait_send()

        @pl.when((ctx < last) & (ctx >= hop - 1))
        def _():
            for i in range(count):
                line(i, 0, hop, ctx - hop + 1, ctx + 1, False).wait_send()

        @pl.when((ctx > 0) & (ctx + hop - 1 <= last))
        def _():
            for i in range(count):
                line(i, 1, hop, ctx + hop - 1, ctx - 1, False).wait_send()


def gather_call(planes, ctxs, number, inputs, lines, boards, shapes, name):
    pieces = sum(chunks for _, _, chunks in lines)
    dma = pltpu.SemaphoreType.DMA

    def kernel(*refs):
        gather_kernel(planes, ctxs, lines, boards, len(inputs), refs)

    return pl.pallas_call(
        kernel,
        out_shape=tuple(jax.ShapeDtypeStruct(shape, dtype) for shape, dtype in shapes),
        in_specs=[pl.BlockSpec(memory_space=pl.ANY)] * len(inputs),
        out_specs=tuple(pl.BlockSpec(memory_space=pl.ANY) for _ in shapes),
        scratch_shapes=[
            dma((pieces, 2, ctxs + 1)),
            dma((pieces, 2, ctxs + 1)),
            dma((pieces, 2 * ctxs)),
            dma((pieces, 2 * ctxs)),
            dma((len(boards), max(planes, 6))),
            dma((len(boards), max(planes, 6))),
            dma((len(boards), planes)),
            dma((len(boards), planes)),
            dma((pieces + len(boards),)),
        ],
        compiler_params=pltpu.CompilerParams(collective_id=number, has_side_effects=True),
        name=name,
    )(*inputs)


def small_sum_kernel(planes, ctxs, value_ref, out_ref, got_one, middle, got_two, sems):
    plane, core, ctx, column, group = neighbours(planes, ctxs)
    greet_all([(p, core, ctx) for p in column] + [(plane, c, z) for c, z in group])

    def hop(index, source, target, peer):
        return pltpu.make_async_remote_copy(
            src_ref=source,
            dst_ref=target,
            send_sem=sems.at[0, index],
            recv_sem=sems.at[1, index],
            device_id=peer,
            device_id_type=MESH_ID,
        )

    first = [
        hop(i, value_ref.at[p], got_one.at[i], (p, core, ctx)) for i, p in enumerate(column)
    ]
    for copy in first:
        copy.start()
    total = value_ref[plane]
    for i, copy in enumerate(first):
        copy.wait_recv()
        total = total + got_one[i]
    middle[...] = total
    base = len(column)
    second = [
        hop(base + i, middle.at[c * ctxs + z], got_two.at[i], (plane, c, z))
        for i, (c, z) in enumerate(group)
    ]
    for copy in second:
        copy.start()
    total = middle[core * ctxs + ctx]
    for i, copy in enumerate(second):
        copy.wait_recv()
        total = total + got_two[i]
    out_ref[...] = total
    for copy in first + second:
        copy.wait_send()


def small_sum(planes, ctxs, value):
    hops = planes + 2 * ctxs - 2
    tile = value.shape[2:]
    return pl.pallas_call(
        functools.partial(small_sum_kernel, planes, ctxs),
        out_shape=jax.ShapeDtypeStruct(tile, F32),
        in_specs=[pl.BlockSpec(memory_space=pltpu.VMEM)],
        out_specs=pl.BlockSpec(memory_space=pltpu.VMEM),
        scratch_shapes=[
            pltpu.VMEM((planes - 1, 2 * ctxs) + tile, F32),
            pltpu.VMEM((2 * ctxs,) + tile, F32),
            pltpu.VMEM((2 * ctxs - 1,) + tile, F32),
            pltpu.SemaphoreType.DMA((2, hops)),
        ],
        compiler_params=pltpu.CompilerParams(collective_id=1, has_side_effects=True),
        name="small_sum",
    )(value)


class Gather:
    def __init__(self, ctxs, pieces, boards, sems):
        self.ctxs, self.pieces, self.boards = ctxs, pieces, boards
        self.line_sem, self.side_sem, self.board_sem, self.pass_sem = sems
        self.plane, self.core, self.ctx = (
            lax.axis_index("plane"),
            lax.axis_index("core"),
            lax.axis_index("ctx"),
        )
        self.last = ctxs - 1
        self.near_x = self.plane + 1 - 2 * lax.rem(self.plane, 2)
        self.near_y = lax.rem(self.plane + 2, 4)
        self.far = 3 - self.plane

    @staticmethod
    def scratch(ctxs, pieces, boards):
        dma = pltpu.SemaphoreType.DMA
        return [
            dma((2, pieces, 2, ctxs + 1)),
            dma((2, pieces, 2 * ctxs)),
            dma((2, boards, 6)),
            dma((2, boards, 3)),
        ]

    def peers(self):
        plane, core, ctx, ctxs = self.plane, self.core, self.ctx, self.ctxs
        return (
            [(plane, core, lax.rem(ctx + k, ctxs)) for k in range(1, ctxs)]
            + [(plane, 1 - core, ctx)]
            + [(near, core, ctx) for near in (self.near_x, self.near_y)]
        )

    def remote(self, slot, sem, index, peer):
        return pltpu.make_async_remote_copy(
            src_ref=slot,
            dst_ref=slot,
            send_sem=sem.at[(0,) + index],
            recv_sem=sem.at[(1,) + index],
            device_id=peer,
            device_id_type=MESH_ID,
        )

    def line(self, i, way, hop, block):
        buffer, rows = self.pieces[i]
        slot = buffer.at[self.core * self.ctxs + block, rows]
        peer = (self.plane, self.core, self.ctx + (1 if way == 0 else -1))
        return self.remote(slot, self.line_sem, (i, way, hop), peer)

    def side(self, i, order, core, block):
        buffer, rows = self.pieces[i]
        slot = buffer.at[core * self.ctxs + block, rows]
        return self.remote(slot, self.side_sem, (i, order), (self.plane, 1 - self.core, self.ctx))

    def send_own(self, items):
        @pl.when(self.ctx < self.last)
        def _():
            for i in items:
                self.line(i, 0, 1, self.ctx).start()

        @pl.when(self.ctx > 0)
        def _():
            for i in items:
                self.line(i, 1, 1, self.ctx).start()

        for i in items:
            self.side(i, 0, self.core, self.ctx).start()

    def hop(self, k, items):
        ctx, last = self.ctx, self.last

        for i in items:

            @pl.when(ctx >= k)
            def _():
                self.line(i, 0, k, ctx - k).wait_recv()

                @pl.when(ctx < last)
                def _():
                    self.line(i, 0, k + 1, ctx - k).start()

                self.side(i, k, self.core, ctx - k).start()

            @pl.when(ctx + k <= last)
            def _():
                self.line(i, 1, k, ctx + k).wait_recv()

                @pl.when(ctx > 0)
                def _():
                    self.line(i, 1, k + 1, ctx + k).start()

                self.side(i, last + k, self.core, ctx + k).start()

    def side_arrive(self, k, items):
        ctx, last = self.ctx, self.last
        if k == 0:
            for i in items:
                self.side(i, 0, 1 - self.core, ctx).wait_recv()
            return

        @pl.when(ctx >= k)
        def _():
            for i in items:
                self.side(i, k, 1 - self.core, ctx - k).wait_recv()

        @pl.when(ctx + k <= last)
        def _():
            for i in items:
                self.side(i, last + k, 1 - self.core, ctx + k).wait_recv()

    def distant(self, k, action):
        ctx, last = self.ctx, self.last
        behind = (ctx >= k).astype(jnp.int32)
        ahead = (ctx + k <= last).astype(jnp.int32)

        def body(i, carry):
            action(jnp.where((behind == 1) & (i == 0), ctx - k, ctx + k))
            return carry

        lax.fori_loop(0, behind + ahead, body, 0)

    def board_slot(self, index, home, half):
        kind, buffer = self.boards[index]
        if kind == "block":
            size = buffer.shape[1] // 2
            return buffer.at[home, pl.ds(half * size, size)]
        if kind == "slots":
            size = buffer.shape[2] // 2
            return buffer.at[:, home, pl.ds(half * size, size)]
        size = self.ctxs // 2
        return buffer.at[pl.ds(self.core * self.ctxs + half * size, size), home]

    def relay(self, index, k, arriving=False):
        plane, near_x, near_y, far = self.plane, self.near_x, self.near_y, self.far
        sent = [(plane, 0, near_x), (plane, 1, near_x), (plane, 0, near_y), (plane, 1, near_y)]
        home, half, peer = (sent + [(near_y, 0, near_x), (near_x, 1, near_y)])[k]
        if arriving:
            home = [near_x, near_x, near_y, near_y, far, far][k]
        slot = self.board_slot(index, home, half)
        return self.remote(slot, self.board_sem, (index, k), (peer, self.core, self.ctx))

    def board_start(self, index):
        for k in (1, 2, 0, 3):
            self.relay(index, k).start()

    def board_pass(self, index):
        self.relay(index, 2, True).wait_recv()
        self.relay(index, 4).start()
        self.relay(index, 1, True).wait_recv()
        self.relay(index, 5).start()

    def share(self, index, k, core):
        buffer = self.boards[index][1]
        home = [self.near_x, self.near_y, self.far][k]
        slot = buffer.at[pl.ds(core * self.ctxs, self.ctxs), home]
        return self.remote(
            slot, self.pass_sem, (index, k), (self.plane, 1 - self.core, self.ctx)
        )

    def board_finish(self, index):
        for k in (0, 3, 4, 5):
            self.relay(index, k, True).wait_recv()
        if self.boards[index][0] == "half":
            for k in range(3):
                self.share(index, k, self.core).start()

    def board_shared(self, index):
        for k in range(3):
            self.share(index, k, 1 - self.core).wait_recv()

    def close(self):
        ctx, last = self.ctx, self.last
        items = range(len(self.pieces))
        for index in range(len(self.boards)):
            for k in range(6):
                self.relay(index, k).wait_send()
            if self.boards[index][0] == "half":
                for k in range(3):
                    self.share(index, k, self.core).wait_send()
        for i in items:
            self.side(i, 0, self.core, ctx).wait_send()
        for k in range(1, self.ctxs):

            @pl.when(ctx >= k)
            def _():
                for i in items:
                    self.side(i, k, self.core, ctx - k).wait_send()

            @pl.when(ctx + k <= last)
            def _():
                for i in items:
                    self.side(i, last + k, self.core, ctx + k).wait_send()

            @pl.when((ctx < last) & (ctx >= k - 1))
            def _():
                for i in items:
                    self.line(i, 0, k, ctx - k + 1).wait_send()

            @pl.when((ctx > 0) & (ctx + k - 1 <= last))
            def _():
                for i in items:
                    self.line(i, 1, k, ctx + k - 1).wait_send()


def front_kernel(ctxs, refs):
    tokens, qkv, mlp, packed, c_ref, a_ref, b_ref = refs[:7]
    x_out, n_out, q_out, k_out, v_out, w_out, g_out, small = refs[7:15]
    xs, ns, qs, ks, vs, ws, gs, wide, load, store, small_sem = refs[15:26]
    own = tokens.shape[0]
    half = own // 2
    pieces = [(xs, pl.ds(0, half)), (xs, pl.ds(half, half))]
    boards = [("slots", ws), ("block", gs)]
    net = Gather(ctxs, pieces, boards, refs[26:])
    plane, core, ctx = net.plane, net.core, net.ctx
    me = core * ctxs + ctx
    loads = [
        pltpu.make_async_copy(qkv, ws.at[:, plane], load.at[0]),
        pltpu.make_async_copy(tokens, xs.at[me], load.at[1]),
        pltpu.make_async_copy(mlp.at[0], wide, load.at[2]),
    ]
    for copy in loads:
        copy.start()
    others = [
        (core if dc == 0 else 1 - core, lax.rem(ctx + dz, ctxs))
        for dc in range(2)
        for dz in range(ctxs)
        if dc + dz > 0
    ]
    column = [lax.rem(plane + k, 4) for k in range(1, 4)]
    greet_all([(plane, c, z) for c, z in others] + [(p, core, ctx) for p in column])

    def tiny(index, source, target, peer):
        return pltpu.make_async_remote_copy(
            src_ref=source,
            dst_ref=target,
            send_sem=small_sem.at[0, index],
            recv_sem=small_sem.at[1, index],
            device_id=peer,
            device_id_type=MESH_ID,
        )

    small[plane, me] = packed[...]
    one = [
        tiny(i, packed, small.at[plane, me], (plane, c, z)) for i, (c, z) in enumerate(others)
    ]
    for copy in one:
        copy.start()
    for copy in loads[:2]:
        copy.wait()
    net.board_start(0)
    net.send_own([0, 1])
    i = 0
    for dc in range(2):
        for dz in range(ctxs):
            if dc + dz > 0:
                c, z = core if dc == 0 else 1 - core, lax.rem(ctx + ctxs - dz, ctxs)
                tiny(i, packed, small.at[plane, c * ctxs + z], (plane, c, z)).wait_recv()
                i += 1
    two = [
        tiny(i + k, small.at[plane], small.at[plane], (p, core, ctx))
        for k, p in enumerate(column)
    ]
    for copy in two:
        copy.start()
    loads[2].wait()

    def narrow(g, carry):
        part = pl.ds(pl.multiple_of(g * 16, 16), 16)
        gs[plane, part, :] = wide[part, :].astype(BF)
        return carry

    lax.fori_loop(0, wide.shape[0] // 16, narrow, 0)
    net.board_pass(0)
    net.board_start(1)
    for k in range(3):
        home = lax.rem(plane + 3 - k, 4)
        tiny(i + k, small.at[plane], small.at[home], (home, core, ctx)).wait_recv()
    tiles = [
        small[p, 2 * j][0:1] + small[p, 2 * j + 1][0:1] for p in range(4) for j in range(ctxs)
    ]
    gain = jnp.concatenate(tiles, 1)
    feats = q_out.shape[-1]
    stores = []

    blocks = [(xs, x_out), (ns, n_out), (qs, q_out), (ks, k_out), (vs, v_out)]

    def put(source, target, index):
        return pltpu.make_async_copy(source, target, store.at[index])

    def compute(side_core):
        def action(block):
            b = side_core * ctxs + block
            values = xs[b].astype(F32)
            normed = (values * norm_scale(values) * gain).astype(BF)
            ns[b] = normed
            rows = pl.ds(pl.multiple_of(block * own, own), own)
            cosine, low_sine, high_sine = [
                widen(ref[rows, :], feats) for ref in (c_ref, a_ref, b_ref)
            ]
            q = mm(normed, ws[0].reshape(feats, D), 1, 1)
            qs[b] = rope(q, cosine, low_sine, high_sine).astype(BF)
            k = mm(normed, ws[1].reshape(feats, D), 1, 1)
            ks[b] = rope(k, cosine, low_sine, high_sine).astype(BF)
            vs[b] = mm(normed, ws[2].reshape(feats, D), 1, 1).astype(BF)
            for i, (source, target) in enumerate(blocks):
                put(source.at[b], target.at[b], 5 * b + i).start()

        return action

    base = 10 * ctxs
    parts = [0, 1]
    stores = [put(s, t, base + i) for i, (s, t) in enumerate([(ws, w_out), (gs, g_out)])]
    net.hop(1, parts)
    net.board_finish(0)
    stores[0].start()
    compute(core)(ctx)
    net.side_arrive(0, parts)
    compute(1 - core)(ctx)
    net.board_pass(1)
    for k in range(1, ctxs):
        net.distant(k, compute(core))
        if k + 1 < ctxs:
            net.hop(k + 1, parts)
        net.side_arrive(k, parts)
        net.distant(k, compute(1 - core))
        if k == min(2, ctxs - 1):
            net.board_finish(1)
            stores[1].start()
    net.close()
    for copy in one + two:
        copy.wait_send()
    for copy in stores:
        copy.wait()
    for b in range(2 * ctxs):
        for i, (source, target) in enumerate(blocks):
            put(source.at[b], target.at[b], 5 * b + i).wait()


def front_call(ctxs, tokens, qkv, mlp, packed, tables):
    team = 2 * ctxs
    own, arows, frows = tokens.shape[0], qkv.shape[1], mlp.shape[1]
    feats = 4 * arows
    block, part = (team, own, D), (team, own, feats)
    shapes = [block, block, part, part, part, (3, 4, arows, D)]
    shapes += [(4, frows, D)]
    dma = pltpu.SemaphoreType.DMA
    hbm, vmem = pl.BlockSpec(memory_space=pl.ANY), pl.BlockSpec(memory_space=pltpu.VMEM)

    def kernel(*refs):
        front_kernel(ctxs, refs)

    return pl.pallas_call(
        kernel,
        out_shape=[jax.ShapeDtypeStruct(shape, BF) for shape in shapes]
        + [jax.ShapeDtypeStruct((4, team, 8, 128), F32)],
        in_specs=[hbm] * 3 + [vmem] * 4,
        out_specs=[hbm] * len(shapes) + [vmem],
        scratch_shapes=[pltpu.VMEM(shape, BF) for shape in shapes]
        + [pltpu.VMEM((frows, D), F32)]
        + [dma((3,)), dma((5 * team + 2,)), dma((2, team + 2))]
        + Gather.scratch(ctxs, 2, 2),
        compiler_params=pltpu.CompilerParams(
            collective_id=0, has_side_effects=True, vmem_limit_bytes=VMEM_LIMIT
        ),
        cost_estimate=pl.CostEstimate(
            flops=6 * team * own * D * feats, bytes_accessed=40 * own * D, transcendentals=0
        ),
        name="front",
    )(tokens, qkv, mlp, packed, *tables)


def attend_part(q_ref, k_ref, v_ref, col_ref, row_ref, l_ref, put, start, length, pair, unit):
    lanes = pl.ds(pl.multiple_of(pair * 128, 128), 128)
    for first in range(0, length, BLOCK):
        keys = first + BLOCK
        rows = pl.ds(pl.multiple_of(start + first, BLOCK), BLOCK)
        past = pl.ds(pl.multiple_of(start, BLOCK), keys)
        same = col_ref[rows, :] == row_ref[:, 0:keys]
        query_place = first + lax.broadcasted_iota(jnp.int32, (BLOCK, keys), 0)
        key_place = lax.broadcasted_iota(jnp.int32, (BLOCK, keys), 1)
        allowed = same & (key_place <= query_place)
        query, key, value = q_ref[rows, lanes], k_ref[past, lanes], v_ref[past, lanes]
        parts = []
        for head in range(128 // HD):
            cut = slice(head * HD, (head + 1) * HD)
            scores = mm(query[:, cut] * HD ** (-0.5), key[:, cut], 1, 1)
            scores = jnp.where(allowed, scores, MASKED)
            highest = jnp.max(scores, -1, keepdims=True)
            shifted = jnp.exp(scores - highest)
            totals = jnp.sum(shifted, -1, keepdims=True)
            weights = (shifted * (1.0 / totals)).astype(BF)
            parts.append(mm(weights, value[:, cut], 1, 0))
            l_ref[unit + head, first:keys, :] = highest + jnp.log(totals)
        put(rows, lanes, jnp.concatenate(parts, 1).astype(BF))


def second_kernel(ctxs, refs):
    q_ref, k_ref, v_ref, col_ref, row_ref, proj, mlp = refs[:7]
    o_out, p_out, d_out, l_ref = refs[7:11]
    outs, ps, ds_, wide, load, store = refs[11:17]
    count, feats = q_ref.shape
    seq = count // 2
    pairs = feats // 128
    plane = lax.axis_index("plane")
    pieces = [(outs, pl.ds(0, seq)), (outs, pl.ds(seq, seq)), (ps, plane)]
    net = Gather(ctxs, pieces, [("block", ds_), ("half", ps)], refs[17:])
    core, ctx = net.core, net.ctx
    me = core * ctxs + ctx
    loads = [
        pltpu.make_async_copy(proj, ps.at[me, plane], load.at[0]),
        pltpu.make_async_copy(mlp.at[1], wide, load.at[1]),
    ]
    for copy in loads:
        copy.start()
    greet_all(net.peers())
    loads[0].wait()
    net.send_own([2])
    loads[1].wait()

    def narrow(g, carry):
        part = pl.ds(pl.multiple_of(g * 16, 16), 16)
        ds_[plane, part, :] = wide[part, :].astype(BF)
        return carry

    lax.fori_loop(0, wide.shape[0] // 16, narrow, 0)
    net.board_start(0)

    def put(rows, lanes, values):
        outs[me, rows, lanes] = values

    hops = list(range(1, ctxs))
    for s in range(2):
        for pair in range(pairs):
            attend_part(
                q_ref, k_ref, v_ref, col_ref, row_ref.at[s], l_ref, put,
                s * seq, seq, pair, (s * pairs + pair) * (128 // HD),
            )
            if s * pairs + pair == 2 * pairs - 1:
                net.send_own([1])
            if hops:
                net.hop(hops.pop(0), [2])
                if not hops:
                    net.board_start(1)
            if s * pairs + pair == pairs - 1:
                net.send_own([0])
                net.board_pass(0)
    for k in hops:
        net.hop(k, [2])
    if hops:
        net.board_start(1)

    def copy_out(b):
        return pltpu.make_async_copy(outs.at[b], o_out.at[b], store.at[b])

    copy_out(me).start()
    for k in range(1, ctxs):
        net.hop(k, [0])
        if k == 2 or ctxs == 2:
            net.board_pass(1)
        net.hop(k, [1])
        net.distant(k, lambda block: copy_out(core * ctxs + block).start())
        net.side_arrive(k - 1, [0, 1])
        if k == 1:
            copy_out((1 - core) * ctxs + ctx).start()
            net.board_finish(0)
        else:
            net.distant(k - 1, lambda block: copy_out((1 - core) * ctxs + block).start())
    tail = [
        pltpu.make_async_copy(ds_, d_out, store.at[2 * ctxs]),
        pltpu.make_async_copy(ps, p_out, store.at[2 * ctxs + 1]),
    ]
    tail[0].start()
    for k in range(ctxs):
        net.side_arrive(k, [2])
    net.board_finish(1)
    net.board_shared(1)
    tail[1].start()
    net.side_arrive(ctxs - 1, [0, 1])
    net.distant(ctxs - 1, lambda block: copy_out((1 - core) * ctxs + block).start())
    net.close()
    for copy in tail:
        copy.wait()
    for b in range(2 * ctxs):
        copy_out(b).wait()


def second_call(ctxs, query, key, value, col, row, proj, mlp):
    team = 2 * ctxs
    count, feats = query.shape
    seq = count // 2
    arows, frows = proj.shape[0], mlp.shape[1]
    shapes = [(team, count, feats), (team, 4, arows, D), (4, frows, D)]
    dma = pltpu.SemaphoreType.DMA
    hbm, vmem = pl.BlockSpec(memory_space=pl.ANY), pl.BlockSpec(memory_space=pltpu.VMEM)

    def kernel(*refs):
        second_kernel(ctxs, refs)

    return pl.pallas_call(
        kernel,
        out_shape=[jax.ShapeDtypeStruct(shape, BF) for shape in shapes]
        + [jax.ShapeDtypeStruct((2 * feats // HD, seq, 1), F32)],
        in_specs=[vmem] * 5 + [hbm] * 2,
        out_specs=[hbm] * 3 + [vmem],
        scratch_shapes=[pltpu.VMEM(shape, BF) for shape in shapes]
        + [pltpu.VMEM((frows, D), F32)]
        + [dma((2,)), dma((team + 2,))]
        + Gather.scratch(ctxs, 3, 2),
        compiler_params=pltpu.CompilerParams(
            collective_id=2, has_side_effects=True, vmem_limit_bytes=VMEM_LIMIT
        ),
        cost_estimate=pl.CostEstimate(
            flops=4 * count * seq * feats, bytes_accessed=24 * count * feats, transcendentals=0
        ),
        name="second",
    )(query, key, value, col, row, proj, mlp)


def third_kernel(ctxs, refs):
    att, proj, x_all, gain, gate, up, down, dy = refs[:8]
    m_out, a_out, n_out, o_out, g_out, u_out, d_out = refs[8:15]
    pv, gv, uv, dv, ys, hs, gs, us, ob, xb, nb, sb = refs[15:27]
    load, block_sem, store, late = refs[27:31]
    team, own = ys.shape[0], ys.shape[1]
    wide = gv.shape[0]
    pieces = [(ys, pl.ds(0, own // 2)), (ys, pl.ds(own // 2, own // 2))]
    net = Gather(ctxs, pieces, [("block", dv)], refs[31:])
    plane, core, ctx = net.plane, net.core, net.ctx
    me = core * ctxs + ctx
    loads = [
        pltpu.make_async_copy(dy, ys.at[me], load.at[0]),
        pltpu.make_async_copy(down, dv.at[plane], load.at[1]),
        pltpu.make_async_copy(proj, pv, load.at[2]),
        pltpu.make_async_copy(gate, gv, load.at[3]),
        pltpu.make_async_copy(up, uv, load.at[4]),
    ]

    def fetch(i):
        slot = lax.rem(i, 2)
        rows = pl.ds(pl.multiple_of(i * own, own), own)
        return (
            pltpu.make_async_copy(att.at[:, rows], ob.at[slot], block_sem.at[0, slot]),
            pltpu.make_async_copy(x_all.at[i], xb.at[slot], block_sem.at[1, slot]),
        )

    def n_store(i):
        return pltpu.make_async_copy(nb.at[lax.rem(i, 2)], n_out.at[i], store.at[0, lax.rem(i, 2)])

    def s_store(i, out):
        return pltpu.make_async_copy(sb.at[lax.rem(i, 2)], out.at[i], store.at[1, lax.rem(i, 2)])

    for copy in loads:
        copy.start()
    for copy in fetch(0):
        copy.start()
    greet_all(net.peers())
    loads[0].wait()
    net.send_own([0, 1])
    loads[1].wait()
    net.board_start(0)
    for copy in loads[2:]:
        copy.wait()

    steps = [(hop, chunk) for hop in range(1, ctxs) for chunk in range(2)]
    stages = []
    for i, step in enumerate(steps[: 2 * (ctxs - 2)] if ctxs > 2 else []):
        stages.append((min(2 * i + 1, team - 1), step))

    def forward(i, carry):
        slot = lax.rem(i, 2)
        for copy in fetch(i):
            copy.wait()

        @pl.when(i + 1 < team)
        def _():
            for copy in fetch(i + 1):
                copy.start()

        total = xb[slot].astype(F32)
        for t in range(team):
            total = total + mm(ob[slot, t], pv[t], 1, 0)

        @pl.when(i >= 2)
        def _():
            n_store(i - 2).wait()

        nb[slot] = (total * norm_scale(total) * gain[...]).astype(BF)
        n_store(i).start()

        @pl.when(i == me)
        def _():
            m_out[...] = total
            keep = pltpu.make_async_copy(ob.at[slot], a_out, late.at[0])
            keep.start()
            keep.wait()

        normed = nb[slot]
        for first in range(0, wide, 512):
            part = slice(first, first + 512)
            g = mm(normed, gv[part, :], 1, 1)
            u = mm(normed, uv[part, :], 1, 1)
            sig = 1.0 / (1.0 + jnp.exp(-g))
            lit = g * sig
            hs[i, :, part] = (lit * u).astype(BF)
            gs[i, :, part] = (u * sig * (1.0 + g * (1.0 - sig))).astype(BF)
            us[i, :, part] = lit.astype(BF)
        for at, (hop, chunk) in stages:

            @pl.when(i == at)
            def _():
                net.hop(hop, [chunk])

        @pl.when(i == 1)
        def _():
            net.board_pass(0)

        return carry

    lax.fori_loop(0, team, forward, 0)
    n_store(team - 2).wait()
    n_store(team - 1).wait()
    net.board_finish(0)

    def outward(i, carry):
        @pl.when(i >= 2)
        def _():
            s_store(i - 2, o_out).wait()

        sb[lax.rem(i, 2)] = mm(hs[i], dv[...].reshape(wide, D), 1, 0).astype(BF)
        s_store(i, o_out).start()

        @pl.when(i == team // 2)
        def _():
            net.hop(ctxs - 1, [0])

        return carry

    def backward(side_core):
        def action(block):
            b = side_core * ctxs + block
            for p in range(4):
                cols = slice(p * (wide // 4), (p + 1) * (wide // 4))
                dh = mm(ys[b], dv[p], 1, 1)
                gs[b, :, cols] = (dh * gs[b, :, cols].astype(F32)).astype(BF)
                us[b, :, cols] = (dh * us[b, :, cols].astype(F32)).astype(BF)
            pltpu.make_async_copy(gs.at[b], g_out.at[b], late.at[1 + b]).start()
            pltpu.make_async_copy(us.at[b], u_out.at[b], late.at[1 + team + b]).start()

        return action

    if ctxs == 2:
        lax.fori_loop(0, team, outward, 0)
    else:
        lax.fori_loop(0, team, outward, 0)
    s_store(team - 2, o_out).wait()
    s_store(team - 1, o_out).wait()
    backward(core)(ctx)
    net.side_arrive(0, [0, 1])
    backward(1 - core)(ctx)
    net.hop(ctxs - 1, [1])
    for k in range(1, ctxs):
        net.distant(k, backward(core))
        net.side_arrive(k, [0, 1])
        net.distant(k, backward(1 - core))
    for p in range(4):
        if p >= 2:
            s_store(p - 2, d_out).wait()
        hidden = hs[:, :, p * (wide // 4) : (p + 1) * (wide // 4)].reshape(team * own, wide // 4)
        sb[p % 2] = mm(hidden, ys[...].reshape(team * own, D), 0, 0).astype(BF)
        s_store(p, d_out).start()
    s_store(2, d_out).wait()
    s_store(3, d_out).wait()
    net.close()
    for b in range(team):
        pltpu.make_async_copy(gs.at[b], g_out.at[b], late.at[1 + b]).wait()
        pltpu.make_async_copy(us.at[b], u_out.at[b], late.at[1 + team + b]).wait()


def third_call(ctxs, att, proj, x_all, gain, gate, up, down, dy):
    team, own, wide = 2 * ctxs, dy.shape[0], gate.shape[0]
    feats = proj.shape[1]
    block, hidden = (team, own, D), (team, own, wide)
    shapes = [(team, own, feats), block, block, hidden, hidden, (4, wide // 4, D)]
    dma = pltpu.SemaphoreType.DMA
    hbm, vmem = pl.BlockSpec(memory_space=pl.ANY), pl.BlockSpec(memory_space=pltpu.VMEM)
    held = [proj.shape, gate.shape, up.shape, (4, wide // 4, D), block, hidden, hidden, hidden]
    held += [(2, team, own, feats), (2, own, D), (2, own, D), (2, own, D)]

    def kernel(*refs):
        third_kernel(ctxs, refs)

    return pl.pallas_call(
        kernel,
        out_shape=[jax.ShapeDtypeStruct((own, D), F32)]
        + [jax.ShapeDtypeStruct(shape, BF) for shape in shapes],
        in_specs=[hbm] * 3 + [vmem] + [hbm] * 4,
        out_specs=[vmem] + [hbm] * len(shapes),
        scratch_shapes=[pltpu.VMEM(shape, BF) for shape in held]
        + [dma((5,)), dma((2, 2)), dma((2, 2)), dma((2 * team + 1,))]
        + Gather.scratch(ctxs, 2, 1),
        compiler_params=pltpu.CompilerParams(
            collective_id=6, has_side_effects=True, vmem_limit_bytes=VMEM_LIMIT
        ),
        cost_estimate=pl.CostEstimate(
            flops=2 * team * own * D * (D + 5 * wide),
            bytes_accessed=30 * own * D,
            transcendentals=0,
        ),
        name="third",
    )(att, proj, x_all, gain, gate, up, down, dy)


class Cargo:
    def __init__(self, arrays, refs):
        refs = list(refs)
        self.parts = []
        for array in arrays:
            ref = None if Cargo.made(array) else refs.pop(0)
            self.parts += [None if ref is None else ref.at[i] for i in range(array.shape[0])]
        count = len(self.parts)
        self.sums, refs = refs[:count], refs[count:]
        self.kept, refs = refs[:count], refs[count:]
        self.got, refs = refs[:count], refs[count:]
        self.last, refs = refs[:count], refs[count:]
        self.load, self.one, self.two = refs
        self.plane, self.core, self.ctx = (
            lax.axis_index("plane"),
            lax.axis_index("core"),
            lax.axis_index("ctx"),
        )
        self.near = (
            self.plane + 1 - 2 * lax.rem(self.plane, 2),
            lax.rem(self.plane + 2, 4),
        )

    @staticmethod
    def made(array):
        return isinstance(array, jax.ShapeDtypeStruct)

    @staticmethod
    def given(arrays):
        return [array for array in arrays if not Cargo.made(array)]

    def peers(self):
        return [(near, self.core, self.ctx) for near in self.near]

    def rows(self, s, half):
        size = self.kept[s].shape[1] // 2
        return pl.ds(half * size, size)

    def remote(self, source, target, sems, index, near):
        return pltpu.make_async_remote_copy(
            src_ref=source,
            dst_ref=target,
            send_sem=sems.at[(0,) + index],
            recv_sem=sems.at[(1,) + index],
            device_id=(near, self.core, self.ctx),
            device_id_type=MESH_ID,
        )

    def first(self, half, s, b):
        block = self.near[half] if b == 0 else 3 - self.plane
        source = self.kept[s].at[block, self.rows(s, half)]
        target = self.got[s].at[half, b]
        return self.remote(source, target, self.one, (half, s, b), self.near[half])

    def fetch(self, s):
        return pltpu.make_async_copy(self.parts[s], self.kept[s], self.load.at[s])

    def second(self, half, s):
        source = self.kept[s].at[self.near[1 - half], self.rows(s, half)]
        target = self.last[s].at[half]
        return self.remote(source, target, self.two, (half, s), self.near[1 - half])

    def begin(self):
        for s in range(len(self.parts)):
            if self.parts[s] is not None:
                self.fetch(s).start()

    def start(self, slots=None):
        for s in range(len(self.parts)) if slots is None else slots:
            if self.parts[s] is not None:
                self.fetch(s).wait()
            for b in (1, 0):
                for half in range(2):
                    self.first(half, s, b).start()

    def middle(self, s):
        kept, got = self.kept[s], self.got[s]
        size = got.shape[2]
        for half in range(2):
            block = self.near[1 - half]
            self.first(half, s, 1).wait_recv()

            def group(g, carry):
                part = pl.ds(pl.multiple_of(g * 16, 16), 16)
                rows = pl.ds(pl.multiple_of(half * size + g * 16, 16), 16)
                total = kept[block, rows, :].astype(F32) + got[half, 1, part, :].astype(F32)
                kept[block, rows, :] = total.astype(BF)
                return carry

            lax.fori_loop(0, size // 16, group, 0)
            self.second(half, s).start()

    def end(self):
        for s in range(len(self.parts)):
            kept, got, last, sums = self.kept[s], self.got[s], self.last[s], self.sums[s]
            size = got.shape[2]
            for half in range(2):
                self.first(half, s, 0).wait_recv()
                self.second(half, s).wait_recv()

                def group(g, carry):
                    part = pl.ds(pl.multiple_of(g * 16, 16), 16)
                    rows = pl.ds(pl.multiple_of(half * size + g * 16, 16), 16)
                    total = kept[self.plane, rows, :].astype(F32)
                    total = total + got[half, 0, part, :].astype(F32)
                    total = total + last[half, part, :].astype(F32)
                    sums[rows, :] = total
                    return carry

                lax.fori_loop(0, size // 16, group, 0)
        for s in range(len(self.parts)):
            for half in range(2):
                self.first(half, s, 0).wait_send()
                self.first(half, s, 1).wait_send()
                self.second(half, s).wait_send()

    @staticmethod
    def rows_of(arrays):
        return [array.shape[2] for array in arrays for _ in range(array.shape[0])]

    @staticmethod
    def out_shapes(arrays):
        return [jax.ShapeDtypeStruct((rows, D), F32) for rows in Cargo.rows_of(arrays)]

    @staticmethod
    def scratch(arrays):
        rows = Cargo.rows_of(arrays)
        if not rows:
            return []
        dma = pltpu.SemaphoreType.DMA
        return (
            [pltpu.VMEM((4, r, D), BF) for r in rows]
            + [pltpu.VMEM((2, 2, r // 2, D), BF) for r in rows]
            + [pltpu.VMEM((2, r // 2, D), BF) for r in rows]
            + [dma((len(rows),)), dma((2, 2, len(rows), 2)), dma((2, 2, len(rows)))]
        )


def team_sum_kernel(ctxs, pairs, refs, cargo, more):
    lhs, rhs, out_ref = refs[:pairs], refs[pairs : 2 * pairs], refs[2 * pairs]
    refs = refs[2 * pairs + 1 :]
    lhs_v, rhs_v = refs[:pairs], refs[pairs : 2 * pairs]
    staged, theirs, mine, from_left, from_right, load, side, hops = refs[2 * pairs :]
    plane, core, ctx = lax.axis_index("plane"), lax.axis_index("core"), lax.axis_index("ctx")
    last = ctxs - 1
    away = last - ctx
    own = out_ref.shape[0]
    rows = own // CHUNKS
    other = (plane, 1 - core, ctx)
    loads = []
    for i in range(pairs):
        loads.append(pltpu.make_async_copy(rhs[i], rhs_v[i], load.at[0, i]))
        loads.append(pltpu.make_async_copy(lhs[i], lhs_v[i], load.at[1, i]))
    for copy in loads:
        copy.start()
    if cargo:
        cargo.begin()
    greet_all(
        [other]
        + [(plane, core, lax.rem(ctx + k, ctxs)) for k in range(1, ctxs)]
        + (cargo.peers() if cargo else [])
    )
    pending = list(range(len(cargo.parts))) if cargo else []
    ready = [i for i in pending if cargo.parts[i] is not None]
    if cargo:
        cargo.start(ready)
    for copy in loads:
        copy.wait()
    fills = []
    if more:
        other_in, other_v, made, tiles, sems = more
        other_copy = pltpu.make_async_copy(other_in, other_v, sems.at[2])
        other_copy.start()
        if made:

            def store(i, p):
                slot = (4 * i + p) % 2
                return pltpu.make_async_copy(tiles.at[slot], made[i].at[0, p], sems.at[slot])

            def tile(i, p):
                size = lhs_v[i].shape[1] // 4
                index = 4 * i + p
                if index >= 2:
                    store((index - 2) // 4, (index - 2) % 4).wait()
                part = lhs_v[i][:, p * size : (p + 1) * size]
                tiles[index % 2] = mm(part, other_v[...], 0, 0).astype(BF)
                store(i, p).start()

            fills = [functools.partial(tile, i, p) for i in range(len(made)) for p in range(4)]

    def produce(block, target):
        where = pl.ds(pl.multiple_of(block * own, own), own)

        def tile(t, carry):
            cols = pl.ds(pl.multiple_of(t * 512, 512), 512)
            total = mm(lhs_v[0][where, :], rhs_v[0][:, cols], 1, 0)
            for i in range(1, pairs):
                total = total + mm(lhs_v[i][where, :], rhs_v[i][:, cols], 1, 0)
            target[:, cols] = total.astype(BF)
            return carry

        lax.fori_loop(0, D // 512, tile, 0)

    def add(index, chunk, extra, slot):
        def group(g, carry):
            part = pl.ds(pl.multiple_of(chunk * rows + g * 16, 16), 16)
            total = mine[index, part, :].astype(F32) + theirs[index, part, :].astype(F32)
            if extra is not None:
                total = total + extra[slot, part, :].astype(F32)
            mine[index, part, :] = total.astype(BF)
            return carry

        lax.fori_loop(0, rows // 16, group, 0)

    def share(index):
        return pltpu.make_async_remote_copy(
            src_ref=staged.at[index],
            dst_ref=theirs.at[index],
            send_sem=side.at[0, index],
            recv_sem=side.at[1, index],
            device_id=other,
            device_id_type=MESH_ID,
        )

    def hop(way, slot, chunk, index):
        part = pl.ds(chunk * rows, rows)
        inbox = from_left if way == 0 else from_right
        return pltpu.make_async_remote_copy(
            src_ref=mine.at[index, part],
            dst_ref=inbox.at[slot, part],
            send_sem=hops.at[0, way, slot, chunk],
            recv_sem=hops.at[1, way, slot, chunk],
            device_id=(plane, core, ctx + 1 if way == 0 else ctx - 1),
            device_id_type=MESH_ID,
        )

    order = []
    for i in range((ctxs + 1) // 2):
        order += [last - i, i] if last - i != i else [i]
    for place in order:
        index = jnp.where(2 * ctx >= ctxs, last - place, place)
        produce((1 - core) * ctxs + index, staged.at[index])
        share(index).start()
        produce(core * ctxs + index, mine.at[index])

        if place > 0:

            @pl.when(ctx == 0)
            def _():
                share(place).wait_recv()
                for chunk in range(CHUNKS):
                    add(place, chunk, None, 0)
                    hop(0, ctxs - place, chunk, place).start()

            @pl.when(ctx == last)
            def _():
                share(last - place).wait_recv()
                for chunk in range(CHUNKS):
                    add(last - place, chunk, None, 0)
                    hop(1, ctxs - place, chunk, last - place).start()

    if more:
        other_copy.wait()
        if not made:
            fresh = [i for i in pending if cargo.parts[i] is None]
            for i, slot in enumerate(fresh):
                size = lhs_v[i].shape[1]
                product = mm(lhs_v[i][...], other_v[...], 0, 0).astype(BF)
                cargo.kept[slot][...] = product.reshape(4, size // 4, D)
                cargo.start([slot])

    for step in range(1, last):

        @pl.when((ctx > 0) & (step >= ctx))
        def _():
            index = last + ctx - step
            share(index).wait_recv()
            for chunk in range(CHUNKS):
                hop(0, step, chunk, index).wait_recv()
                add(index, chunk, from_left, step)

                @pl.when(ctx < last)
                def _():
                    hop(0, step + 1, chunk, index).start()

        @pl.when((away > 0) & (step >= away))
        def _():
            index = step - away
            share(index).wait_recv()
            for chunk in range(CHUNKS):
                hop(1, step, chunk, index).wait_recv()
                add(index, chunk, from_right, step)

                @pl.when(ctx > 0)
                def _():
                    hop(1, step + 1, chunk, index).start()

        for fill in fills[:3]:
            fill()
        fills = fills[3:]
        if pending:
            cargo.middle(pending.pop(0))
    for fill in fills:
        fill()
    for s in pending:
        cargo.middle(s)

    share(ctx).wait_recv()

    def close(way):
        for chunk in range(CHUNKS):
            hop(way, last, chunk, ctx).wait_recv()

    def finish(inboxes):
        def group(g, carry):
            part = pl.ds(pl.multiple_of(g * 16, 16), 16)
            total = mine[ctx, part, :].astype(F32) + theirs[ctx, part, :].astype(F32)
            for inbox in inboxes:
                total = total + inbox[last, part, :].astype(F32)
            out_ref[part, :] = total
            return carry

        lax.fori_loop(0, own // 16, group, 0)

    @pl.when(ctx == 0)
    def _():
        close(1)
        finish([from_right])

    @pl.when(ctx == last)
    def _():
        close(0)
        finish([from_left])

    @pl.when((ctx > 0) & (ctx < last))
    def _():
        close(0)
        close(1)
        finish([from_left, from_right])

    for index in range(ctxs):
        share(index).wait_send()
    for slot in range(1, ctxs):

        @pl.when((ctx < last) & (slot >= ctx + 1))
        def _():
            for chunk in range(CHUNKS):
                hop(0, slot, chunk, ctxs + ctx - slot).wait_send()

        @pl.when((ctx > 0) & (slot >= away + 1))
        def _():
            for chunk in range(CHUNKS):
                hop(1, slot, chunk, slot - 1 - away).wait_send()

    if more and made:
        store(len(made) - 1, 2).wait()
        store(len(made) - 1, 3).wait()
    if cargo:
        cargo.end()


def team_sum(ctxs, number, pairs, name, freight=(), other=None, outer=False):
    count = pairs[0][0].shape[0]
    own = count // (2 * ctxs)
    lhs, rhs = [a for a, _ in pairs], [b for _, b in pairs]
    dma = pltpu.SemaphoreType.DMA

    inputs = 2 * len(pairs)
    given = Cargo.given(freight)
    outputs = 1 + len(Cargo.rows_of(freight))
    scratch = [pltpu.VMEM(a.shape, BF) for a in lhs + rhs]
    scratch += [pltpu.VMEM((ctxs, own, D), BF)] * 5
    scratch += [dma((2, len(pairs))), dma((2, ctxs)), dma((2, 2, ctxs, CHUNKS))]
    made = [(1, 4, a.shape[1] // 4, D) for a in lhs] if outer else []
    extra = [other] if other is not None else []
    held = [pltpu.VMEM(a.shape, BF) for a in extra]
    held += [pltpu.VMEM((2,) + made[0][2:], BF)] if made else []
    held += [dma((3,))] if extra else []

    def kernel(*refs):
        ins, refs = refs[:inputs], refs[inputs:]
        parts, refs = refs[: len(given)], refs[len(given) :]
        more, refs = refs[: len(extra)], refs[len(extra) :]
        outs, refs = refs[:outputs], refs[outputs:]
        products, refs = refs[: len(made)], refs[len(made) :]
        mine, refs = refs[: len(scratch)], refs[len(scratch) :]
        spare, buffers = refs[: len(refs) - len(held)], refs[len(refs) - len(held) :]
        cargo = Cargo(freight, parts + outs[1:] + spare) if freight else None
        if more:
            tiles = buffers[1] if made else None
            more = (more[0], buffers[0], products, tiles, buffers[-1])
        team_sum_kernel(ctxs, len(pairs), ins + outs[:1] + mine, cargo, more)

    depth = sum(b.shape[0] for b in rhs)
    return pl.pallas_call(
        kernel,
        out_shape=[jax.ShapeDtypeStruct((own, D), F32)]
        + Cargo.out_shapes(freight)
        + [jax.ShapeDtypeStruct(shape, BF) for shape in made],
        in_specs=[pl.BlockSpec(memory_space=pl.ANY)] * (inputs + len(given) + len(extra)),
        out_specs=[pl.BlockSpec(memory_space=pltpu.VMEM)] * outputs
        + [pl.BlockSpec(memory_space=pl.ANY)] * len(made),
        scratch_shapes=scratch + Cargo.scratch(freight) + held,
        compiler_params=pltpu.CompilerParams(
            collective_id=number, has_side_effects=True, vmem_limit_bytes=VMEM_LIMIT
        ),
        cost_estimate=pl.CostEstimate(
            flops=2 * count * depth * D,
            bytes_accessed=2 * (count + D) * depth + 4 * own * D,
            transcendentals=0,
        ),
        name=name,
    )(*lhs, *rhs, *given, *extra)


def middle_kernel(ctxs, refs, freight):
    da, att, proj, out_part = refs[:4]
    refs = refs[4:]
    part, grad, joined, outs = refs[0], refs[1], refs[2], refs[3 : 3 + ctxs]
    first, sums, refs = refs[3 + ctxs], refs[4 + ctxs], refs[5 + ctxs :]
    pv, ov, sent, staged, mine, theirs, others, load, swap, side, shift = refs[:11]
    cargo = Cargo(freight, [part, sums] + list(refs[11:]))
    plane, core, ctx = cargo.plane, cargo.core, cargo.ctx
    me = core * ctxs + ctx
    loads = [
        pltpu.make_async_copy(proj, pv, load.at[0]),
        pltpu.make_async_copy(out_part, ov, load.at[1]),
    ]
    for copy in loads:
        copy.start()
    cargo.begin()
    partners = [
        (dc, dz) for dz in range(ctxs - 1, -1, -1) for dc in range(2) if dc + dz > 0
    ]

    def partner(dc, dz):
        return (core if dc == 0 else 1 - core, lax.rem(ctx + dz, ctxs))

    greet_all([(plane,) + partner(*step) for step in partners] + cargo.peers())
    cargo.start()
    loads[0].wait()

    def remote(source, target, sems, index, peer):
        return pltpu.make_async_remote_copy(
            src_ref=source,
            dst_ref=target,
            send_sem=sems.at[(0,) + index],
            recv_sem=sems.at[(1,) + index],
            device_id=(plane,) + peer,
            device_id_type=MESH_ID,
        )

    def piece(i, c, z, home):
        return remote(sent.at[c * ctxs + z], grad.at[home], swap, (i,), (c, z))

    for i, step in enumerate(partners):
        c, z = partner(*step)
        sent[c * ctxs + z] = mm(da[...], pv[c * ctxs + z], 1, 1).astype(BF)
        piece(i, c, z, me).start()
    grad[me] = mm(da[...], pv[me], 1, 1).astype(BF)
    loads[1].wait()

    def share(kind, z):
        source = ov.at[(1 - core) * ctxs + z] if kind == 0 else staged.at[z]
        target = others.at[z] if kind == 0 else theirs.at[z]
        return remote(source, target, side, (kind, z), (1 - core, ctx))

    for z in range(ctxs):
        share(0, z).start()
    for z in range(ctxs):
        staged[z] = mm(att[(1 - core) * ctxs + z], da[...], 0, 0).astype(BF)
        share(1, z).start()
    for z in range(ctxs):
        mine[z] = mm(att[core * ctxs + z], da[...], 0, 0).astype(BF)
    size = pv.shape[1]
    for k in list(range(1, ctxs)) + [0]:
        z = lax.rem(ctx + k, ctxs)
        share(0, z).wait_recv()
        target = outs[k - 1]

        def group(g, carry):
            part_ = pl.ds(pl.multiple_of(g * 16, 16), 16)
            total = ov[core * ctxs + z, part_, :].astype(F32) + others[z, part_, :].astype(F32)
            target[part_, :] = total.astype(BF)
            return carry

        lax.fori_loop(0, target.shape[0] // 16, group, 0)
        if k == 1:
            pass_on = remote(outs[0], first, shift, (0,), (core, z))
            pass_on.start()
    cargo.middle(0)
    for z in range(ctxs):
        share(1, z).wait_recv()
        for p in range(4):

            def group(g, carry):
                rows = pl.ds(pl.multiple_of(p * (size // 4) + g * 16, 16), 16)
                total = mine[z, rows, :].astype(F32) + theirs[z, rows, :].astype(F32)
                joined[p, z, pl.ds(pl.multiple_of(g * 16, 16), 16), :] = total.astype(BF)
                return carry

            lax.fori_loop(0, size // 64, group, 0)
    for i, (dc, dz) in enumerate(partners):
        c, z = core if dc == 0 else 1 - core, lax.rem(ctx + ctxs - dz, ctxs)
        piece(i, c, z, c * ctxs + z).wait_recv()
    cargo.end()
    pass_on.wait()
    for i, step in enumerate(partners):
        c, z = partner(*step)
        piece(i, c, z, me).wait_send()
    for z in range(ctxs):
        share(0, z).wait_send()
        share(1, z).wait_send()


def middle_call(ctxs, da, att, proj, out_part, part):
    team, own = 2 * ctxs, da.shape[0]
    feats = proj.shape[1]
    freight = (part,)
    dma = pltpu.SemaphoreType.DMA
    hbm, vmem = pl.BlockSpec(memory_space=pl.ANY), pl.BlockSpec(memory_space=pltpu.VMEM)
    block = (ctxs, own, D)

    def kernel(*refs):
        middle_kernel(ctxs, refs, freight)

    return pl.pallas_call(
        kernel,
        out_shape=[
            jax.ShapeDtypeStruct((team, own, feats), BF),
            jax.ShapeDtypeStruct((4, ctxs, feats // 4, D), BF),
        ]
        + [jax.ShapeDtypeStruct((own, D), BF)] * (ctxs + 1)
        + Cargo.out_shapes(freight),
        in_specs=[vmem, vmem, hbm, hbm, hbm],
        out_specs=[vmem] * (4 + ctxs),
        scratch_shapes=[
            pltpu.VMEM(proj.shape, BF),
            pltpu.VMEM(out_part.shape, BF),
            pltpu.VMEM((team, own, feats), BF),
            pltpu.VMEM((ctxs, feats, D), BF),
            pltpu.VMEM((ctxs, feats, D), BF),
            pltpu.VMEM((ctxs, feats, D), BF),
            pltpu.VMEM(block, BF),
            dma((2,)),
            dma((2, team - 1)),
            dma((2, 2, ctxs)),
            dma((2, 1)),
        ]
        + Cargo.scratch(freight),
        compiler_params=pltpu.CompilerParams(
            collective_id=7, has_side_effects=True, vmem_limit_bytes=VMEM_LIMIT
        ),
        cost_estimate=pl.CostEstimate(
            flops=4 * own * D * D, bytes_accessed=60 * own * D, transcendentals=0
        ),
        name="middle",
    )(da, att, proj, out_part, part)


def qkv_kernel(feats, x_ref, gain_ref, w_ref, c_ref, a_ref, b_ref, n_ref, q_ref, k_ref, v_ref):
    values = x_ref[...].astype(F32)
    normed = (values * norm_scale(values) * gain_ref[...]).astype(BF)
    n_ref[...] = normed
    cosine, low_sine, high_sine = [widen(ref[...], feats) for ref in (c_ref, a_ref, b_ref)]
    q = mm(normed, w_ref[0:feats], 1, 1)
    q_ref[...] = rope(q, cosine, low_sine, high_sine).astype(BF)
    k = mm(normed, w_ref[feats : 2 * feats], 1, 1)
    k_ref[...] = rope(k, cosine, low_sine, high_sine).astype(BF)
    v_ref[...] = mm(normed, w_ref[2 * feats :], 1, 1).astype(BF)


def qkv_call(x_all, gain, weights, tables):
    count = x_all.shape[0]
    feats = weights.shape[0] // 3
    turns = tables[0].shape[0] // BLOCK
    rows = pl.BlockSpec((BLOCK, D), lambda i: (i, 0))
    part = pl.BlockSpec((BLOCK, feats), lambda i: (i, 0))
    table = pl.BlockSpec((BLOCK, 128), lambda i: (i % turns, 0))
    out = jax.ShapeDtypeStruct((count, feats), BF)
    return pl.pallas_call(
        functools.partial(qkv_kernel, feats),
        grid=(count // BLOCK,),
        out_shape=(jax.ShapeDtypeStruct((count, D), BF), out, out, out),
        in_specs=[
            rows,
            pl.BlockSpec((1, D), lambda i: (0, 0)),
            pl.BlockSpec((3 * feats, D), lambda i: (0, 0)),
            table,
            table,
            table,
        ],
        out_specs=(rows, part, part, part),
        compiler_params=params(),
        cost_estimate=pl.CostEstimate(
            flops=6 * count * D * feats, bytes_accessed=4 * count * D, transcendentals=0
        ),
        name="qkv",
    )(x_all, gain, weights, *tables)


def allowed_keys(col_ref, row_ref, first, size, keys):
    same = col_ref[first : first + size, :] == row_ref[:, 0:keys]
    query_place = first + lax.broadcasted_iota(jnp.int32, (size, keys), 0)
    key_place = lax.broadcasted_iota(jnp.int32, (size, keys), 1)
    return same & (key_place <= query_place)


def attend_kernel(q_ref, k_ref, v_ref, col_ref, row_ref, o_ref, l_ref):
    length = q_ref.shape[0]
    for first in range(0, length, BLOCK):
        keys = first + BLOCK
        allowed = allowed_keys(col_ref, row_ref, first, BLOCK, keys)
        parts = []
        for head in range(q_ref.shape[1] // HD):
            lanes = slice(head * HD, (head + 1) * HD)
            query = q_ref[first:keys, lanes] * HD ** (-0.5)
            scores = jnp.where(allowed, mm(query, k_ref[0:keys, lanes], 1, 1), MASKED)
            highest = jnp.max(scores, -1, keepdims=True)
            shifted = jnp.exp(scores - highest)
            totals = jnp.sum(shifted, -1, keepdims=True)
            weights = (shifted * (1.0 / totals)).astype(BF)
            parts.append(mm(weights, v_ref[0:keys, lanes], 1, 0))
            l_ref[head, first:keys, :] = highest + jnp.log(totals)
        o_ref[first:keys, :] = jnp.concatenate(parts, 1).astype(BF)


def attend_call(query, key, value, col, row, seq):
    count, feats = query.shape
    pairs = feats // 128
    part = pl.BlockSpec((seq, 128), lambda s, h: (s, h))
    each = 128 // HD
    return pl.pallas_call(
        attend_kernel,
        grid=(2, pairs),
        out_shape=(
            jax.ShapeDtypeStruct((count, feats), BF),
            jax.ShapeDtypeStruct((2 * pairs * each, seq, 1), F32),
        ),
        in_specs=[
            part,
            part,
            part,
            pl.BlockSpec((seq, 1), lambda s, h: (s, 0)),
            pl.BlockSpec((None, 1, seq), lambda s, h: (s, 0, 0)),
        ],
        out_specs=(part, pl.BlockSpec((each, seq, 1), lambda s, h: (s * pairs + h, 0, 0))),
        compiler_params=params(2),
        cost_estimate=pl.CostEstimate(
            flops=4 * count * seq * feats, bytes_accessed=8 * count * feats, transcendentals=0
        ),
        name="attend",
    )(query, key, value, col, row)


def attend_back_kernel(
    q_ref, k_ref, v_ref, g_ref, l_ref, col_ref, row_ref, c_ref, a_ref, b_ref,
    dq_ref, dk_ref, dv_ref, key_total, value_total, query_total,
):
    length = q_ref.shape[0]
    scale = HD ** (-0.5)
    key_total[...] = jnp.zeros_like(key_total)
    value_total[...] = jnp.zeros_like(value_total)
    for first in range(0, length, BLOCK):
        keys = first + BLOCK
        allowed = allowed_keys(col_ref, row_ref, first, BLOCK, keys)
        dq_parts, dk_parts, dv_parts = [], [], []
        for head in range(q_ref.shape[1] // HD):
            lanes = slice(head * HD, (head + 1) * HD)
            query = q_ref[first:keys, lanes] * scale
            key = k_ref[0:keys, lanes]
            grad = g_ref[first:keys, lanes]
            scores = jnp.where(allowed, mm(query, key, 1, 1), MASKED)
            probs = jnp.exp(scores - l_ref[head, first:keys, :])
            grad_probs = mm(grad, v_ref[0:keys, lanes], 1, 1)
            inner = jnp.sum(probs * grad_probs, -1, keepdims=True)
            grad_scores = (probs * (grad_probs - inner)).astype(BF)
            dq_parts.append(mm(grad_scores, key, 1, 0) * scale)
            dk_parts.append(mm(grad_scores, query, 0, 0))
            dv_parts.append(mm(probs.astype(BF), grad, 0, 0))
        query_total[first:keys, :] = jnp.concatenate(dq_parts, 1)
        key_total[0:keys, :] += jnp.concatenate(dk_parts, 1)
        value_total[0:keys, :] += jnp.concatenate(dv_parts, 1)
    cosine, low_sine, high_sine = c_ref[...], a_ref[...], b_ref[...]
    dq_ref[...] = rope_back(query_total[...], cosine, low_sine, high_sine).astype(BF)
    dk_ref[...] = rope_back(key_total[...], cosine, low_sine, high_sine).astype(BF)
    dv_ref[...] = value_total[...].astype(BF)


def attend_back_call(
    query, key, value, grad, log_sums, col, row, tables, seq, freight=(), rider=(), number=None
):
    count, feats = query.shape
    pairs = feats // 128
    part = pl.BlockSpec((seq, 128), lambda s, h: (s, h))
    table = pl.BlockSpec((seq, 128), lambda s, h: (0, 0))
    each = 128 // HD
    out = jax.ShapeDtypeStruct((count, feats), BF)
    outputs = len(Cargo.rows_of(freight))

    def kernel(*refs):
        ins, refs = refs[:10], refs[10:]
        parts, refs = refs[: len(freight)], refs[len(freight) :]
        riders, refs = refs[: len(rider)], refs[len(rider) :]
        outs, refs = refs[:3], refs[3:]
        sums, refs = refs[:outputs], refs[outputs:]
        landed, refs = refs[: len(rider)], refs[len(rider) :]
        mine, spare = refs[:3], refs[3:]
        step = pl.program_id(0) * pairs + pl.program_id(1)
        if rider:
            held, got, sems = spare[-3:]
            spare = spare[:-3]
            plane, core, ctx = [lax.axis_index(name) for name in ALL]
            across = (plane, core, lax.rem(ctx + 2, 4))
            fetch = pltpu.make_async_copy(riders[0], held, sems.at[0])
            ride = pltpu.make_async_remote_copy(
                src_ref=held,
                dst_ref=got,
                send_sem=sems.at[1],
                recv_sem=sems.at[2],
                device_id=across,
                device_id_type=MESH_ID,
            )
        cargo = Cargo(freight, parts + sums + spare) if freight else None
        if freight:

            @pl.when(step == 0)
            def _():
                cargo.begin()
                if rider:
                    fetch.start()
                greet_all(cargo.peers() + ([across] if rider else []))
                if rider:
                    fetch.wait()
                    ride.start()
                cargo.start()

            @pl.when(step == 2 * pairs - 1)
            def _():
                for s in range(outputs):
                    cargo.middle(s)

        attend_back_kernel(*ins, *outs, *mine)
        if freight:

            @pl.when(step == 2 * pairs - 1)
            def _():
                cargo.end()
                if rider:
                    ride.wait()
                    landed[0][...] = got[...]

    more = dict(collective_id=number, has_side_effects=True) if freight else {}
    return pl.pallas_call(
        kernel,
        grid=(2, pairs),
        out_shape=[out, out, out]
        + Cargo.out_shapes(freight)
        + [jax.ShapeDtypeStruct(array.shape, BF) for array in rider],
        in_specs=[
            part,
            part,
            part,
            part,
            pl.BlockSpec((each, seq, 1), lambda s, h: (s * pairs + h, 0, 0)),
            pl.BlockSpec((seq, 1), lambda s, h: (s, 0)),
            pl.BlockSpec((None, 1, seq), lambda s, h: (s, 0, 0)),
            table,
            table,
            table,
        ]
        + [pl.BlockSpec(memory_space=pl.ANY)] * (len(freight) + len(rider)),
        out_specs=[part, part, part]
        + [pl.BlockSpec((rows, D), lambda s, h: (0, 0)) for rows in Cargo.rows_of(freight)]
        + [pl.BlockSpec(array.shape, lambda s, h: (0, 0)) for array in rider],
        scratch_shapes=[pltpu.VMEM((seq, 128), F32)] * 3
        + Cargo.scratch(freight)
        + ([pltpu.VMEM(rider[0].shape, BF)] * 2 + [pltpu.SemaphoreType.DMA((3,))] if rider else []),
        compiler_params=params(2, **more),
        cost_estimate=pl.CostEstimate(
            flops=10 * count * seq * feats, bytes_accessed=14 * count * feats, transcendentals=0
        ),
        name="attend_back",
    )(query, key, value, grad, log_sums, col, row, *tables, *freight, *rider)


def project_kernel(o_ref, w_ref, x_ref, gain_ref, m_ref, n_ref):
    total = x_ref[...].astype(F32)
    for index in range(o_ref.shape[0]):
        total = total + mm(o_ref[index], w_ref[index], 1, 0)
    m_ref[...] = total
    n_ref[...] = (total * norm_scale(total) * gain_ref[...]).astype(BF)


def project_call(attended, weights, x_all, gain):
    team, count, feats = attended.shape
    rows = pl.BlockSpec((BLOCK, D), lambda i: (i, 0))
    return pl.pallas_call(
        project_kernel,
        grid=(count // BLOCK,),
        out_shape=(
            jax.ShapeDtypeStruct((count, D), F32),
            jax.ShapeDtypeStruct((count, D), BF),
        ),
        in_specs=[
            pl.BlockSpec((team, BLOCK, feats), lambda i: (0, i, 0)),
            pl.BlockSpec((team, feats, D), lambda i: (0, 0, 0), pipeline_mode=pl.Buffered(1)),
            rows,
            pl.BlockSpec((1, D), lambda i: (0, 0)),
        ],
        out_specs=(rows, rows),
        compiler_params=params(),
        cost_estimate=pl.CostEstimate(
            flops=2 * count * D * D, bytes_accessed=10 * count * D, transcendentals=0
        ),
        name="project",
    )(attended, weights, x_all, gain)


def shifted(value, axis, size, step):
    return lax.ppermute(value, axis, [(i, (i + step) % size) for i in range(size)])


def plane_reduce(parts, planes):
    home = lax.axis_index("plane")
    rows = parts[0].shape[1]

    def block(index, first, size):
        return jnp.stack(
            [
                lax.dynamic_slice(part, (index, first, 0), (1, size, D))[0].astype(BF)
                for part in parts
            ],
            0,
        )

    if planes != 4:
        total = block(home, 0, rows).astype(F32)
        for k in range(1, planes):
            part = block(lax.rem(home + k, planes), 0, rows)
            total = total + shifted(part, "plane", planes, k).astype(F32)
        return total
    near_x, near_y = home + 1 - 2 * lax.rem(home, 2), lax.rem(home + 2, 4)
    far = 3 - home
    along = ([(0, 1), (1, 0), (2, 3), (3, 2)], [(0, 2), (2, 0), (1, 3), (3, 1)])
    size = rows // 2
    sums = []
    for half in range(2):
        one, two = (near_x, near_y) if half == 0 else (near_y, near_x)
        first = half * size
        sent = jnp.stack([block(one, first, size), block(far, first, size)], 0)
        got = lax.ppermute(sent, "plane", along[half]).astype(F32)
        kept = block(home, first, size).astype(F32) + got[0]
        passed = (block(two, first, size).astype(F32) + got[1]).astype(BF)
        sums.append(kept + lax.ppermute(passed, "plane", along[1 - half]).astype(F32))
    return jnp.concatenate(sums, 1)


def core_join(parts, ctxs):
    core = lax.axis_index("core")
    parts = parts.reshape((2, ctxs) + parts.shape[1:])
    got = shifted(lax.dynamic_index_in_dim(parts, 1 - core, 0, False), "core", 2, 1)
    kept = lax.dynamic_index_in_dim(parts, core, 0, False)
    joined = (kept.astype(F32) + got.astype(F32)).astype(BF)
    return jnp.moveaxis(joined, 1, 0)


def line_reduce(parts, ctxs):
    ctx = lax.axis_index("ctx")
    total = lax.dynamic_index_in_dim(parts, ctx, 0, False)
    for k in range(1, ctxs):
        part = lax.dynamic_index_in_dim(parts, lax.rem(ctx + k, ctxs), 0, False)
        total = total + shifted(part.astype(BF), "ctx", ctxs, k).astype(F32)
    return total


def after(value, *others):
    return lax.optimization_barrier((value,) + others)[0]


def team_join(parts, ctxs):
    core, ctx = lax.axis_index("core"), lax.axis_index("ctx")
    own = parts.shape[0] // (2 * ctxs)
    parts = parts.reshape(2 * ctxs, own, D)

    def block(which, k):
        return lax.dynamic_index_in_dim(parts, which * ctxs + (ctx + k) % ctxs, 0, False)

    joined = []
    for k in list(range(1, ctxs)) + [0]:
        got = shifted(block(1 - core, k), "core", 2, 1)
        both = block(core, k).astype(F32) + got.astype(F32)
        joined.append(both.astype(BF) if k > 0 else both)
    return joined


def team_finish(joined, ctxs):
    total = joined[-1].astype(F32)
    for k in range(1, ctxs):
        total = total + shifted(joined[k - 1], "ctx", ctxs, k).astype(F32)
    return total


def local(
    planes,
    ctxs,
    tokens,
    cotangent,
    segments,
    attn_weight,
    attn_first,
    attn_second,
    mlp_weight,
    mlp_first,
    mlp_second,
    gain_weight,
    gain_first,
    gain_second,
):
    team = 2 * ctxs
    devices = planes * team
    own = tokens.shape[0]
    seq = ctxs * own
    count = 2 * seq
    arows = attn_weight.shape[0]
    frows = mlp_weight.shape[0]
    gcols = gain_weight.shape[1]
    feats = planes * arows
    hidden_count = planes * frows
    whole_heads = arows % HD == 0
    me = lax.axis_index(TEAM)

    lines_seg = own // 128
    square = planes == 4 and ctxs == 4 and whole_heads and gcols == 64
    packed = jnp.zeros((8, 128), F32)
    own_gain = lax.reduce_precision(gain_weight, 8, 7)
    if square:
        side = lax.rem(lax.axis_index("ctx"), 2)
        packed = lax.dynamic_update_slice(packed, own_gain, (0, side * gcols))
    else:
        packed = packed.at[0:2, 0:gcols].set(own_gain)
    packed = packed.at[2 : 2 + lines_seg].set(segments.astype(F32).reshape(lines_seg, 128))
    attn_low = attn_weight.astype(BF)
    qkv_low = jnp.moveaxis(attn_low[:, :3], 1, 0)
    proj_low = attn_low[:, 3]
    gate_low, up_low, down_low = [mlp_weight[:, i].astype(BF) for i in range(3)]
    tables = rope_tables(seq)
    if square:
        mlp_slots = jnp.moveaxis(mlp_weight, 1, 0)
        x_all, normed, query, key, value, qkv, gate_w, small = front_call(
            ctxs, tokens, qkv_low, mlp_slots, packed, tables
        )
        normed = normed.reshape(count, D)
        query, key, value = [part.reshape(count, feats) for part in (query, key, value)]
        qkv = qkv.reshape(3 * feats, D)
        gate_w = gate_w.reshape(hidden_count, D)
        gains = small.reshape(planes, ctxs, 2, 8, 128)[:, :, :, 0:2].sum(2)
        gains = gains.transpose(2, 0, 1, 3).reshape(2, D)
        team_small = lax.dynamic_index_in_dim(small, lax.axis_index("plane"), 0, False)
        seg = team_small[:, 2 : 2 + lines_seg].reshape(count)
        seg_col, seg_row = seg.reshape(count, 1), seg.reshape(2, 1, seq)
        att_all, proj, up_w, log_sums = second_call(
            ctxs, query, key, value, seg_col, seg_row, proj_low, mlp_slots
        )
        proj = proj.reshape(team, feats, D)
        up_w = up_w.reshape(hidden_count, D)
        middle_own, att_own, normed_two, out_part, dgate, dup, down_part = third_call(
            ctxs, att_all, proj, x_all, gains[1:2], gate_w, up_w, down_low, cotangent
        )
        normed_two, out_part = normed_two.reshape(count, D), out_part.reshape(count, D)
        dgate, dup = dgate.reshape(count, hidden_count), dup.reshape(count, hidden_count)
        down_part = down_part.reshape(1, planes, frows, D)
    else:
        inputs = [tokens, packed, gate_low, up_low]
        lines = [(0, 0, 2), (1, 1, 1)]
        shapes = [((team, own, D), BF), ((team, 8, 128), F32)]
        boards = []
        if whole_heads:
            inputs += [proj_low, qkv_low]
            lines.append((4, 2, 1))
            shapes.append(((team, arows, D), BF))
            boards.append(("slots", lambda ins, outs: ins[5], len(shapes)))
            shapes.append(((3, planes, arows, D), BF))
        boards.append(("block", lambda ins, outs: ins[2], len(shapes)))
        shapes.append(((planes, frows, D), BF))
        boards.append(("block", lambda ins, outs: ins[3], len(shapes)))
        shapes.append(((planes, frows, D), BF))
        boards.append(("late", lambda ins, outs: outs[1], len(shapes)))
        shapes.append(((planes, team, 8, 128), F32))
        gathered = gather_call(planes, ctxs, 0, inputs, lines, boards, shapes, "gather_first")
        x_all = gathered[0].reshape(count, D)
        small = gathered[-1]
        gate_w = gathered[-3].reshape(hidden_count, D)
        up_w = gathered[-2].reshape(hidden_count, D)
        gains = small[:, :, 0:2, 0:gcols].transpose(2, 0, 1, 3).reshape(2, D)
        seg = gathered[1][:, 2 : 2 + lines_seg].reshape(count)
        seg_col, seg_row = seg.reshape(count, 1), seg.reshape(2, 1, seq)
        if whole_heads:
            qkv = gathered[3].reshape(3 * feats, D)
        else:
            qkv = lax.all_gather(qkv_low, ALL, axis=1, tiled=True)
            qkv = lax.dynamic_slice_in_dim(qkv, me * feats, feats, 1).reshape(3 * feats, D)
            proj = lax.all_gather(proj_low, ALL, axis=0, tiled=True).reshape(team, feats, D)

        normed, query, key, value = qkv_call(x_all, gains[0:1], qkv, tables)
        attended, log_sums = attend_call(query, key, value, seg_col, seg_row, seq)

        inputs = [attended, down_low]
        lines = [(0, 0, 2)]
        shapes = [((team, count, feats), BF)]
        boards = []
        if whole_heads:
            inputs.append(gathered[2])
            boards.append(("half", lambda ins, outs: ins[2], len(shapes)))
            shapes.append(((team, planes, arows, D), BF))
        boards.append(("block", lambda ins, outs: ins[1], len(shapes)))
        shapes.append(((planes, frows, D), BF))
        gathered = gather_call(planes, ctxs, 2, inputs, lines, boards, shapes, "gather_second")
        att_all = gathered[0]
        down_w = gathered[-1].reshape(hidden_count, D)
        if whole_heads:
            proj = gathered[1].reshape(team, feats, D)
        dy_all = lax.all_gather(after(cotangent, att_all), TEAM, axis=0, tiled=True)
        middle, normed_two = project_call(att_all, proj, x_all, gains[1:2])
        mlp_w = (gate_w, up_w, down_w)

        gate = mm(normed_two, mlp_w[0], 1, 1)
        up = mm(normed_two, mlp_w[1], 1, 1)
        hidden = (jax.nn.silu(gate) * up).astype(BF)
        out_part = mm(hidden, mlp_w[2], 1, 0).astype(BF)
        grad_hidden = mm(after(dy_all, out_part), mlp_w[2], 1, 1)
        sig = jax.nn.sigmoid(gate)
        dgate = (grad_hidden * up * sig * (1.0 + gate * (1.0 - sig))).astype(BF)
        dup = (grad_hidden * gate * sig).astype(BF)
        down_part = mm(hidden, dy_all, 0, 0).astype(BF).reshape(1, planes, frows, D)
        middle_own = lax.dynamic_slice_in_dim(middle, me * own, own, 0)
        att_own = lax.dynamic_slice_in_dim(att_all, me * own, own, 1)
    if square:
        dn2, *down_sum, gate_part, up_part = team_sum(
            ctxs,
            3,
            [(dgate, gate_w), (dup, up_w)],
            "sum_two",
            (down_part,),
            normed_two,
            True,
        )
    else:
        (dn2,) = team_sum(ctxs, 3, [(dgate, gate_w), (dup, up_w)], "sum_two")
        gate_part = mm(dgate, normed_two, 0, 0).astype(BF).reshape(1, planes, frows, D)
        up_part = mm(dup, normed_two, 0, 0).astype(BF).reshape(1, planes, frows, D)

    middle_part, gain_two_grad = norm_back(dn2, middle_own, norm_scale(middle_own), gains[1])
    grad_middle = cotangent.astype(F32) + middle_part
    grad_branch = grad_middle.astype(BF)
    freight, rider = (), ()
    if square:
        grad_att, proj_part, *rest = middle_call(
            ctxs, grad_branch, att_own, proj, out_part.reshape(team, own, D), gate_part
        )
        joined, first_out, gate_sum = rest[:ctxs], rest[ctxs], rest[ctxs + 1]
        rider = (joined[1],)
        freight = (proj_part.reshape(1, planes, ctxs * arows, D),)
    else:
        grad_att = jnp.einsum("td,sfd->stf", grad_branch, proj, preferred_element_type=F32)
        grad_att = lax.all_to_all(
            grad_att.astype(BF), TEAM, split_axis=0, concat_axis=0, tiled=True
        )
        output = (middle_own + team_finish(team_join(out_part, ctxs), ctxs)).astype(BF)
        proj_part = jnp.einsum("tsf,sd->tfd", att_own, grad_branch, preferred_element_type=F32)
        proj_part = proj_part.astype(BF)
        if whole_heads:
            proj_part = core_join(proj_part.reshape(team, planes, arows, D), ctxs)
            proj_part = proj_part.reshape(1, planes, ctxs * arows, D)
        else:
            proj_grad = lax.psum_scatter(
                proj_part.reshape(D, D), ALL, scatter_dimension=0, tiled=True
            ).astype(F32)

    dq, dk, dv, *proj_sum = attend_back_call(
        query,
        key,
        value,
        grad_att.reshape(count, feats),
        log_sums,
        seg_col,
        seg_row,
        tables,
        seq,
        freight,
        rider,
        5,
    )
    pairs = [(dq, qkv[0:feats]), (dk, qkv[feats : 2 * feats]), (dv, qkv[2 * feats :])]
    if square:
        freight = (up_part, jax.ShapeDtypeStruct((3, planes, arows, D), BF))
        dn1, up_sum, *attn_sums = team_sum(ctxs, 4, pairs, "sum_one", freight, normed)
        proj_sum, second_out = proj_sum
        mlp_grad = jnp.stack([gate_sum, up_sum, down_sum[0]], 1)
    else:
        (dn1,) = team_sum(ctxs, 4, pairs, "sum_one")
        dqkv = jnp.concatenate([dq, dk, dv], 1)
        qkv_part = mm(dqkv, normed, 0, 0).astype(BF)
        mlp_grad = [plane_reduce([p[0]], planes)[0] for p in (gate_part, up_part, down_part)]
        mlp_grad = jnp.stack(mlp_grad, 1)
        if whole_heads:
            attn_part = qkv_part.reshape(3, planes, arows, D)
            attn_grad = plane_reduce([attn_part[i] for i in range(3)], planes)
            proj_grad = plane_reduce([proj_part[0]], planes)[0].reshape(ctxs, arows, D)
            proj_grad = line_reduce(proj_grad, ctxs)
        else:
            padded = lax.dynamic_update_slice_in_dim(
                jnp.zeros((3, D, D), BF), qkv_part.reshape(3, feats, D), me * feats, 1
            )
            attn_grad = lax.psum_scatter(padded, ALL, scatter_dimension=1, tiled=True)
            attn_grad = attn_grad.astype(F32)
            proj_grad = lax.psum_scatter(
                proj_part.reshape(D, D), ALL, scatter_dimension=0, tiled=True
            ).astype(F32)
        attn_grad = jnp.moveaxis(jnp.concatenate([attn_grad, proj_grad[None]], 0), 0, 1)

    source = tokens.astype(F32)
    source_part, gain_one_grad = norm_back(dn1, source, norm_scale(source), gains[0])
    grad_input = grad_middle + source_part
    gain_part = jnp.stack([gain_one_grad, gain_two_grad], 0).reshape(2, planes, team, gcols)
    gain_part = gain_part.transpose(1, 2, 0, 3)
    gain_part = jnp.pad(gain_part, ((0, 0), (0, 0), (0, 6), (0, 128 - gcols)))
    gain_grad = small_sum(planes, ctxs, gain_part)
    if square:
        gain_grad, last_out, proj_sum = lax.optimization_barrier((gain_grad, joined[2], proj_sum))
        output = middle_own + joined[3].astype(F32) + first_out.astype(F32)
        output = output + second_out.astype(F32) + shifted(last_out, "ctx", 4, 3).astype(F32)
        output = output.astype(BF)
        proj_sum = line_reduce(proj_sum.reshape(ctxs, arows, D), ctxs)
        attn_grad = jnp.stack(attn_sums + [proj_sum], 1)
    gain_grad = gain_grad[0:2, 0:gcols]

    attn_rate = (
        RATE_FACTOR
        * D ** (-0.5)
        * jnp.array([1.0, 1.0, 1.0, OUTPUT_BOOST], jnp.float32).reshape(1, 4, 1)
    )
    mlp_rate = RATE_FACTOR * jnp.array(
        [D ** (-0.5), D ** (-0.5), FF ** (-0.5)], jnp.float32
    ).reshape(1, 3, 1)
    attn_new = adam_update(attn_weight, attn_first, attn_second, attn_grad, attn_rate, WEIGHT_DECAY)
    mlp_new = adam_update(mlp_weight, mlp_first, mlp_second, mlp_grad, mlp_rate, WEIGHT_DECAY)
    gain_new = adam_update(gain_weight, gain_first, gain_second, gain_grad, GAIN_RATE, 0.0)
    return (
        output,
        grad_input,
        attn_new[0],
        attn_new[1][:, :3, :],
        attn_new[1][:, 3, :],
        attn_new[2],
        mlp_new[0],
        mlp_new[1],
        mlp_new[2],
        gain_new[0],
        gain_new[1],
        gain_new[2],
    )


def solution(mesh):
    dp, ctxs = mesh.shape["dp"], mesh.shape["ctx"]
    planes = dp // 2
    inner = Mesh(mesh.devices.reshape(planes, 2, ctxs), ALL)
    rows = P(ALL, None)
    cube = P(ALL, None, None)
    gain = P(None, ALL)

    def step(*args):
        return local(planes, ctxs, *args)

    return jax.shard_map(
        step,
        mesh=inner,
        in_specs=(rows, rows, P(ALL)) + (cube,) * 6 + (gain,) * 3,
        out_specs=(rows, rows, cube, cube, rows) + (cube,) * 4 + (gain,) * 3,
        check_vma=False,
    )
```

time: 4080 us -> 678 us (0.17)
  waiting for transfers between devices: 3140 us -> 26 us
  Pallas kernels: 0 us -> 574 us
  matrix products: 387 us -> 0 us
  other arithmetic: 259 us -> 38.1 us
  local copies, waits for them, and re-layouts: 193 us -> 24.9 us
  blocking collectives: 73.1 us -> 0 us
    reduce_scatter x3 -> x0, waiting for transfers between devices: 1720 us -> none  [the longest x1 1590 us: reduce_rows(): lax.psum_scatter(term(column_slices(columns)), ('dp', 'ctx'), scatter_dim...]
    unnamed x11 -> x0, waiting for transfers between devices: 722 us -> none
    all_gather x4 -> x0, waiting for transfers between devices: 698 us -> none  [the longest x1 457 us: local(): piece = lax.all_gather(mlp_low, ('dp', 'ctx'), axis=0, tiled=True)]
    pallas_call x0 -> x8, Pallas kernels: none -> 574 us  [the longest x2 166 us: team_sum(): pl.pallas_call(kernel, out_shape=[jax.ShapeDtypeStruct((own, D), F32)] +...]
    dot_general x68 -> x0, matrix products: 387 us -> none  [the longest x1 51.7 us: mlp_term(): jnp.einsum('tkc,td->ckd', jnp.stack([dgate_part, dup_part], 1), normed_tw...]
    concatenate x2 -> x0, other arithmetic: 179 us -> none  [the longest x1 134 us: mlp_term(): return jnp.concatenate([inputs_part, down_part[:, None, :]], 1)]
    concatenate x1 -> x0, local copies, waits for them, and re-layouts: 78.8 us -> none  [attn_term(): return jnp.concatenate([inputs_part, output_part[:, None, :]], 1)]
    all_gather x2 -> x0, blocking collectives: 73.1 us -> none  [the longest x1 62 us: local(): lax.all_gather(gain_weight.astype(jnp.bfloat16), ('dp', 'ctx'), axis=1, t...]
  transfers between devices with their start and end apart: 9 -> 4, of which waited for: 8 -> 1; matrix products, arithmetic and copies ran while one was open for 13% -> 5% of each run, Pallas kernels for 0% -> 0%
where the time goes in v1:
time: 678 us; the launch traced here: 670 us
  Pallas kernels  574 us (85%)
  other arithmetic  38.1 us (6%)
  waiting for transfers between devices  26 us (4%)
  local copies, waits for them, and re-layouts  24.9 us (4%)
    pallas_call x2, Pallas kernels, team_sum(): pl.pallas_call(kernel, out_shape=[jax.ShapeDtypeStruct((own, D), F32)] +...  166 us
    pallas_call x1, Pallas kernels, second_call(): pl.pallas_call(kernel, out_shape=[jax.ShapeDtypeStruct(shape, BF) for sha...  106 us
    pallas_call x1, Pallas kernels, third_call(): pl.pallas_call(kernel, out_shape=[jax.ShapeDtypeStruct((own, D), F32)] +...  90.5 us
    pallas_call x1, Pallas kernels, front_call(): pl.pallas_call(kernel, out_shape=[jax.ShapeDtypeStruct(shape, BF) for sha...  79.6 us
    pallas_call x1, Pallas kernels, middle_call(): pl.pallas_call(kernel, out_shape=[jax.ShapeDtypeStruct((team, own, feats)...  60.1 us
    pallas_call x1, Pallas kernels, attend_back_call(): pl.pallas_call(kernel, grid=(2, pairs), out_shape=[out, out, out] + Cargo...  57.8 us
    ppermute x4, waiting for transfers between devices, shifted(): lax.ppermute(value, axis, [(i, (i + step) % size) for i in range(size)])  26 us
    sub x3, other arithmetic, adam_update(): return (first_new, second_new, master - rate * (direction + decay * master))  23.1 us
  transfers between devices with their start and end apart: 4, of which 1 were waited for; matrix products, arithmetic and copies ran while one was open for 5% of the time, Pallas kernels for 0%

profile of v1, /device:TPU:24, one launch (start us, length us, event | category | flops | bytes accessed | tf_op | source)
XLA Modules:
  0.0 670.2 jit_solution(10675658728822357580)
XLA Ops:
  0.7 2.7 copy.62
  5.1 2.7 fusion.12.refs_6_
  9.2 79.6 %front.1 = (bf16[8,256,2048]{2,1,0:T(8,128)(2,1)}, bf16[8,256,2048]{2,1,0:T(8,128)(2,1)}, bf16[8,256,256]{2,1,0:T(8,128)(2,1)}, bf16[8,256,256]{2,1,0:T(8,128)(2...) custom-call(bf16[256,2048]{1,0:T(8,128)(2,1)} %refs_0_.1, ...), custom_call_target="tpu_custom_call" | custom-call | flops 6442450944 | bytes 20971520 | tf_op jit(solution)/shard_map/front/pallas_call | solution.py:825
  92.5 105.7 %second.1 = (bf16[8,2048,256]{2,1,0:T(8,128)(2,1)}, bf16[8,4,64,2048]{3,2,1,0:T(8,128)(2,1)}, bf16[4,256,2048]{2,1,0:T(8,128)(2,1)}, f32[8,1024,1]{2,1,0:T(8,128)}) custom-call(bf16[2048,256]{1,0:T(8,128)(2,1)} %bitcast.68, bf16[2048,256]{1,0:T(8,128)(2,1)} %bitcast.70, bf16[2048,256]{1,0:T(8,128)(2,1)} %bitcast.72, f32[2048,1]{1,0:T(8,128)} %copy.46.refs_3_.refs_5_, ...), custom_call_target="tpu_custom_call" | custom-call | flops 2147483648 | bytes 12582912 | tf_op jit(solution)/shard_map/second/pallas_call | solution.py:972
  198.2 90.5 %third.1 = (f32[256,2048]{1,0:T(8,128)}, bf16[8,256,256]{2,1,0:T(8,128)(2,1)}, bf16[8,256,2048]{2,1,0:T(8,128)(2,1)}, bf16[8,256,2048]{2,1,0:T(8,128)(2,1)}, bf1...) custom-call(bf16[8,2048,256]{2,1,0:T(8,128)(2,1)} %get-tuple-element.71.refs_0_, ...), custom_call_target="tpu_custom_call" | custom-call | flops 60129542144 | bytes 15728640 | tf_op jit(solution)/shard_map/third/pallas_call | solution.py:1165
  288.7 1.8 multiply_reduce_fusion.2
  290.5 86.1 %sum_two.1 = (f32[256,2048]{1,0:T(8,128)}, f32[256,2048]{1,0:T(8,128)}, bf16[1,4,256,2048]{3,2,1,0:T(8,128)(2,1)}, bf16[1,4,256,2048]{3,2,1,0:T(8,128)(2,1)}) custom-call(bf16[2048,1024]{1,0:T(8,128)(2,1)} %bitcast.101, bf16[2048,1024]{1,0:T(8,128)(2,1)} %bitcast.102, bf16[1024,2048]{1,0:T(8,128)(2,1)} %bitcast.100, bf16[1024,2048]{1,0:T(8,128)(2,1)} %bitcast.95, ...), custom_call_target="tpu_custom_call" | custom-call | flops 17179869184 | bytes 18874368 | tf_op jit(solution)/shard_map/sum_two/pallas_call | solution.py:1580
  376.7 2.3 multiply_reduce_fusion.1
  379.2 1.7 fusion.20.refs_0_
  381.4 1.8 fusion.25
  383.2 60.1 %middle.1 = (bf16[8,256,256]{2,1,0:T(8,128)(2,1)}, bf16[4,4,64,2048]{3,2,1,0:T(8,128)(2,1)}, bf16[256,2048]{1,0:T(8,128)(2,1)}, bf16[256,2048]{1,0:T(8,128)(2,1)...) custom-call(bf16[256,2048]{1,0:T(8,128)(2,1)} %fusion.20.refs_0_, ...), custom_call_target="tpu_custom_call" | custom-call | flops 4294967296 | bytes 31457280 | tf_op jit(solution)/shard_map/middle/pallas_call | solution.py:1712
  443.3 57.8 %attend_back.1 = (bf16[2048,256]{1,0:T(8,128)(2,1)}, bf16[2048,256]{1,0:T(8,128)(2,1)}, bf16[2048,256]{1,0:T(8,128)(2,1)}, f32[256,2048]{1,0:T(8,128)}, bf16[256,2048]{1,0:T(8,128)(2,1)}) custom-call(bf16[2048,256]{1,0:T(8,128)(2,1)} %bitcast.69, bf16[2048,256]{1,0:T(8,128)(2,1)} %bitcast.71, bf16[2048,256]{1,0:T(8,128)(2,1)} %bitcast.73, ...), custom_call_target="tpu_custom_call" | custom-call | flops 5368709120 | bytes 7340032 | tf_op jit(solution)/shard_map/attend_back/pallas_call | solution.py:1939
  501.1 79.7 %sum_one.1 = (f32[256,2048]{1,0:T(8,128)}, f32[256,2048]{1,0:T(8,128)}, f32[64,2048]{1,0:T(8,128)}, f32[64,2048]{1,0:T(8,128)}, f32[64,2048]{1,0:T(8,128)}) custom-call(bf16[2048,256]{1,0:T(8,128)(2,1)} %get-tuple-element.92.refs_0_, bf16[2048,256]{1,0:T(8,128)(2,1)} %get-tuple-element.93.refs_1_, bf16[2048,256]{1,0:T(8,128)(2,1)} %get-tuple-element.94.refs_2_, ...), custom_call_target="tpu_custom_call" | custom-call | flops 6442450944 | bytes 8388608 | tf_op jit(solution)/shard_map/sum_one/pallas_call | solution.py:1580
  580.8 2.2 fusion.10
  583.8 14.2 %small_sum.1 = f32[8,128]{1,0:T(8,128)} custom-call(f32[4,8,8,128]{3,2,1,0:T(8,128)} %pad.6.value_ref), custom_call_target="tpu_custom_call" | custom-call | tf_op jit(solution)/shard_map/small_sum/pallas_call | solution.py:459
  598.1 2.3 fusion.16
  600.4 2.6 collective-permute-start.1
  604.1 2.5 collective-permute-start
  606.6 14.6 %multiply_subtract_fusion = (f32[256,3,2048]{2,0,1:T(8,128)}, f32[256,3,2048]{2,0,1:T(8,128)}, f32[256,3,2048]{2,0,1:T(8,128)}) fusion(f32[256,3,2048]{2,0,1:T(8,128)} %param.25, f32[3]{0:T(128)S(1)} %copy-done.23, f32[256,1,2048]{2,0,1:T(8,128)} %bitcast.65, f32[256,1,2048]{2,0,1:T(8,128)} %bitcast.67, f32[256,1,2048]{2,0,1:T(8,128)} %bitcast.66, ...), kind=kLoop, calls=%fused_computation.3 | loop fusion | flops 26738688 | bytes 44040204 | tf_op jit(solution)/shard_map/sub | solution.py:102
  622.6 26.0 %collective-permute-done.2 = bf16[64,2048]{1,0:T(8,128)(2,1)} collective-permute-done((bf16[64,2048]{1,0:T(8,128)(2,1)}, bf16[64,2048]{1,0:T(8,128)(2,1)}, u32[]{:S(2)}, u32[]{:S(2)}) %collective-permute-start.2) | collective-permute-done | bytes 262176 | tf_op jit(solution)/shard_map/ppermute | solution.py:2006
  650.1 7.1 %multiply_subtract_fusion.1 = (f32[64,4,2048]{2,0,1:T(8,128)S(1)}, f32[64,4,2048]{2,0,1:T(8,128)S(1)}, f32[64,4,2048]{2,0,1:T(8,128)S(1)}) fusion(f32[64,4,2048]{2,1,0:T(4,128)} %param.22, f32[4]{0:T(128)S(1)} %copy-done.22, f32[64,1,2048]{2,0,1:T(8,128)S(1)} %fusion.15, f32[64,1,2048]{2,0,1:T(8,128)S(1)} %bitcast.81, f32[64,1,2048]{2,0,1:T(8,128)S(1)} %bitcast.80, ...), kind=kLoop, calls=%fused_computation.25 | loop fusion | flops 9437184 | bytes 14680080 | tf_op jit(solution)/shard_map/sub | solution.py:102
  657.2 2.7 copy.52
  659.8 2.7 copy.53
  665.5 4.5 fusion.9
  (76 shorter events, 15.4 us)
Async XLA Ops:
  0.6 4.4 copy-start.17
  3.4 4.4 copy-start.3
  4.3 4.2 copy-start.21
  89.6 2.9 copy-start.16
  290.5 86.2 %copy-start = (f32[256,2048]{1,0:T(8,128)S(1)}, f32[256,2048]{1,0:T(8,128)}, u32[]{:S(2)}) copy-start(f32[256,2048]{1,0:T(8,128)} %get-tuple-element.76) | copy-start | bytes 6291460
  290.5 86.2 %copy-start.15 = (f32[1,4,4,128]{3,0,2,1:T(1,128)S(1)}, f32[1,4,4,128]{3,0,2,1:T(1,128)}, u32[]{:S(2)}) copy-start(f32[1,4,4,128]{3,0,2,1:T(1,128)} %get-tuple-element.168) | copy-start | bytes 24580
  376.7 2.5 copy-start.6
  501.1 79.7 %copy-start.4 = (bf16[256,2048]{1,0:T(8,128)(2,1)S(1)}, bf16[256,2048]{1,0:T(8,128)(2,1)}, u32[]{:S(2)}) copy-start(bf16[256,2048]{1,0:T(8,128)(2,1)} %refs_0_.1) | copy-start | bytes 3145732
  580.8 25.8 %copy-start.23 = (f32[3]{0:T(128)S(1)}, f32[3]{0:T(128)}, u32[]{:S(2)}) copy-start(f32[3]{0:T(128)} %constant.141) | copy-start | bytes 40
  600.4 22.3 %collective-permute-start.1 = (bf16[64,2048]{1,0:T(8,128)(2,1)}, bf16[64,2048]{1,0:T(8,128)(2,1)}, u32[]{:S(2)}, u32[]{:S(2)}) collective-permute-start(bf16[64,2048]{1,0:T(8,128)(2,1)} %get-tuple-element.162), channel_id=1, source_target_pairs={{0,1},{1,2},{2,3},{3,0},{4,5},{5,6},{6,7},{7,4},{8,9},{9,10},{10,1... | collective-permute-start | bytes 786440 | tf_op jit(solution)/shard_map/ppermute | solution.py:2006
  602.9 45.7 %collective-permute-start.2 = (bf16[64,2048]{1,0:T(8,128)(2,1)}, bf16[64,2048]{1,0:T(8,128)(2,1)}, u32[]{:S(2)}, u32[]{:S(2)}) collective-permute-start(bf16[64,2048]{1,0:T(8,128)(2,1)} %get-tuple-element.164), channel_id=1, source_target_pairs={{0,2},{1,3},{2,0},{3,1},{4,6},{5,7},{6,4},{7,5},{8,10},{9,11},{10,... | collective-permute-start | bytes 786440 | tf_op jit(solution)/shard_map/ppermute | solution.py:2006
  602.9 45.7 %collective-permute-start.3 = (bf16[64,2048]{1,0:T(8,128)(2,1)S(1)}, bf16[64,2048]{1,0:T(8,128)(2,1)}, u32[]{:S(2)}, u32[]{:S(2)}) collective-permute-start(bf16[64,2048]{1,0:T(8,128)(2,1)S(1)} %get-tuple-element.163), channel_id=1, source_target_pairs={{0,3},{1,0},{2,1},{3,2},{4,7},{5,4},{6,5},{7,6},{8,11},{9,8},{10,9... | collective-permute-start | bytes 786440 | tf_op jit(solution)/shard_map/ppermute | solution.py:2006
  604.1 60.5 %collective-permute-start = (bf16[256,2048]{1,0:T(8,128)(2,1)}, bf16[256,2048]{1,0:T(8,128)(2,1)}, u32[]{:S(2)}, u32[]{:S(2)}) collective-permute-start(bf16[256,2048]{1,0:T(8,128)(2,1)} %get-tuple-element.101), channel_id=1, source_target_pairs={{0,3},{1,0},{2,1},{3,2},{4,7},{5,4},{6,5},{7,6},{8,11},{9,8},{10,9... | collective-permute-start | bytes 3145736 | tf_op jit(solution)/shard_map/ppermute | solution.py:2006
  606.6 14.6 %copy-start.19 = (f32[2,64]{1,0:T(2,128)S(1)}, f32[2,64]{1,0:T(2,128)}, u32[]{:S(2)}) copy-start(f32[2,64]{1,0:T(2,128)} %param.30) | copy-start | bytes 1540
  606.6 14.6 %copy-start.20 = (f32[2,64]{1,0:T(2,128)S(1)}, f32[2,64]{1,0:T(2,128)}, u32[]{:S(2)}) copy-start(f32[2,64]{1,0:T(2,128)} %param.29) | copy-start | bytes 1540
  606.6 43.4 %copy-start.22 = (f32[4]{0:T(128)S(1)}, f32[4]{0:T(128)}, u32[]{:S(2)}) copy-start(f32[4]{0:T(128)} %constant.140) | copy-start | bytes 52
  621.2 28.8 %copy-start.12 = (f32[64,2048]{1,0:T(8,128)S(1)}, f32[64,2048]{1,0:T(8,128)}, u32[]{:S(2)}) copy-start(f32[64,2048]{1,0:T(8,128)} %get-tuple-element.102) | copy-start | bytes 1572868
  621.2 28.8 %copy-start.13 = (f32[64,2048]{1,0:T(8,128)S(1)}, f32[64,2048]{1,0:T(8,128)}, u32[]{:S(2)}) copy-start(f32[64,2048]{1,0:T(8,128)} %get-tuple-element.103) | copy-start | bytes 1572868
  621.2 28.8 %copy-start.14 = (f32[64,2048]{1,0:T(8,128)S(1)}, f32[64,2048]{1,0:T(8,128)}, u32[]{:S(2)}) copy-start(f32[64,2048]{1,0:T(8,128)} %get-tuple-element.104) | copy-start | bytes 1572868
  659.8 4.8 copy-start.7
  659.8 4.8 copy-start.9
  659.8 4.8 copy-start.10
  659.8 4.8 copy-start.11
  662.5 3.0 copy-start.5
  (4 other events, 7.3 us)

commit v2 on v1

--- a/solution.py
+++ b/solution.py
@@ -517,7 +517,8 @@
     def line(self, i, way, hop, block):
         buffer, rows = self.pieces[i]
         slot = buffer.at[self.core * self.ctxs + block, rows]
-        peer = (self.plane, self.core, self.ctx + (1 if way == 0 else -1))
+        away = 1 if way == 0 else self.ctxs - 1
+        peer = (self.plane, self.core, lax.rem(self.ctx + away, self.ctxs))
         return self.remote(slot, self.line_sem, (i, way, hop), peer)
 
     def side(self, i, order, core, block):
@@ -990,19 +991,19 @@
 
 
 def third_kernel(ctxs, refs):
-    att, proj, x_all, gain, gate, up, down, dy = refs[:8]
+    att, proj, x_all, gain, gate, up, mlp, dy = refs[:8]
     m_out, a_out, n_out, o_out, g_out, u_out, d_out = refs[8:15]
-    pv, gv, uv, dv, ys, hs, gs, us, ob, xb, nb, sb = refs[15:27]
-    load, block_sem, store, late = refs[27:31]
+    pv, gv, uv, dv, ys, hs, gs, us, ob, xb, nb, sb, narrowed = refs[15:28]
+    load, block_sem, store, late = refs[28:32]
     team, own = ys.shape[0], ys.shape[1]
     wide = gv.shape[0]
     pieces = [(ys, pl.ds(0, own // 2)), (ys, pl.ds(own // 2, own // 2))]
-    net = Gather(ctxs, pieces, [("block", dv)], refs[31:])
+    net = Gather(ctxs, pieces, [("block", dv)], refs[32:])
     plane, core, ctx = net.plane, net.core, net.ctx
     me = core * ctxs + ctx
     loads = [
         pltpu.make_async_copy(dy, ys.at[me], load.at[0]),
-        pltpu.make_async_copy(down, dv.at[plane], load.at[1]),
+        pltpu.make_async_copy(mlp.at[2], narrowed, load.at[1]),
         pltpu.make_async_copy(proj, pv, load.at[2]),
         pltpu.make_async_copy(gate, gv, load.at[3]),
         pltpu.make_async_copy(up, uv, load.at[4]),
@@ -1011,10 +1012,14 @@
     def fetch(i):
         slot = lax.rem(i, 2)
         rows = pl.ds(pl.multiple_of(i * own, own), own)
-        return (
-            pltpu.make_async_copy(att.at[:, rows], ob.at[slot], block_sem.at[0, slot]),
-            pltpu.make_async_copy(x_all.at[i], xb.at[slot], block_sem.at[1, slot]),
-        )
+        size = att.shape[2]
+        copies = [
+            pltpu.make_async_copy(
+                att.at[t, rows], ob.at[slot, :, pl.ds(t * size, size)], block_sem.at[t, slot]
+            )
+            for t in range(team)
+        ]
+        return copies + [pltpu.make_async_copy(x_all.at[i], xb.at[slot], block_sem.at[team, slot])]
 
     def n_store(i):
         return pltpu.make_async_copy(nb.at[lax.rem(i, 2)], n_out.at[i], store.at[0, lax.rem(i, 2)])
@@ -1030,6 +1035,13 @@
     loads[0].wait()
     net.send_own([0, 1])
     loads[1].wait()
+
+    def narrow(g, carry):
+        part = pl.ds(pl.multiple_of(g * 16, 16), 16)
+        dv[plane, part, :] = narrowed[part, :].astype(BF)
+        return carry
+
+    lax.fori_loop(0, narrowed.shape[0] // 16, narrow, 0)
     net.board_start(0)
     for copy in loads[2:]:
         copy.wait()
@@ -1050,8 +1062,7 @@
                 copy.start()
 
         total = xb[slot].astype(F32)
-        for t in range(team):
-            total = total + mm(ob[slot, t], pv[t], 1, 0)
+        total = total + mm(ob[slot], pv[...].reshape(ob.shape[2], D), 1, 0)
 
         @pl.when(i >= 2)
         def _():
@@ -1149,15 +1160,15 @@
         pltpu.make_async_copy(us.at[b], u_out.at[b], late.at[1 + team + b]).wait()
 
 
-def third_call(ctxs, att, proj, x_all, gain, gate, up, down, dy):
+def third_call(ctxs, att, proj, x_all, gain, gate, up, mlp, dy):
     team, own, wide = 2 * ctxs, dy.shape[0], gate.shape[0]
     feats = proj.shape[1]
     block, hidden = (team, own, D), (team, own, wide)
-    shapes = [(team, own, feats), block, block, hidden, hidden, (4, wide // 4, D)]
+    shapes = [(own, team * feats), block, block, hidden, hidden, (4, wide // 4, D)]
     dma = pltpu.SemaphoreType.DMA
     hbm, vmem = pl.BlockSpec(memory_space=pl.ANY), pl.BlockSpec(memory_space=pltpu.VMEM)
     held = [proj.shape, gate.shape, up.shape, (4, wide // 4, D), block, hidden, hidden, hidden]
-    held += [(2, team, own, feats), (2, own, D), (2, own, D), (2, own, D)]
+    held += [(2, own, team * feats), (2, own, D), (2, own, D), (2, own, D)]
 
     def kernel(*refs):
         third_kernel(ctxs, refs)
@@ -1169,7 +1180,8 @@
         in_specs=[hbm] * 3 + [vmem] + [hbm] * 4,
         out_specs=[vmem] + [hbm] * len(shapes),
         scratch_shapes=[pltpu.VMEM(shape, BF) for shape in held]
-        + [dma((5,)), dma((2, 2)), dma((2, 2)), dma((2 * team + 1,))]
+        + [pltpu.VMEM((wide // 4, D), F32)]
+        + [dma((5,)), dma((team + 1, 2)), dma((2, 2)), dma((2 * team + 1,))]
         + Gather.scratch(ctxs, 2, 1),
         compiler_params=pltpu.CompilerParams(
             collective_id=6, has_side_effects=True, vmem_limit_bytes=VMEM_LIMIT
@@ -1180,7 +1192,7 @@
             transcendentals=0,
         ),
         name="third",
-    )(att, proj, x_all, gain, gate, up, down, dy)
+    )(att, proj, x_all, gain, gate, up, mlp, dy)
 
 
 class Cargo:
@@ -1332,12 +1344,22 @@
     own = out_ref.shape[0]
     rows = own // CHUNKS
     other = (plane, 1 - core, ctx)
-    loads = []
-    for i in range(pairs):
-        loads.append(pltpu.make_async_copy(rhs[i], rhs_v[i], load.at[0, i]))
-        loads.append(pltpu.make_async_copy(lhs[i], lhs_v[i], load.at[1, i]))
+    loads = [pltpu.make_async_copy(rhs[i], rhs_v[i], load.at[2 * ctxs, i]) for i in range(pairs)]
     for copy in loads:
         copy.start()
+
+    def lhs_load(block, i):
+        where = pl.ds(pl.multiple_of(block * own, own), own)
+        return pltpu.make_async_copy(lhs[i].at[where], lhs_v[i].at[where], load.at[block, i])
+
+    order = []
+    for i in range((ctxs + 1) // 2):
+        order += [last - i, i] if last - i != i else [i]
+    order = [jnp.where(2 * ctx >= ctxs, last - place, place) for place in order]
+    for index in order:
+        for side_core in (1 - core, core):
+            for i in range(pairs):
+                lhs_load(side_core * ctxs + index, i).start()
     if cargo:
         cargo.begin()
     greet_all(
@@ -1375,6 +1397,8 @@
 
     def produce(block, target):
         where = pl.ds(pl.multiple_of(block * own, own), own)
+        for i in range(pairs):
+            lhs_load(block, i).wait()
 
         def tile(t, carry):
             cols = pl.ds(pl.multiple_of(t * 512, 512), 512)
@@ -1415,15 +1439,14 @@
             dst_ref=inbox.at[slot, part],
             send_sem=hops.at[0, way, slot, chunk],
             recv_sem=hops.at[1, way, slot, chunk],
-            device_id=(plane, core, ctx + 1 if way == 0 else ctx - 1),
+            device_id=(plane, core, lax.rem(ctx + (1 if way == 0 else last), ctxs)),
             device_id_type=MESH_ID,
         )
 
-    order = []
+    places = []
     for i in range((ctxs + 1) // 2):
-        order += [last - i, i] if last - i != i else [i]
-    for place in order:
-        index = jnp.where(2 * ctx >= ctxs, last - place, place)
+        places += [last - i, i] if last - i != i else [i]
+    for place, index in zip(places, order):
         produce((1 - core) * ctxs + index, staged.at[index])
         share(index).start()
         produce(core * ctxs + index, mine.at[index])
@@ -1555,7 +1578,7 @@
     outputs = 1 + len(Cargo.rows_of(freight))
     scratch = [pltpu.VMEM(a.shape, BF) for a in lhs + rhs]
     scratch += [pltpu.VMEM((ctxs, own, D), BF)] * 5
-    scratch += [dma((2, len(pairs))), dma((2, ctxs)), dma((2, 2, ctxs, CHUNKS))]
+    scratch += [dma((2 * ctxs + 1, len(pairs))), dma((2, ctxs)), dma((2, 2, ctxs, CHUNKS))]
     made = [(1, 4, a.shape[1] // 4, D) for a in lhs] if outer else []
     extra = [other] if other is not None else []
     held = [pltpu.VMEM(a.shape, BF) for a in extra]
@@ -1611,8 +1634,8 @@
         pltpu.make_async_copy(proj, pv, load.at[0]),
         pltpu.make_async_copy(out_part, ov, load.at[1]),
     ]
-    for copy in loads:
-        copy.start()
+    loads[1].start()
+    loads[0].start()
     cargo.begin()
     partners = [
         (dc, dz) for dz in range(ctxs - 1, -1, -1) for dc in range(2) if dc + dz > 0
@@ -1622,8 +1645,6 @@
         return (core if dc == 0 else 1 - core, lax.rem(ctx + dz, ctxs))
 
     greet_all([(plane,) + partner(*step) for step in partners] + cargo.peers())
-    cargo.start()
-    loads[0].wait()
 
     def remote(source, target, sems, index, peer):
         return pltpu.make_async_remote_copy(
@@ -1638,27 +1659,22 @@
     def piece(i, c, z, home):
         return remote(sent.at[c * ctxs + z], grad.at[home], swap, (i,), (c, z))
 
+    def share(kind, z):
+        source = ov.at[(1 - core) * ctxs + z] if kind == 0 else staged.at[z]
+        target = others.at[z] if kind == 0 else theirs.at[z]
+        return remote(source, target, side, (kind, z), (1 - core, ctx))
+
+    loads[1].wait()
+    for k in list(range(1, ctxs)) + [0]:
+        share(0, lax.rem(ctx + k, ctxs)).start()
+    loads[0].wait()
     for i, step in enumerate(partners):
         c, z = partner(*step)
         sent[c * ctxs + z] = mm(da[...], pv[c * ctxs + z], 1, 1).astype(BF)
         piece(i, c, z, me).start()
-    grad[me] = mm(da[...], pv[me], 1, 1).astype(BF)
-    loads[1].wait()
-
-    def share(kind, z):
-        source = ov.at[(1 - core) * ctxs + z] if kind == 0 else staged.at[z]
-        target = others.at[z] if kind == 0 else theirs.at[z]
-        return remote(source, target, side, (kind, z), (1 - core, ctx))
-
-    for z in range(ctxs):
-        share(0, z).start()
-    for z in range(ctxs):
-        staged[z] = mm(att[(1 - core) * ctxs + z], da[...], 0, 0).astype(BF)
-        share(1, z).start()
-    for z in range(ctxs):
-        mine[z] = mm(att[core * ctxs + z], da[...], 0, 0).astype(BF)
-    size = pv.shape[1]
-    for k in list(range(1, ctxs)) + [0]:
+    cargo.start()
+
+    def join(k):
         z = lax.rem(ctx + k, ctxs)
         share(0, z).wait_recv()
         target = outs[k - 1]
@@ -1670,9 +1686,24 @@
             return carry
 
         lax.fori_loop(0, target.shape[0] // 16, group, 0)
-        if k == 1:
-            pass_on = remote(outs[0], first, shift, (0,), (core, z))
-            pass_on.start()
+
+    join(1)
+    pass_on = remote(outs[0], first, shift, (0,), (core, lax.rem(ctx + 1, ctxs)))
+    pass_on.start()
+    grad[me] = mm(da[...], pv[me], 1, 1).astype(BF)
+    width = grad.shape[2]
+
+    def heads(t):
+        return att[:, pl.ds(pl.multiple_of(t * width, width), width)]
+
+    for z in range(ctxs):
+        staged[z] = mm(heads((1 - core) * ctxs + z), da[...], 0, 0).astype(BF)
+        share(1, z).start()
+    for z in range(ctxs):
+        mine[z] = mm(heads(core * ctxs + z), da[...], 0, 0).astype(BF)
+    size = pv.shape[1]
+    for k in list(range(2, ctxs)) + [0]:
+        join(k)
     cargo.middle(0)
     for z in range(ctxs):
         share(1, z).wait_recv()
@@ -2150,7 +2181,7 @@
         proj = proj.reshape(team, feats, D)
         up_w = up_w.reshape(hidden_count, D)
         middle_own, att_own, normed_two, out_part, dgate, dup, down_part = third_call(
-            ctxs, att_all, proj, x_all, gains[1:2], gate_w, up_w, down_low, cotangent
+            ctxs, att_all, proj, x_all, gains[1:2], gate_w, up_w, mlp_slots, cotangent
         )
         normed_two, out_part = normed_two.reshape(count, D), out_part.reshape(count, D)
         dgate, dup = dgate.reshape(count, hidden_count), dup.reshape(count, hidden_count)
@@ -2312,11 +2343,12 @@
     gain_part = jnp.pad(gain_part, ((0, 0), (0, 0), (0, 6), (0, 128 - gcols)))
     gain_grad = small_sum(planes, ctxs, gain_part)
     if square:
-        gain_grad, last_out, proj_sum = lax.optimization_barrier((gain_grad, joined[2], proj_sum))
+        gain_grad, proj_sum = lax.optimization_barrier((gain_grad, proj_sum))
+        proj_sum = line_reduce(proj_sum.reshape(ctxs, arows, D), ctxs)
+        proj_sum, last_out = lax.optimization_barrier((proj_sum, joined[2]))
         output = middle_own + joined[3].astype(F32) + first_out.astype(F32)
         output = output + second_out.astype(F32) + shifted(last_out, "ctx", 4, 3).astype(F32)
         output = output.astype(BF)
-        proj_sum = line_reduce(proj_sum.reshape(ctxs, arows, D), ctxs)
         attn_grad = jnp.stack(attn_sums + [proj_sum], 1)
     gain_grad = gain_grad[0:2, 0:gcols]
 

time: 678 us -> 664 us (0.979)
  waiting for transfers between devices: 26 us -> 17.2 us
    ppermute x4, waiting for transfers between devices: 26 us -> 17.2 us  [shifted(): lax.ppermute(value, axis, [(i, (i + step) % size) for i in range(size)])]
  transfers between devices with their start and end apart: 4 -> 4, of which waited for: 1 -> 2; matrix products, arithmetic and copies ran while one was open for 5% -> 5% of each run, Pallas kernels for 0% -> 0%
where the time goes in v2:
time: 664 us; the launch traced here: 654 us
  Pallas kernels  572 us (86%)
  other arithmetic  37.1 us (6%)
  local copies, waits for them, and re-layouts  21.5 us (3%)
  waiting for transfers between devices  17.2 us (3%)
    pallas_call x2, Pallas kernels, team_sum(): pl.pallas_call(kernel, out_shape=[jax.ShapeDtypeStruct((own, D), F32)] +...  165 us
    pallas_call x1, Pallas kernels, second_call(): pl.pallas_call(kernel, out_shape=[jax.ShapeDtypeStruct(shape, BF) for sha...  106 us
    pallas_call x1, Pallas kernels, third_call(): pl.pallas_call(kernel, out_shape=[jax.ShapeDtypeStruct((own, D), F32)] +...  90.6 us
    pallas_call x1, Pallas kernels, front_call(): pl.pallas_call(kernel, out_shape=[jax.ShapeDtypeStruct(shape, BF) for sha...  79.6 us
    pallas_call x1, Pallas kernels, middle_call(): pl.pallas_call(kernel, out_shape=[jax.ShapeDtypeStruct((team, own, feats)...  58.9 us
    pallas_call x1, Pallas kernels, attend_back_call(): pl.pallas_call(kernel, grid=(2, pairs), out_shape=[out, out, out] + Cargo...  57.9 us
    sub x3, other arithmetic, adam_update(): return (first_new, second_new, master - rate * (direction + decay * master))  23 us
    ppermute x4, waiting for transfers between devices, shifted(): lax.ppermute(value, axis, [(i, (i + step) % size) for i in range(size)])  17.2 us
  transfers between devices with their start and end apart: 4, of which 2 were waited for; matrix products, arithmetic and copies ran while one was open for 5% of the time, Pallas kernels for 0%

profile of v2, /device:TPU:24, one launch (start us, length us, event | category | flops | bytes accessed | tf_op | source)
XLA Modules:
  0.0 654.1 jit_solution(16824091949352572353)
XLA Ops:
  0.7 2.8 copy.62
  6.6 79.6 %front.1 = (bf16[8,256,2048]{2,1,0:T(8,128)(2,1)}, bf16[8,256,2048]{2,1,0:T(8,128)(2,1)}, bf16[8,256,256]{2,1,0:T(8,128)(2,1)}, bf16[8,256,256]{2,1,0:T(8,128)(2...) custom-call(bf16[256,2048]{1,0:T(8,128)(2,1)} %refs_0_.1, ...), custom_call_target="tpu_custom_call" | custom-call | flops 6442450944 | bytes 20971520 | tf_op jit(solution)/shard_map/front/pallas_call | solution.py:826
  89.9 105.8 %second.1 = (bf16[8,2048,256]{2,1,0:T(8,128)(2,1)}, bf16[8,4,64,2048]{3,2,1,0:T(8,128)(2,1)}, bf16[4,256,2048]{2,1,0:T(8,128)(2,1)}, f32[8,1024,1]{2,1,0:T(8,128)}) custom-call(bf16[2048,256]{1,0:T(8,128)(2,1)} %bitcast.65, bf16[2048,256]{1,0:T(8,128)(2,1)} %bitcast.67, bf16[2048,256]{1,0:T(8,128)(2,1)} %bitcast.69, f32[2048,1]{1,0:T(8,128)} %copy.46.refs_3_.refs_5_, ...), custom_call_target="tpu_custom_call" | custom-call | flops 2147483648 | bytes 12582912 | tf_op jit(solution)/shard_map/second/pallas_call | solution.py:973
  195.6 90.6 %third.1 = (f32[256,2048]{1,0:T(8,128)}, bf16[256,2048]{1,0:T(8,128)(2,1)}, bf16[8,256,2048]{2,1,0:T(8,128)(2,1)}, bf16[8,256,2048]{2,1,0:T(8,128)(2,1)}, bf16[8...) custom-call(bf16[8,2048,256]{2,1,0:T(8,128)(2,1)} %get-tuple-element.72.refs_0_, ...), custom_call_target="tpu_custom_call" | custom-call | flops 60129542144 | bytes 15728640 | tf_op jit(solution)/shard_map/third/pallas_call | solution.py:1176
  286.3 1.8 multiply_reduce_fusion.2
  288.1 85.7 %sum_two.1 = (f32[256,2048]{1,0:T(8,128)}, f32[256,2048]{1,0:T(8,128)}, bf16[1,4,256,2048]{3,2,1,0:T(8,128)(2,1)}, bf16[1,4,256,2048]{3,2,1,0:T(8,128)(2,1)}) custom-call(bf16[2048,1024]{1,0:T(8,128)(2,1)} %bitcast.98, bf16[2048,1024]{1,0:T(8,128)(2,1)} %bitcast.99, bf16[1024,2048]{1,0:T(8,128)(2,1)} %bitcast.97, bf16[1024,2048]{1,0:T(8,128)(2,1)} %bitcast.92, ...), custom_call_target="tpu_custom_call" | custom-call | flops 17179869184 | bytes 18874368 | tf_op jit(solution)/shard_map/sum_two/pallas_call | solution.py:1603
  373.9 2.3 multiply_reduce_fusion.1
  376.3 1.7 fusion.18.refs_0_
  378.6 1.8 fusion.23
  380.4 58.9 %middle.1 = (bf16[8,256,256]{2,1,0:T(8,128)(2,1)}, bf16[4,4,64,2048]{3,2,1,0:T(8,128)(2,1)}, bf16[256,2048]{1,0:T(8,128)(2,1)}, bf16[256,2048]{1,0:T(8,128)(2,1)...) custom-call(bf16[256,2048]{1,0:T(8,128)(2,1)} %fusion.18.refs_0_, ...), custom_call_target="tpu_custom_call" | custom-call | flops 4294967296 | bytes 31457280 | tf_op jit(solution)/shard_map/middle/pallas_call | solution.py:1743
  439.2 57.9 %attend_back.1 = (bf16[2048,256]{1,0:T(8,128)(2,1)}, bf16[2048,256]{1,0:T(8,128)(2,1)}, bf16[2048,256]{1,0:T(8,128)(2,1)}, f32[256,2048]{1,0:T(8,128)}, bf16[256,2048]{1,0:T(8,128)(2,1)}) custom-call(bf16[2048,256]{1,0:T(8,128)(2,1)} %bitcast.66, bf16[2048,256]{1,0:T(8,128)(2,1)} %bitcast.68, bf16[2048,256]{1,0:T(8,128)(2,1)} %bitcast.70, ...), custom_call_target="tpu_custom_call" | custom-call | flops 5368709120 | bytes 7340032 | tf_op jit(solution)/shard_map/attend_back/pallas_call | solution.py:1970
  497.1 79.6 %sum_one.1 = (f32[256,2048]{1,0:T(8,128)}, f32[256,2048]{1,0:T(8,128)}, f32[64,2048]{1,0:T(8,128)}, f32[64,2048]{1,0:T(8,128)}, f32[64,2048]{1,0:T(8,128)}) custom-call(bf16[2048,256]{1,0:T(8,128)(2,1)} %get-tuple-element.93.refs_0_, bf16[2048,256]{1,0:T(8,128)(2,1)} %get-tuple-element.94.refs_1_, bf16[2048,256]{1,0:T(8,128)(2,1)} %get-tuple-element.95.refs_2_, ...), custom_call_target="tpu_custom_call" | custom-call | flops 6442450944 | bytes 8388608 | tf_op jit(solution)/shard_map/sum_one/pallas_call | solution.py:1603
  576.8 2.2 fusion.10
  579.8 14.3 %small_sum.1 = f32[8,128]{1,0:T(8,128)} custom-call(f32[4,8,8,128]{3,2,1,0:T(8,128)} %pad.6.value_ref), custom_call_target="tpu_custom_call" | custom-call | tf_op jit(solution)/shard_map/small_sum/pallas_call | solution.py:459
  594.2 2.3 fusion.14
  596.5 2.6 collective-permute-start
  600.2 14.6 %multiply_subtract_fusion = (f32[256,3,2048]{2,0,1:T(8,128)}, f32[256,3,2048]{2,0,1:T(8,128)}, f32[256,3,2048]{2,0,1:T(8,128)}) fusion(f32[256,3,2048]{2,0,1:T(8,128)} %param.25, f32[3]{0:T(128)S(1)} %copy-done.23, f32[256,1,2048]{2,0,1:T(8,128)} %bitcast.61, f32[256,1,2048]{2,0,1:T(8,128)} %bitcast.63, f32[256,1,2048]{2,0,1:T(8,128)} %bitcast.62, ...), kind=kLoop, calls=%fused_computation.3 | loop fusion | flops 26738688 | bytes 44040204 | tf_op jit(solution)/shard_map/sub | solution.py:102
  616.2 6.0 collective-permute-done.1
  622.3 1.4 fusion.13
  624.6 7.1 %multiply_subtract_fusion.1 = (f32[64,4,2048]{2,0,1:T(8,128)S(1)}, f32[64,4,2048]{2,0,1:T(8,128)S(1)}, f32[64,4,2048]{2,0,1:T(8,128)S(1)}) fusion(f32[64,4,2048]{2,1,0:T(4,128)} %param.22, f32[4]{0:T(128)S(1)} %copy-done.22, f32[64,1,2048]{2,0,1:T(8,128)S(1)} %bitcast.64, f32[64,1,2048]{2,0,1:T(8,128)S(1)} %bitcast.78, f32[64,1,2048]{2,0,1:T(8,128)S(1)} %bitcast.77, ...), kind=kLoop, calls=%fused_computation.24 | loop fusion | flops 9437184 | bytes 14680080 | tf_op jit(solution)/shard_map/sub | solution.py:102
  631.7 2.7 copy.52
  634.3 2.7 copy.53
  639.1 11.1 %collective-permute-done.3 = bf16[256,2048]{1,0:T(8,128)(2,1)S(1)} collective-permute-done((bf16[256,2048]{1,0:T(8,128)(2,1)}, bf16[256,2048]{1,0:T(8,128)(2,1)S(1)}, u32[]{:S(2)}, u32[]{:S(2)}) %collective-permute-start.3) | collective-permute-done | bytes 1048608 | tf_op jit(solution)/shard_map/ppermute | solution.py:2037
  650.3 3.5 fusion.9
  (75 shorter events, 14.0 us)
Async XLA Ops:
  0.6 4.5 copy-start.17
  0.7 4.5 copy-start.3
  3.5 2.5 copy-start.21
  87.0 2.9 copy-start.16
  288.1 85.7 %copy-start = (f32[256,2048]{1,0:T(8,128)S(1)}, f32[256,2048]{1,0:T(8,128)}, u32[]{:S(2)}) copy-start(f32[256,2048]{1,0:T(8,128)} %get-tuple-element.77) | copy-start | bytes 6291460
  288.1 85.7 %copy-start.15 = (f32[1,4,4,128]{3,0,2,1:T(1,128)S(1)}, f32[1,4,4,128]{3,0,2,1:T(1,128)}, u32[]{:S(2)}) copy-start(f32[1,4,4,128]{3,0,2,1:T(1,128)} %get-tuple-element.170) | copy-start | bytes 24580
  497.1 79.7 %copy-start.4 = (bf16[256,2048]{1,0:T(8,128)(2,1)S(1)}, bf16[256,2048]{1,0:T(8,128)(2,1)}, u32[]{:S(2)}) copy-start(bf16[256,2048]{1,0:T(8,128)(2,1)} %refs_0_.1) | copy-start | bytes 3145732
  576.8 23.4 %copy-start.23 = (f32[3]{0:T(128)S(1)}, f32[3]{0:T(128)}, u32[]{:S(2)}) copy-start(f32[3]{0:T(128)} %constant.141) | copy-start | bytes 40
  596.5 19.8 %collective-permute-start = (bf16[64,2048]{1,0:T(8,128)(2,1)}, bf16[64,2048]{1,0:T(8,128)(2,1)}, u32[]{:S(2)}, u32[]{:S(2)}) collective-permute-start(bf16[64,2048]{1,0:T(8,128)(2,1)} %get-tuple-element.166), channel_id=1, source_target_pairs={{0,1},{1,2},{2,3},{3,0},{4,5},{5,6},{6,7},{7,4},{8,9},{9,10},{10,1... | collective-permute-start | bytes 786440 | tf_op jit(solution)/shard_map/ppermute | solution.py:2037
  599.0 23.2 %collective-permute-start.1 = (bf16[64,2048]{1,0:T(8,128)(2,1)}, bf16[64,2048]{1,0:T(8,128)(2,1)}, u32[]{:S(2)}, u32[]{:S(2)}) collective-permute-start(bf16[64,2048]{1,0:T(8,128)(2,1)} %get-tuple-element.168), channel_id=1, source_target_pairs={{0,2},{1,3},{2,0},{3,1},{4,6},{5,7},{6,4},{7,5},{8,10},{9,11},{10,... | collective-permute-start | bytes 786440 | tf_op jit(solution)/shard_map/ppermute | solution.py:2037
  599.1 23.2 %collective-permute-start.2 = (bf16[64,2048]{1,0:T(8,128)(2,1)S(1)}, bf16[64,2048]{1,0:T(8,128)(2,1)}, u32[]{:S(2)}, u32[]{:S(2)}) collective-permute-start(bf16[64,2048]{1,0:T(8,128)(2,1)S(1)} %get-tuple-element.167), channel_id=1, source_target_pairs={{0,3},{1,0},{2,1},{3,2},{4,7},{5,4},{6,5},{7,6},{8,11},{9,8},{10,9... | collective-permute-start | bytes 786440 | tf_op jit(solution)/shard_map/ppermute | solution.py:2037
  600.2 14.6 %copy-start.19 = (f32[2,64]{1,0:T(2,128)S(1)}, f32[2,64]{1,0:T(2,128)}, u32[]{:S(2)}) copy-start(f32[2,64]{1,0:T(2,128)} %param.30) | copy-start | bytes 1540
  600.2 14.6 %copy-start.20 = (f32[2,64]{1,0:T(2,128)S(1)}, f32[2,64]{1,0:T(2,128)}, u32[]{:S(2)}) copy-start(f32[2,64]{1,0:T(2,128)} %param.29) | copy-start | bytes 1540
  600.2 24.3 %copy-start.22 = (f32[4]{0:T(128)S(1)}, f32[4]{0:T(128)}, u32[]{:S(2)}) copy-start(f32[4]{0:T(128)} %constant.140) | copy-start | bytes 52
  614.8 9.7 %copy-start.12 = (f32[64,2048]{1,0:T(8,128)S(1)}, f32[64,2048]{1,0:T(8,128)}, u32[]{:S(2)}) copy-start(f32[64,2048]{1,0:T(8,128)} %get-tuple-element.104) | copy-start | bytes 1572868
  614.8 9.7 %copy-start.13 = (f32[64,2048]{1,0:T(8,128)S(1)}, f32[64,2048]{1,0:T(8,128)}, u32[]{:S(2)}) copy-start(f32[64,2048]{1,0:T(8,128)} %get-tuple-element.105) | copy-start | bytes 1572868
  614.8 9.7 %copy-start.14 = (f32[64,2048]{1,0:T(8,128)S(1)}, f32[64,2048]{1,0:T(8,128)}, u32[]{:S(2)}) copy-start(f32[64,2048]{1,0:T(8,128)} %get-tuple-element.106) | copy-start | bytes 1572868
  623.7 26.6 %collective-permute-start.3 = (bf16[256,2048]{1,0:T(8,128)(2,1)}, bf16[256,2048]{1,0:T(8,128)(2,1)S(1)}, u32[]{:S(2)}, u32[]{:S(2)}) collective-permute-start(bf16[256,2048]{1,0:T(8,128)(2,1)} %get-tuple-element.103), channel_id=1, source_target_pairs={{0,3},{1,0},{2,1},{3,2},{4,7},{5,4},{6,5},{7,6},{8,11},{9,8},{10,9... | collective-permute-start | bytes 3145736 | tf_op jit(solution)/shard_map/ppermute | solution.py:2037
  634.3 15.9 %copy-start.7 = (bf16[256,2048]{1,0:T(8,128)(2,1)S(1)}, bf16[256,2048]{1,0:T(8,128)(2,1)}, u32[]{:S(2)}) copy-start(bf16[256,2048]{1,0:T(8,128)(2,1)} %refs_7_.2) | copy-start | bytes 3145732
  634.3 15.9 %copy-start.9 = (bf16[256,2048]{1,0:T(8,128)(2,1)S(1)}, bf16[256,2048]{1,0:T(8,128)(2,1)}, u32[]{:S(2)}) copy-start(bf16[256,2048]{1,0:T(8,128)(2,1)} %get-tuple-element.86) | copy-start | bytes 3145732
  634.3 15.9 %copy-start.10 = (bf16[256,2048]{1,0:T(8,128)(2,1)S(1)}, bf16[256,2048]{1,0:T(8,128)(2,1)}, u32[]{:S(2)}) copy-start(bf16[256,2048]{1,0:T(8,128)(2,1)} %get-tuple-element.87) | copy-start | bytes 3145732
  634.3 15.9 %copy-start.11 = (bf16[256,2048]{1,0:T(8,128)(2,1)S(1)}, bf16[256,2048]{1,0:T(8,128)(2,1)}, u32[]{:S(2)}) copy-start(bf16[256,2048]{1,0:T(8,128)(2,1)} %get-tuple-element.92) | copy-start | bytes 3145732
  637.0 13.3 %copy-start.2 = (f32[256,2048]{1,0:T(8,128)S(1)}, f32[256,2048]{1,0:T(8,128)}, u32[]{:S(2)}) copy-start(f32[256,2048]{1,0:T(8,128)} %get-tuple-element.82) | copy-start | bytes 6291460
  637.0 13.3 %copy-start.5 = (f32[256,2048]{1,0:T(8,128)S(1)}, f32[256,2048]{1,0:T(8,128)}, u32[]{:S(2)}) copy-start(f32[256,2048]{1,0:T(8,128)} %get-tuple-element.99) | copy-start | bytes 6291460
  (4 other events, 7.6 us)

commit v3 on v2

--- a/solution.py
+++ b/solution.py
@@ -1112,11 +1112,6 @@
 
         sb[lax.rem(i, 2)] = mm(hs[i], dv[...].reshape(wide, D), 1, 0).astype(BF)
         s_store(i, o_out).start()
-
-        @pl.when(i == team // 2)
-        def _():
-            net.hop(ctxs - 1, [0])
-
         return carry
 
     def backward(side_core):
@@ -1132,20 +1127,22 @@
 
         return action
 
-    if ctxs == 2:
-        lax.fori_loop(0, team, outward, 0)
-    else:
-        lax.fori_loop(0, team, outward, 0)
-    s_store(team - 2, o_out).wait()
-    s_store(team - 1, o_out).wait()
     backward(core)(ctx)
     net.side_arrive(0, [0, 1])
     backward(1 - core)(ctx)
-    net.hop(ctxs - 1, [1])
-    for k in range(1, ctxs):
+    for k in range(1, ctxs - 1):
+        if k == ctxs - 2:
+            net.hop(ctxs - 1, [0])
         net.distant(k, backward(core))
         net.side_arrive(k, [0, 1])
         net.distant(k, backward(1 - core))
+    lax.fori_loop(0, team, outward, 0)
+    s_store(team - 2, o_out).wait()
+    s_store(team - 1, o_out).wait()
+    net.hop(ctxs - 1, [1])
+    net.distant(ctxs - 1, backward(core))
+    net.side_arrive(ctxs - 1, [0, 1])
+    net.distant(ctxs - 1, backward(1 - core))
     for p in range(4):
         if p >= 2:
             s_store(p - 2, d_out).wait()
@@ -2312,6 +2309,12 @@
         freight = (up_part, jax.ShapeDtypeStruct((3, planes, arows, D), BF))
         dn1, up_sum, *attn_sums = team_sum(ctxs, 4, pairs, "sum_one", freight, normed)
         proj_sum, second_out = proj_sum
+        dn1, last_out, proj_sum = lax.optimization_barrier((dn1, joined[2], proj_sum))
+        output = middle_own + joined[3].astype(F32) + first_out.astype(F32)
+        output = output + second_out.astype(F32) + shifted(last_out, "ctx", 4, 3).astype(F32)
+        output = output.astype(BF)
+        proj_sum = line_reduce(proj_sum.reshape(ctxs, arows, D), ctxs)
+        attn_grad = jnp.stack(attn_sums + [proj_sum], 1)
         mlp_grad = jnp.stack([gate_sum, up_sum, down_sum[0]], 1)
     else:
         (dn1,) = team_sum(ctxs, 4, pairs, "sum_one")
@@ -2341,17 +2344,6 @@
     gain_part = jnp.stack([gain_one_grad, gain_two_grad], 0).reshape(2, planes, team, gcols)
     gain_part = gain_part.transpose(1, 2, 0, 3)
     gain_part = jnp.pad(gain_part, ((0, 0), (0, 0), (0, 6), (0, 128 - gcols)))
-    gain_grad = small_sum(planes, ctxs, gain_part)
-    if square:
-        gain_grad, proj_sum = lax.optimization_barrier((gain_grad, proj_sum))
-        proj_sum = line_reduce(proj_sum.reshape(ctxs, arows, D), ctxs)
-        proj_sum, last_out = lax.optimization_barrier((proj_sum, joined[2]))
-        output = middle_own + joined[3].astype(F32) + first_out.astype(F32)
-        output = output + second_out.astype(F32) + shifted(last_out, "ctx", 4, 3).astype(F32)
-        output = output.astype(BF)
-        attn_grad = jnp.stack(attn_sums + [proj_sum], 1)
-    gain_grad = gain_grad[0:2, 0:gcols]
-
     attn_rate = (
         RATE_FACTOR
         * D ** (-0.5)
@@ -2362,6 +2354,10 @@
     ).reshape(1, 3, 1)
     attn_new = adam_update(attn_weight, attn_first, attn_second, attn_grad, attn_rate, WEIGHT_DECAY)
     mlp_new = adam_update(mlp_weight, mlp_first, mlp_second, mlp_grad, mlp_rate, WEIGHT_DECAY)
+    if square:
+        gain_part, output, attn_last = lax.optimization_barrier((gain_part, output, attn_new[2]))
+        attn_new = (attn_new[0], attn_new[1], attn_last)
+    gain_grad = small_sum(planes, ctxs, gain_part)[0:2, 0:gcols]
     gain_new = adam_update(gain_weight, gain_first, gain_second, gain_grad, GAIN_RATE, 0.0)
     return (
         output,

time: 664 us -> 672 us (1.012)
  transfers between devices with their start and end apart: 4 -> 4, of which waited for: 2 -> 1; matrix products, arithmetic and copies ran while one was open for 5% -> 5% of each run, Pallas kernels for 0% -> 0%
where the time goes in v3:
time: 672 us; the launch traced here: 662 us
  Pallas kernels  568 us (85%)
  other arithmetic  37.8 us (6%)
  waiting for transfers between devices  23.1 us (3%)
  local copies, waits for them, and re-layouts  22.3 us (3%)
  starting transfers between devices  9.52 us (1%)
    pallas_call x2, Pallas kernels, team_sum(): pl.pallas_call(kernel, out_shape=[jax.ShapeDtypeStruct((own, D), F32)] +...  163 us
    pallas_call x1, Pallas kernels, second_call(): pl.pallas_call(kernel, out_shape=[jax.ShapeDtypeStruct(shape, BF) for sha...  106 us
    pallas_call x1, Pallas kernels, third_call(): pl.pallas_call(kernel, out_shape=[jax.ShapeDtypeStruct((own, D), F32)] +...  93.1 us
    pallas_call x1, Pallas kernels, front_call(): pl.pallas_call(kernel, out_shape=[jax.ShapeDtypeStruct(shape, BF) for sha...  79.7 us
    pallas_call x1, Pallas kernels, attend_back_call(): pl.pallas_call(kernel, grid=(2, pairs), out_shape=[out, out, out] + Cargo...  58.5 us
    pallas_call x1, Pallas kernels, middle_call(): pl.pallas_call(kernel, out_shape=[jax.ShapeDtypeStruct((team, own, feats)...  57.4 us
    ppermute x4, waiting for transfers between devices, shifted(): lax.ppermute(value, axis, [(i, (i + step) % size) for i in range(size)])  23.1 us
    sub x3, other arithmetic, adam_update(): return (first_new, second_new, master - rate * (direction + decay * master))  22.9 us
  transfers between devices with their start and end apart: 4, of which 1 were waited for; matrix products, arithmetic and copies ran while one was open for 5% of the time, Pallas kernels for 0%

profile of v3, /device:TPU:24, one launch (start us, length us, event | category | flops | bytes accessed | tf_op | source)
XLA Modules:
  0.0 662.4 jit_solution(6228485993819672654)
XLA Ops:
  0.7 2.7 copy.62
  6.2 79.7 %front.1 = (bf16[8,256,2048]{2,1,0:T(8,128)(2,1)}, bf16[8,256,2048]{2,1,0:T(8,128)(2,1)}, bf16[8,256,256]{2,1,0:T(8,128)(2,1)}, bf16[8,256,256]{2,1,0:T(8,128)(2...) custom-call(bf16[256,2048]{1,0:T(8,128)(2,1)} %refs_0_.1, ...), custom_call_target="tpu_custom_call" | custom-call | flops 6442450944 | bytes 20971520 | tf_op jit(solution)/shard_map/front/pallas_call | solution.py:826
  89.5 105.7 %second.1 = (bf16[8,2048,256]{2,1,0:T(8,128)(2,1)}, bf16[8,4,64,2048]{3,2,1,0:T(8,128)(2,1)}, bf16[4,256,2048]{2,1,0:T(8,128)(2,1)}, f32[8,1024,1]{2,1,0:T(8,128)}) custom-call(bf16[2048,256]{1,0:T(8,128)(2,1)} %bitcast.67, bf16[2048,256]{1,0:T(8,128)(2,1)} %bitcast.69, bf16[2048,256]{1,0:T(8,128)(2,1)} %bitcast.71, f32[2048,1]{1,0:T(8,128)} %copy.46.refs_3_.refs_5_, ...), custom_call_target="tpu_custom_call" | custom-call | flops 2147483648 | bytes 12582912 | tf_op jit(solution)/shard_map/second/pallas_call | solution.py:973
  195.3 93.1 %third.1 = (f32[256,2048]{1,0:T(8,128)}, bf16[256,2048]{1,0:T(8,128)(2,1)}, bf16[8,256,2048]{2,1,0:T(8,128)(2,1)}, bf16[8,256,2048]{2,1,0:T(8,128)(2,1)}, bf16[8...) custom-call(bf16[8,2048,256]{2,1,0:T(8,128)(2,1)} %get-tuple-element.74.refs_0_, ...), custom_call_target="tpu_custom_call" | custom-call | flops 60129542144 | bytes 15728640 | tf_op jit(solution)/shard_map/third/pallas_call | solution.py:1173
  288.4 1.8 multiply_reduce_fusion.2
  290.3 83.3 %sum_two.1 = (f32[256,2048]{1,0:T(8,128)}, f32[256,2048]{1,0:T(8,128)}, bf16[1,4,256,2048]{3,2,1,0:T(8,128)(2,1)}, bf16[1,4,256,2048]{3,2,1,0:T(8,128)(2,1)}) custom-call(bf16[2048,1024]{1,0:T(8,128)(2,1)} %bitcast.100, bf16[2048,1024]{1,0:T(8,128)(2,1)} %bitcast.101, bf16[1024,2048]{1,0:T(8,128)(2,1)} %bitcast.99, bf16[1024,2048]{1,0:T(8,128)(2,1)} %bitcast.94, ...), custom_call_target="tpu_custom_call" | custom-call | flops 17179869184 | bytes 18874368 | tf_op jit(solution)/shard_map/sum_two/pallas_call | solution.py:1600
  373.6 2.3 multiply_reduce_fusion.1
  376.1 1.7 fusion.19.refs_0_
  378.3 1.8 fusion.24
  380.1 57.4 %middle.1 = (bf16[8,256,256]{2,1,0:T(8,128)(2,1)}, bf16[4,4,64,2048]{3,2,1,0:T(8,128)(2,1)}, bf16[256,2048]{1,0:T(8,128)(2,1)}, bf16[256,2048]{1,0:T(8,128)(2,1)...) custom-call(bf16[256,2048]{1,0:T(8,128)(2,1)} %fusion.19.refs_0_, ...), custom_call_target="tpu_custom_call" | custom-call | flops 4294967296 | bytes 31457280 | tf_op jit(solution)/shard_map/middle/pallas_call | solution.py:1740
  437.5 58.5 %attend_back.1 = (bf16[2048,256]{1,0:T(8,128)(2,1)}, bf16[2048,256]{1,0:T(8,128)(2,1)}, bf16[2048,256]{1,0:T(8,128)(2,1)}, f32[256,2048]{1,0:T(8,128)}, bf16[256,2048]{1,0:T(8,128)(2,1)}) custom-call(bf16[2048,256]{1,0:T(8,128)(2,1)} %bitcast.68, bf16[2048,256]{1,0:T(8,128)(2,1)} %bitcast.70, bf16[2048,256]{1,0:T(8,128)(2,1)} %bitcast.72, ...), custom_call_target="tpu_custom_call" | custom-call | flops 5368709120 | bytes 7340032 | tf_op jit(solution)/shard_map/attend_back/pallas_call | solution.py:1967
  496.1 79.7 %sum_one.1 = (f32[256,2048]{1,0:T(8,128)}, f32[256,2048]{1,0:T(8,128)}, f32[64,2048]{1,0:T(8,128)}, f32[64,2048]{1,0:T(8,128)}, f32[64,2048]{1,0:T(8,128)}) custom-call(bf16[2048,256]{1,0:T(8,128)(2,1)} %get-tuple-element.92.refs_0_, bf16[2048,256]{1,0:T(8,128)(2,1)} %get-tuple-element.93.refs_1_, bf16[2048,256]{1,0:T(8,128)(2,1)} %get-tuple-element.94.refs_2_, ...), custom_call_target="tpu_custom_call" | custom-call | flops 6442450944 | bytes 8388608 | tf_op jit(solution)/shard_map/sum_one/pallas_call | solution.py:1600
  575.8 2.3 fusion.15
  578.1 5.8 collective-permute-start.1
  584.5 3.1 collective-permute-start
  587.9 2.2 fusion.10
  590.3 14.6 %multiply_subtract_fusion = (f32[256,3,2048]{2,0,1:T(8,128)}, f32[256,3,2048]{2,0,1:T(8,128)}, f32[256,3,2048]{2,0,1:T(8,128)}) fusion(f32[256,3,2048]{2,0,1:T(8,128)} %param.25, f32[3]{0:T(128)S(1)} %copy-done.22, f32[256,1,2048]{2,0,1:T(8,128)} %bitcast.64, f32[256,1,2048]{2,0,1:T(8,128)} %bitcast.66, f32[256,1,2048]{2,0,1:T(8,128)} %bitcast.65, ...), kind=kLoop, calls=%fused_computation.3 | loop fusion | flops 26738688 | bytes 44040204 | tf_op jit(solution)/shard_map/sub | solution.py:102
  605.6 23.1 %collective-permute-done.2 = bf16[64,2048]{1,0:T(8,128)(2,1)} collective-permute-done((bf16[64,2048]{1,0:T(8,128)(2,1)}, bf16[64,2048]{1,0:T(8,128)(2,1)}, u32[]{:S(2)}, u32[]{:S(2)}) %collective-permute-start.2) | collective-permute-done | bytes 262176 | tf_op jit(solution)/shard_map/ppermute | solution.py:2034
  628.7 1.4 fusion.14
  630.1 7.1 %multiply_subtract_fusion.1 = (f32[64,4,2048]{2,0,1:T(8,128)S(1)}, f32[64,4,2048]{2,0,1:T(8,128)S(1)}, f32[64,4,2048]{2,0,1:T(8,128)S(1)}) fusion(f32[64,4,2048]{2,1,0:T(4,128)} %param.22, f32[4]{0:T(128)S(1)} %copy-done.21, f32[64,1,2048]{2,0,1:T(8,128)S(1)} %fusion.14, f32[64,1,2048]{2,0,1:T(8,128)S(1)} %bitcast.80, f32[64,1,2048]{2,0,1:T(8,128)S(1)} %bitcast.79, ...), kind=kLoop, calls=%fused_computation.24 | loop fusion | flops 9437184 | bytes 14680080 | tf_op jit(solution)/shard_map/sub | solution.py:102
  637.2 2.7 copy.52
  642.9 4.3 fusion.9
  647.2 2.7 copy.53
  649.8 11.0 %small_sum.1 = f32[8,128]{1,0:T(8,128)} custom-call(f32[4,8,8,128]{3,2,1,0:T(8,128)} %pad.6.value_ref), custom_call_target="tpu_custom_call" | custom-call | tf_op jit(solution)/shard_map/small_sum/pallas_call | solution.py:459
  (74 shorter events, 13.2 us)
Async XLA Ops:
  0.6 4.4 copy-start.16
  0.7 4.9 copy-start.20
  86.6 2.9 copy-start.15
  290.2 83.3 %copy-start = (f32[256,2048]{1,0:T(8,128)S(1)}, f32[256,2048]{1,0:T(8,128)}, u32[]{:S(2)}) copy-start(f32[256,2048]{1,0:T(8,128)} %get-tuple-element.79) | copy-start | bytes 6291460
  290.3 83.3 %copy-start.14 = (f32[1,4,4,128]{3,0,2,1:T(1,128)S(1)}, f32[1,4,4,128]{3,0,2,1:T(1,128)}, u32[]{:S(2)}) copy-start(f32[1,4,4,128]{3,0,2,1:T(1,128)} %get-tuple-element.174) | copy-start | bytes 24580
  373.6 2.3 copy-start.1
  373.6 2.5 copy-start.5
  575.7 11.9 %copy-start.3 = (bf16[256,2048]{1,0:T(8,128)(2,1)S(1)}, bf16[256,2048]{1,0:T(8,128)(2,1)}, u32[]{:S(2)}) copy-start(bf16[256,2048]{1,0:T(8,128)(2,1)} %refs_0_.1) | copy-start | bytes 3145732
  578.1 27.5 %collective-permute-start.1 = (bf16[64,2048]{1,0:T(8,128)(2,1)}, bf16[64,2048]{1,0:T(8,128)(2,1)}, u32[]{:S(2)}, u32[]{:S(2)}) collective-permute-start(bf16[64,2048]{1,0:T(8,128)(2,1)} %get-tuple-element.170), channel_id=1, source_target_pairs={{0,1},{1,2},{2,3},{3,0},{4,5},{5,6},{6,7},{7,4},{8,9},{9,10},{10,1... | collective-permute-start | bytes 786440 | tf_op jit(solution)/shard_map/ppermute | solution.py:2034
  584.0 44.7 %collective-permute-start.2 = (bf16[64,2048]{1,0:T(8,128)(2,1)}, bf16[64,2048]{1,0:T(8,128)(2,1)}, u32[]{:S(2)}, u32[]{:S(2)}) collective-permute-start(bf16[64,2048]{1,0:T(8,128)(2,1)} %get-tuple-element.172), channel_id=1, source_target_pairs={{0,2},{1,3},{2,0},{3,1},{4,6},{5,7},{6,4},{7,5},{8,10},{9,11},{10,... | collective-permute-start | bytes 786440 | tf_op jit(solution)/shard_map/ppermute | solution.py:2034
  584.0 6.3 copy-start.22
  584.0 44.7 %collective-permute-start.3 = (bf16[64,2048]{1,0:T(8,128)(2,1)S(1)}, bf16[64,2048]{1,0:T(8,128)(2,1)}, u32[]{:S(2)}, u32[]{:S(2)}) collective-permute-start(bf16[64,2048]{1,0:T(8,128)(2,1)S(1)} %get-tuple-element.171), channel_id=1, source_target_pairs={{0,3},{1,0},{2,1},{3,2},{4,7},{5,4},{6,5},{7,6},{8,11},{9,8},{10,9... | collective-permute-start | bytes 786440 | tf_op jit(solution)/shard_map/ppermute | solution.py:2034
  584.5 57.4 %collective-permute-start = (bf16[256,2048]{1,0:T(8,128)(2,1)}, bf16[256,2048]{1,0:T(8,128)(2,1)}, u32[]{:S(2)}, u32[]{:S(2)}) collective-permute-start(bf16[256,2048]{1,0:T(8,128)(2,1)} %get-tuple-element.105), channel_id=1, source_target_pairs={{0,3},{1,0},{2,1},{3,2},{4,7},{5,4},{6,5},{7,6},{8,11},{9,8},{10,9... | collective-permute-start | bytes 3145736 | tf_op jit(solution)/shard_map/ppermute | solution.py:2034
  590.3 39.8 %copy-start.21 = (f32[4]{0:T(128)S(1)}, f32[4]{0:T(128)}, u32[]{:S(2)}) copy-start(f32[4]{0:T(128)} %constant.140) | copy-start | bytes 52
  604.9 25.2 %copy-start.11 = (f32[64,2048]{1,0:T(8,128)S(1)}, f32[64,2048]{1,0:T(8,128)}, u32[]{:S(2)}) copy-start(f32[64,2048]{1,0:T(8,128)} %get-tuple-element.106) | copy-start | bytes 1572868
  604.9 25.2 %copy-start.12 = (f32[64,2048]{1,0:T(8,128)S(1)}, f32[64,2048]{1,0:T(8,128)}, u32[]{:S(2)}) copy-start(f32[64,2048]{1,0:T(8,128)} %get-tuple-element.107) | copy-start | bytes 1572868
  604.9 25.2 %copy-start.13 = (f32[64,2048]{1,0:T(8,128)S(1)}, f32[64,2048]{1,0:T(8,128)}, u32[]{:S(2)}) copy-start(f32[64,2048]{1,0:T(8,128)} %get-tuple-element.108) | copy-start | bytes 1572868
  637.2 4.8 copy-start.6
  637.2 4.8 copy-start.8
  637.2 4.8 copy-start.9
  637.2 4.8 copy-start.10
  639.9 3.0 copy-start.4
  647.2 13.7 %copy-start.18 = (f32[2,64]{1,0:T(2,128)S(1)}, f32[2,64]{1,0:T(2,128)}, u32[]{:S(2)}) copy-start(f32[2,64]{1,0:T(2,128)} %param.30) | copy-start | bytes 1540
  647.2 13.7 %copy-start.19 = (f32[2,64]{1,0:T(2,128)S(1)}, f32[2,64]{1,0:T(2,128)}, u32[]{:S(2)}) copy-start(f32[2,64]{1,0:T(2,128)} %param.29) | copy-start | bytes 1540
  (3 other events, 5.0 us)

commit v4 on v2

--- a/solution.py
+++ b/solution.py
@@ -843,9 +843,11 @@
     )(tokens, qkv, mlp, packed, *tables)
 
 
-def attend_part(q_ref, k_ref, v_ref, col_ref, row_ref, l_ref, put, start, length, pair, unit):
+def attend_part(
+    q_ref, k_ref, v_ref, col_ref, row_ref, l_ref, put, start, begin, end, pair, unit
+):
     lanes = pl.ds(pl.multiple_of(pair * 128, 128), 128)
-    for first in range(0, length, BLOCK):
+    for first in range(begin, end, BLOCK):
         keys = first + BLOCK
         rows = pl.ds(pl.multiple_of(start + first, BLOCK), BLOCK)
         past = pl.ds(pl.multiple_of(start, BLOCK), keys)
@@ -876,7 +878,9 @@
     seq = count // 2
     pairs = feats // 128
     plane = lax.axis_index("plane")
-    pieces = [(outs, pl.ds(0, seq)), (outs, pl.ds(seq, seq)), (ps, plane)]
+    half = seq // 2
+    pieces = [(outs, pl.ds(i * half, half)) for i in range(4)] + [(ps, plane)]
+    parts, rows_piece = [0, 1, 2, 3], [4]
     net = Gather(ctxs, pieces, [("block", ds_), ("half", ps)], refs[17:])
     core, ctx = net.core, net.ctx
     me = core * ctxs + ctx
@@ -888,7 +892,7 @@
         copy.start()
     greet_all(net.peers())
     loads[0].wait()
-    net.send_own([2])
+    net.send_own(rows_piece)
     loads[1].wait()
 
     def narrow(g, carry):
@@ -903,23 +907,22 @@
         outs[me, rows, lanes] = values
 
     hops = list(range(1, ctxs))
-    for s in range(2):
+    for part in parts:
+        s, begin = part // 2, (part % 2) * half
         for pair in range(pairs):
             attend_part(
                 q_ref, k_ref, v_ref, col_ref, row_ref.at[s], l_ref, put,
-                s * seq, seq, pair, (s * pairs + pair) * (128 // HD),
+                s * seq, begin, begin + half, pair, (s * pairs + pair) * (128 // HD),
             )
-            if s * pairs + pair == 2 * pairs - 1:
-                net.send_own([1])
-            if hops:
-                net.hop(hops.pop(0), [2])
-                if not hops:
-                    net.board_start(1)
-            if s * pairs + pair == pairs - 1:
-                net.send_own([0])
-                net.board_pass(0)
+        net.send_own([part])
+        if hops:
+            net.hop(hops.pop(0), rows_piece)
+            if not hops:
+                net.board_start(1)
+        if part == 1:
+            net.board_pass(0)
     for k in hops:
-        net.hop(k, [2])
+        net.hop(k, rows_piece)
     if hops:
         net.board_start(1)
 
@@ -928,12 +931,12 @@
 
     copy_out(me).start()
     for k in range(1, ctxs):
-        net.hop(k, [0])
+        net.hop(k, parts[:2])
         if k == 2 or ctxs == 2:
             net.board_pass(1)
-        net.hop(k, [1])
+        net.hop(k, parts[2:])
         net.distant(k, lambda block: copy_out(core * ctxs + block).start())
-        net.side_arrive(k - 1, [0, 1])
+        net.side_arrive(k - 1, parts)
         if k == 1:
             copy_out((1 - core) * ctxs + ctx).start()
             net.board_finish(0)
@@ -945,11 +948,11 @@
     ]
     tail[0].start()
     for k in range(ctxs):
-        net.side_arrive(k, [2])
+        net.side_arrive(k, rows_piece)
     net.board_finish(1)
     net.board_shared(1)
     tail[1].start()
-    net.side_arrive(ctxs - 1, [0, 1])
+    net.side_arrive(ctxs - 1, parts)
     net.distant(ctxs - 1, lambda block: copy_out((1 - core) * ctxs + block).start())
     net.close()
     for copy in tail:
@@ -979,7 +982,7 @@
         scratch_shapes=[pltpu.VMEM(shape, BF) for shape in shapes]
         + [pltpu.VMEM((frows, D), F32)]
         + [dma((2,)), dma((team + 2,))]
-        + Gather.scratch(ctxs, 3, 2),
+        + Gather.scratch(ctxs, 5, 2),
         compiler_params=pltpu.CompilerParams(
             collective_id=2, has_side_effects=True, vmem_limit_bytes=VMEM_LIMIT
         ),
@@ -1105,18 +1108,19 @@
     n_store(team - 1).wait()
     net.board_finish(0)
 
+    def pair_store(i, out):
+        return pltpu.make_async_copy(sb, out.at[pl.ds(2 * i, 2)], store.at[1, 0])
+
     def outward(i, carry):
-        @pl.when(i >= 2)
+        both = hs[pl.ds(2 * i, 2)].reshape(2 * own, wide)
+        result = mm(both, dv[...].reshape(wide, D), 1, 0).astype(BF)
+
+        @pl.when(i >= 1)
         def _():
-            s_store(i - 2, o_out).wait()
-
-        sb[lax.rem(i, 2)] = mm(hs[i], dv[...].reshape(wide, D), 1, 0).astype(BF)
-        s_store(i, o_out).start()
-
-        @pl.when(i == team // 2)
-        def _():
-            net.hop(ctxs - 1, [0])
-
+            pair_store(i - 1, o_out).wait()
+
+        sb[...] = result.reshape(2, own, D)
+        pair_store(i, o_out).start()
         return carry
 
     def backward(side_core):
@@ -1132,20 +1136,21 @@
 
         return action
 
-    if ctxs == 2:
-        lax.fori_loop(0, team, outward, 0)
-    else:
-        lax.fori_loop(0, team, outward, 0)
-    s_store(team - 2, o_out).wait()
-    s_store(team - 1, o_out).wait()
     backward(core)(ctx)
     net.side_arrive(0, [0, 1])
     backward(1 - core)(ctx)
-    net.hop(ctxs - 1, [1])
-    for k in range(1, ctxs):
+    for k in range(1, ctxs - 1):
+        if k == ctxs - 2:
+            net.hop(ctxs - 1, [0])
         net.distant(k, backward(core))
         net.side_arrive(k, [0, 1])
         net.distant(k, backward(1 - core))
+    lax.fori_loop(0, team // 2, outward, 0)
+    pair_store(team // 2 - 1, o_out).wait()
+    net.hop(ctxs - 1, [1])
+    net.distant(ctxs - 1, backward(core))
+    net.side_arrive(ctxs - 1, [0, 1])
+    net.distant(ctxs - 1, backward(1 - core))
     for p in range(4):
         if p >= 2:
             s_store(p - 2, d_out).wait()

time: 664 us -> 663 us (level)
  no operation moved by 1% of the time
where the time goes in v4:
time: 663 us; the launch traced here: 654 us
  Pallas kernels  572 us (86%)
  other arithmetic  37.1 us (6%)
  local copies, waits for them, and re-layouts  21.5 us (3%)
  waiting for transfers between devices  17.2 us (3%)
    pallas_call x2, Pallas kernels, team_sum(): pl.pallas_call(kernel, out_shape=[jax.ShapeDtypeStruct((own, D), F32)] +...  163 us
    pallas_call x1, Pallas kernels, second_call(): pl.pallas_call(kernel, out_shape=[jax.ShapeDtypeStruct(shape, BF) for sha...  105 us
    pallas_call x1, Pallas kernels, third_call(): pl.pallas_call(kernel, out_shape=[jax.ShapeDtypeStruct((own, D), F32)] +...  94.9 us
    pallas_call x1, Pallas kernels, front_call(): pl.pallas_call(kernel, out_shape=[jax.ShapeDtypeStruct(shape, BF) for sha...  79.6 us
    pallas_call x1, Pallas kernels, attend_back_call(): pl.pallas_call(kernel, grid=(2, pairs), out_shape=[out, out, out] + Cargo...  58.5 us
    pallas_call x1, Pallas kernels, middle_call(): pl.pallas_call(kernel, out_shape=[jax.ShapeDtypeStruct((team, own, feats)...  56.6 us
    sub x3, other arithmetic, adam_update(): return (first_new, second_new, master - rate * (direction + decay * master))  23 us
    ppermute x4, waiting for transfers between devices, shifted(): lax.ppermute(value, axis, [(i, (i + step) % size) for i in range(size)])  17.2 us
  transfers between devices with their start and end apart: 4, of which 2 were waited for; matrix products, arithmetic and copies ran while one was open for 5% of the time, Pallas kernels for 0%

profile of v4, /device:TPU:24, one launch (start us, length us, event | category | flops | bytes accessed | tf_op | source)
XLA Modules:
  0.0 654.0 jit_solution(16511545898354381011)
XLA Ops:
  0.7 2.8 copy.62
  6.6 79.6 %front.1 = (bf16[8,256,2048]{2,1,0:T(8,128)(2,1)}, bf16[8,256,2048]{2,1,0:T(8,128)(2,1)}, bf16[8,256,256]{2,1,0:T(8,128)(2,1)}, bf16[8,256,256]{2,1,0:T(8,128)(2...) custom-call(bf16[256,2048]{1,0:T(8,128)(2,1)} %refs_0_.1, ...), custom_call_target="tpu_custom_call" | custom-call | flops 6442450944 | bytes 20971520 | tf_op jit(solution)/shard_map/front/pallas_call | solution.py:826
  89.9 104.8 %second.1 = (bf16[8,2048,256]{2,1,0:T(8,128)(2,1)}, bf16[8,4,64,2048]{3,2,1,0:T(8,128)(2,1)}, bf16[4,256,2048]{2,1,0:T(8,128)(2,1)}, f32[8,1024,1]{2,1,0:T(8,128)}) custom-call(bf16[2048,256]{1,0:T(8,128)(2,1)} %bitcast.65, bf16[2048,256]{1,0:T(8,128)(2,1)} %bitcast.67, bf16[2048,256]{1,0:T(8,128)(2,1)} %bitcast.69, f32[2048,1]{1,0:T(8,128)} %copy.46.refs_3_.refs_5_, ...), custom_call_target="tpu_custom_call" | custom-call | flops 2147483648 | bytes 12582912 | tf_op jit(solution)/shard_map/second/pallas_call | solution.py:976
  194.6 94.9 %third.1 = (f32[256,2048]{1,0:T(8,128)}, bf16[256,2048]{1,0:T(8,128)(2,1)}, bf16[8,256,2048]{2,1,0:T(8,128)(2,1)}, bf16[8,256,2048]{2,1,0:T(8,128)(2,1)}, bf16[8...) custom-call(bf16[8,2048,256]{2,1,0:T(8,128)(2,1)} %get-tuple-element.72.refs_0_, ...), custom_call_target="tpu_custom_call" | custom-call | flops 60129542144 | bytes 15728640 | tf_op jit(solution)/shard_map/third/pallas_call | solution.py:1181
  289.6 1.8 multiply_reduce_fusion.2
  291.4 83.3 %sum_two.1 = (f32[256,2048]{1,0:T(8,128)}, f32[256,2048]{1,0:T(8,128)}, bf16[1,4,256,2048]{3,2,1,0:T(8,128)(2,1)}, bf16[1,4,256,2048]{3,2,1,0:T(8,128)(2,1)}) custom-call(bf16[2048,1024]{1,0:T(8,128)(2,1)} %bitcast.98, bf16[2048,1024]{1,0:T(8,128)(2,1)} %bitcast.99, bf16[1024,2048]{1,0:T(8,128)(2,1)} %bitcast.97, bf16[1024,2048]{1,0:T(8,128)(2,1)} %bitcast.92, ...), custom_call_target="tpu_custom_call" | custom-call | flops 17179869184 | bytes 18874368 | tf_op jit(solution)/shard_map/sum_two/pallas_call | solution.py:1608
  374.7 2.3 multiply_reduce_fusion.1
  377.2 1.7 fusion.18.refs_0_
  379.5 1.8 fusion.23
  381.2 56.6 %middle.1 = (bf16[8,256,256]{2,1,0:T(8,128)(2,1)}, bf16[4,4,64,2048]{3,2,1,0:T(8,128)(2,1)}, bf16[256,2048]{1,0:T(8,128)(2,1)}, bf16[256,2048]{1,0:T(8,128)(2,1)...) custom-call(bf16[256,2048]{1,0:T(8,128)(2,1)} %fusion.18.refs_0_, ...), custom_call_target="tpu_custom_call" | custom-call | flops 4294967296 | bytes 31457280 | tf_op jit(solution)/shard_map/middle/pallas_call | solution.py:1748
  437.8 58.5 %attend_back.1 = (bf16[2048,256]{1,0:T(8,128)(2,1)}, bf16[2048,256]{1,0:T(8,128)(2,1)}, bf16[2048,256]{1,0:T(8,128)(2,1)}, f32[256,2048]{1,0:T(8,128)}, bf16[256,2048]{1,0:T(8,128)(2,1)}) custom-call(bf16[2048,256]{1,0:T(8,128)(2,1)} %bitcast.66, bf16[2048,256]{1,0:T(8,128)(2,1)} %bitcast.68, bf16[2048,256]{1,0:T(8,128)(2,1)} %bitcast.70, ...), custom_call_target="tpu_custom_call" | custom-call | flops 5368709120 | bytes 7340032 | tf_op jit(solution)/shard_map/attend_back/pallas_call | solution.py:1975
  496.3 79.8 %sum_one.1 = (f32[256,2048]{1,0:T(8,128)}, f32[256,2048]{1,0:T(8,128)}, f32[64,2048]{1,0:T(8,128)}, f32[64,2048]{1,0:T(8,128)}, f32[64,2048]{1,0:T(8,128)}) custom-call(bf16[2048,256]{1,0:T(8,128)(2,1)} %get-tuple-element.93.refs_0_, bf16[2048,256]{1,0:T(8,128)(2,1)} %get-tuple-element.94.refs_1_, bf16[2048,256]{1,0:T(8,128)(2,1)} %get-tuple-element.95.refs_2_, ...), custom_call_target="tpu_custom_call" | custom-call | flops 6442450944 | bytes 8388608 | tf_op jit(solution)/shard_map/sum_one/pallas_call | solution.py:1608
  576.2 2.2 fusion.10
  579.2 14.5 %small_sum.1 = f32[8,128]{1,0:T(8,128)} custom-call(f32[4,8,8,128]{3,2,1,0:T(8,128)} %pad.6.value_ref), custom_call_target="tpu_custom_call" | custom-call | tf_op jit(solution)/shard_map/small_sum/pallas_call | solution.py:459
  593.8 2.3 fusion.14
  596.0 3.0 collective-permute-start
  600.2 14.6 %multiply_subtract_fusion = (f32[256,3,2048]{2,0,1:T(8,128)}, f32[256,3,2048]{2,0,1:T(8,128)}, f32[256,3,2048]{2,0,1:T(8,128)}) fusion(f32[256,3,2048]{2,0,1:T(8,128)} %param.25, f32[3]{0:T(128)S(1)} %copy-done.23, f32[256,1,2048]{2,0,1:T(8,128)} %bitcast.61, f32[256,1,2048]{2,0,1:T(8,128)} %bitcast.63, f32[256,1,2048]{2,0,1:T(8,128)} %bitcast.62, ...), kind=kLoop, calls=%fused_computation.3 | loop fusion | flops 26738688 | bytes 44040204 | tf_op jit(solution)/shard_map/sub | solution.py:102
  616.2 6.0 collective-permute-done.1
  622.2 1.4 fusion.13
  624.5 7.1 %multiply_subtract_fusion.1 = (f32[64,4,2048]{2,0,1:T(8,128)S(1)}, f32[64,4,2048]{2,0,1:T(8,128)S(1)}, f32[64,4,2048]{2,0,1:T(8,128)S(1)}) fusion(f32[64,4,2048]{2,1,0:T(4,128)} %param.22, f32[4]{0:T(128)S(1)} %copy-done.22, f32[64,1,2048]{2,0,1:T(8,128)S(1)} %bitcast.64, f32[64,1,2048]{2,0,1:T(8,128)S(1)} %bitcast.78, f32[64,1,2048]{2,0,1:T(8,128)S(1)} %bitcast.77, ...), kind=kLoop, calls=%fused_computation.24 | loop fusion | flops 9437184 | bytes 14680080 | tf_op jit(solution)/shard_map/sub | solution.py:102
  631.6 2.7 copy.52
  634.3 2.7 copy.53
  639.1 11.1 %collective-permute-done.3 = bf16[256,2048]{1,0:T(8,128)(2,1)S(1)} collective-permute-done((bf16[256,2048]{1,0:T(8,128)(2,1)}, bf16[256,2048]{1,0:T(8,128)(2,1)S(1)}, u32[]{:S(2)}, u32[]{:S(2)}) %collective-permute-start.3) | collective-permute-done | bytes 1048608 | tf_op jit(solution)/shard_map/ppermute | solution.py:2042
  650.2 3.5 fusion.9
  (75 shorter events, 14.0 us)
Async XLA Ops:
  0.6 4.5 copy-start.17
  0.7 4.5 copy-start.3
  3.5 2.5 copy-start.21
  87.0 2.9 copy-start.16
  291.4 83.3 %copy-start = (f32[256,2048]{1,0:T(8,128)S(1)}, f32[256,2048]{1,0:T(8,128)}, u32[]{:S(2)}) copy-start(f32[256,2048]{1,0:T(8,128)} %get-tuple-element.77) | copy-start | bytes 6291460
  291.4 83.3 %copy-start.15 = (f32[1,4,4,128]{3,0,2,1:T(1,128)S(1)}, f32[1,4,4,128]{3,0,2,1:T(1,128)}, u32[]{:S(2)}) copy-start(f32[1,4,4,128]{3,0,2,1:T(1,128)} %get-tuple-element.170) | copy-start | bytes 24580
  496.3 79.8 %copy-start.4 = (bf16[256,2048]{1,0:T(8,128)(2,1)S(1)}, bf16[256,2048]{1,0:T(8,128)(2,1)}, u32[]{:S(2)}) copy-start(bf16[256,2048]{1,0:T(8,128)(2,1)} %refs_0_.1) | copy-start | bytes 3145732
  576.2 24.0 %copy-start.23 = (f32[3]{0:T(128)S(1)}, f32[3]{0:T(128)}, u32[]{:S(2)}) copy-start(f32[3]{0:T(128)} %constant.141) | copy-start | bytes 40
  596.0 20.2 %collective-permute-start = (bf16[64,2048]{1,0:T(8,128)(2,1)}, bf16[64,2048]{1,0:T(8,128)(2,1)}, u32[]{:S(2)}, u32[]{:S(2)}) collective-permute-start(bf16[64,2048]{1,0:T(8,128)(2,1)} %get-tuple-element.166), channel_id=1, source_target_pairs={{0,1},{1,2},{2,3},{3,0},{4,5},{5,6},{6,7},{7,4},{8,9},{9,10},{10,1... | collective-permute-start | bytes 786440 | tf_op jit(solution)/shard_map/ppermute | solution.py:2042
  599.0 23.2 %collective-permute-start.1 = (bf16[64,2048]{1,0:T(8,128)(2,1)}, bf16[64,2048]{1,0:T(8,128)(2,1)}, u32[]{:S(2)}, u32[]{:S(2)}) collective-permute-start(bf16[64,2048]{1,0:T(8,128)(2,1)} %get-tuple-element.168), channel_id=1, source_target_pairs={{0,2},{1,3},{2,0},{3,1},{4,6},{5,7},{6,4},{7,5},{8,10},{9,11},{10,... | collective-permute-start | bytes 786440 | tf_op jit(solution)/shard_map/ppermute | solution.py:2042
  599.0 23.2 %collective-permute-start.2 = (bf16[64,2048]{1,0:T(8,128)(2,1)S(1)}, bf16[64,2048]{1,0:T(8,128)(2,1)}, u32[]{:S(2)}, u32[]{:S(2)}) collective-permute-start(bf16[64,2048]{1,0:T(8,128)(2,1)S(1)} %get-tuple-element.167), channel_id=1, source_target_pairs={{0,3},{1,0},{2,1},{3,2},{4,7},{5,4},{6,5},{7,6},{8,11},{9,8},{10,9... | collective-permute-start | bytes 786440 | tf_op jit(solution)/shard_map/ppermute | solution.py:2042
  600.2 14.6 %copy-start.19 = (f32[2,64]{1,0:T(2,128)S(1)}, f32[2,64]{1,0:T(2,128)}, u32[]{:S(2)}) copy-start(f32[2,64]{1,0:T(2,128)} %param.30) | copy-start | bytes 1540
  600.2 14.6 %copy-start.20 = (f32[2,64]{1,0:T(2,128)S(1)}, f32[2,64]{1,0:T(2,128)}, u32[]{:S(2)}) copy-start(f32[2,64]{1,0:T(2,128)} %param.29) | copy-start | bytes 1540
  600.2 24.3 %copy-start.22 = (f32[4]{0:T(128)S(1)}, f32[4]{0:T(128)}, u32[]{:S(2)}) copy-start(f32[4]{0:T(128)} %constant.140) | copy-start | bytes 52
  614.8 9.7 %copy-start.12 = (f32[64,2048]{1,0:T(8,128)S(1)}, f32[64,2048]{1,0:T(8,128)}, u32[]{:S(2)}) copy-start(f32[64,2048]{1,0:T(8,128)} %get-tuple-element.104) | copy-start | bytes 1572868
  614.8 9.7 %copy-start.13 = (f32[64,2048]{1,0:T(8,128)S(1)}, f32[64,2048]{1,0:T(8,128)}, u32[]{:S(2)}) copy-start(f32[64,2048]{1,0:T(8,128)} %get-tuple-element.105) | copy-start | bytes 1572868
  614.8 9.7 %copy-start.14 = (f32[64,2048]{1,0:T(8,128)S(1)}, f32[64,2048]{1,0:T(8,128)}, u32[]{:S(2)}) copy-start(f32[64,2048]{1,0:T(8,128)} %get-tuple-element.106) | copy-start | bytes 1572868
  623.6 26.6 %collective-permute-start.3 = (bf16[256,2048]{1,0:T(8,128)(2,1)}, bf16[256,2048]{1,0:T(8,128)(2,1)S(1)}, u32[]{:S(2)}, u32[]{:S(2)}) collective-permute-start(bf16[256,2048]{1,0:T(8,128)(2,1)} %get-tuple-element.103), channel_id=1, source_target_pairs={{0,3},{1,0},{2,1},{3,2},{4,7},{5,4},{6,5},{7,6},{8,11},{9,8},{10,9... | collective-permute-start | bytes 3145736 | tf_op jit(solution)/shard_map/ppermute | solution.py:2042
  634.3 15.9 %copy-start.7 = (bf16[256,2048]{1,0:T(8,128)(2,1)S(1)}, bf16[256,2048]{1,0:T(8,128)(2,1)}, u32[]{:S(2)}) copy-start(bf16[256,2048]{1,0:T(8,128)(2,1)} %refs_7_.2) | copy-start | bytes 3145732
  634.3 15.9 %copy-start.9 = (bf16[256,2048]{1,0:T(8,128)(2,1)S(1)}, bf16[256,2048]{1,0:T(8,128)(2,1)}, u32[]{:S(2)}) copy-start(bf16[256,2048]{1,0:T(8,128)(2,1)} %get-tuple-element.86) | copy-start | bytes 3145732
  634.3 15.9 %copy-start.10 = (bf16[256,2048]{1,0:T(8,128)(2,1)S(1)}, bf16[256,2048]{1,0:T(8,128)(2,1)}, u32[]{:S(2)}) copy-start(bf16[256,2048]{1,0:T(8,128)(2,1)} %get-tuple-element.87) | copy-start | bytes 3145732
  634.3 15.9 %copy-start.11 = (bf16[256,2048]{1,0:T(8,128)(2,1)S(1)}, bf16[256,2048]{1,0:T(8,128)(2,1)}, u32[]{:S(2)}) copy-start(bf16[256,2048]{1,0:T(8,128)(2,1)} %get-tuple-element.92) | copy-start | bytes 3145732
  637.0 13.3 %copy-start.2 = (f32[256,2048]{1,0:T(8,128)S(1)}, f32[256,2048]{1,0:T(8,128)}, u32[]{:S(2)}) copy-start(f32[256,2048]{1,0:T(8,128)} %get-tuple-element.82) | copy-start | bytes 6291460
  637.0 13.3 %copy-start.5 = (f32[256,2048]{1,0:T(8,128)S(1)}, f32[256,2048]{1,0:T(8,128)}, u32[]{:S(2)}) copy-start(f32[256,2048]{1,0:T(8,128)} %get-tuple-element.99) | copy-start | bytes 6291460
  (4 other events, 7.6 us)

commit v5 on v4

--- a/solution.py
+++ b/solution.py
@@ -1517,6 +1517,11 @@
         fill()
     for s in pending:
         cargo.middle(s)
+    if more and made:
+        store(len(made) - 1, 2).wait()
+        store(len(made) - 1, 3).wait()
+    if cargo:
+        cargo.end()
 
     share(ctx).wait_recv()
 
@@ -1564,12 +1569,6 @@
         def _():
             for chunk in range(CHUNKS):
                 hop(1, slot, chunk, slot - 1 - away).wait_send()
-
-    if more and made:
-        store(len(made) - 1, 2).wait()
-        store(len(made) - 1, 3).wait()
-    if cargo:
-        cargo.end()
 
 
 def team_sum(ctxs, number, pairs, name, freight=(), other=None, outer=False):
@@ -1721,10 +1720,10 @@
                 return carry
 
             lax.fori_loop(0, size // 64, group, 0)
+    cargo.end()
     for i, (dc, dz) in enumerate(partners):
         c, z = core if dc == 0 else 1 - core, lax.rem(ctx + ctxs - dz, ctxs)
         piece(i, c, z, c * ctxs + z).wait_recv()
-    cargo.end()
     pass_on.wait()
     for i, step in enumerate(partners):
         c, z = partner(*step)
@@ -2348,9 +2347,8 @@
     gain_part = jnp.pad(gain_part, ((0, 0), (0, 0), (0, 6), (0, 128 - gcols)))
     gain_grad = small_sum(planes, ctxs, gain_part)
     if square:
-        gain_grad, proj_sum = lax.optimization_barrier((gain_grad, proj_sum))
+        gain_grad, last_out, proj_sum = lax.optimization_barrier((gain_grad, joined[2], proj_sum))
         proj_sum = line_reduce(proj_sum.reshape(ctxs, arows, D), ctxs)
-        proj_sum, last_out = lax.optimization_barrier((proj_sum, joined[2]))
         output = middle_own + joined[3].astype(F32) + first_out.astype(F32)
         output = output + second_out.astype(F32) + shifted(last_out, "ctx", 4, 3).astype(F32)
         output = output.astype(BF)

time: 663 us -> 671 us (1.012)
  waiting for transfers between devices: 17.2 us -> 26 us
    ppermute x4, waiting for transfers between devices: 17.2 us -> 26 us  [shifted(): lax.ppermute(value, axis, [(i, (i + step) % size) for i in range(size)])]
  transfers between devices with their start and end apart: 4 -> 4, of which waited for: 2 -> 1; matrix products, arithmetic and copies ran while one was open for 5% -> 5% of each run, Pallas kernels for 0% -> 0%
where the time goes in v5:
time: 671 us; the launch traced here: 664 us
  Pallas kernels  570 us (85%)
  other arithmetic  38.3 us (6%)
  waiting for transfers between devices  26 us (4%)
  local copies, waits for them, and re-layouts  22.3 us (3%)
    pallas_call x2, Pallas kernels, team_sum(): pl.pallas_call(kernel, out_shape=[jax.ShapeDtypeStruct((own, D), F32)] +...  162 us
    pallas_call x1, Pallas kernels, second_call(): pl.pallas_call(kernel, out_shape=[jax.ShapeDtypeStruct(shape, BF) for sha...  105 us
    pallas_call x1, Pallas kernels, third_call(): pl.pallas_call(kernel, out_shape=[jax.ShapeDtypeStruct((own, D), F32)] +...  94.9 us
    pallas_call x1, Pallas kernels, front_call(): pl.pallas_call(kernel, out_shape=[jax.ShapeDtypeStruct(shape, BF) for sha...  79.6 us
    pallas_call x1, Pallas kernels, attend_back_call(): pl.pallas_call(kernel, grid=(2, pairs), out_shape=[out, out, out] + Cargo...  58.1 us
    pallas_call x1, Pallas kernels, middle_call(): pl.pallas_call(kernel, out_shape=[jax.ShapeDtypeStruct((team, own, feats)...  56.4 us
    ppermute x4, waiting for transfers between devices, shifted(): lax.ppermute(value, axis, [(i, (i + step) % size) for i in range(size)])  26 us
    sub x3, other arithmetic, adam_update(): return (first_new, second_new, master - rate * (direction + decay * master))  23.3 us
  transfers between devices with their start and end apart: 4, of which 1 were waited for; matrix products, arithmetic and copies ran while one was open for 5% of the time, Pallas kernels for 0%

profile of v5, /device:TPU:24, one launch (start us, length us, event | category | flops | bytes accessed | tf_op | source)
XLA Modules:
  0.0 664.4 jit_solution(5940282330671683669)
XLA Ops:
  0.7 2.8 copy.62
  6.6 79.6 %front.1 = (bf16[8,256,2048]{2,1,0:T(8,128)(2,1)}, bf16[8,256,2048]{2,1,0:T(8,128)(2,1)}, bf16[8,256,256]{2,1,0:T(8,128)(2,1)}, bf16[8,256,256]{2,1,0:T(8,128)(2...) custom-call(bf16[256,2048]{1,0:T(8,128)(2,1)} %refs_0_.1, ...), custom_call_target="tpu_custom_call" | custom-call | flops 6442450944 | bytes 20971520 | tf_op jit(solution)/shard_map/front/pallas_call | solution.py:826
  89.9 104.8 %second.1 = (bf16[8,2048,256]{2,1,0:T(8,128)(2,1)}, bf16[8,4,64,2048]{3,2,1,0:T(8,128)(2,1)}, bf16[4,256,2048]{2,1,0:T(8,128)(2,1)}, f32[8,1024,1]{2,1,0:T(8,128)}) custom-call(bf16[2048,256]{1,0:T(8,128)(2,1)} %bitcast.67, bf16[2048,256]{1,0:T(8,128)(2,1)} %bitcast.69, bf16[2048,256]{1,0:T(8,128)(2,1)} %bitcast.71, f32[2048,1]{1,0:T(8,128)} %copy.46.refs_3_.refs_5_, ...), custom_call_target="tpu_custom_call" | custom-call | flops 2147483648 | bytes 12582912 | tf_op jit(solution)/shard_map/second/pallas_call | solution.py:976
  194.6 94.9 %third.1 = (f32[256,2048]{1,0:T(8,128)}, bf16[256,2048]{1,0:T(8,128)(2,1)}, bf16[8,256,2048]{2,1,0:T(8,128)(2,1)}, bf16[8,256,2048]{2,1,0:T(8,128)(2,1)}, bf16[8...) custom-call(bf16[8,2048,256]{2,1,0:T(8,128)(2,1)} %get-tuple-element.71.refs_0_, ...), custom_call_target="tpu_custom_call" | custom-call | flops 60129542144 | bytes 15728640 | tf_op jit(solution)/shard_map/third/pallas_call | solution.py:1181
  289.6 1.8 multiply_reduce_fusion.2
  291.4 82.8 %sum_two.1 = (f32[256,2048]{1,0:T(8,128)}, f32[256,2048]{1,0:T(8,128)}, bf16[1,4,256,2048]{3,2,1,0:T(8,128)(2,1)}, bf16[1,4,256,2048]{3,2,1,0:T(8,128)(2,1)}) custom-call(bf16[2048,1024]{1,0:T(8,128)(2,1)} %bitcast.100, bf16[2048,1024]{1,0:T(8,128)(2,1)} %bitcast.101, bf16[1024,2048]{1,0:T(8,128)(2,1)} %bitcast.99, bf16[1024,2048]{1,0:T(8,128)(2,1)} %bitcast.94, ...), custom_call_target="tpu_custom_call" | custom-call | flops 17179869184 | bytes 18874368 | tf_op jit(solution)/shard_map/sum_two/pallas_call | solution.py:1607
  374.3 2.3 multiply_reduce_fusion.1
  376.8 1.7 fusion.19.refs_0_
  379.0 1.8 fusion.24
  380.8 56.4 %middle.1 = (bf16[8,256,256]{2,1,0:T(8,128)(2,1)}, bf16[4,4,64,2048]{3,2,1,0:T(8,128)(2,1)}, bf16[256,2048]{1,0:T(8,128)(2,1)}, bf16[256,2048]{1,0:T(8,128)(2,1)...) custom-call(bf16[256,2048]{1,0:T(8,128)(2,1)} %fusion.19.refs_0_, ...), custom_call_target="tpu_custom_call" | custom-call | flops 4294967296 | bytes 31457280 | tf_op jit(solution)/shard_map/middle/pallas_call | solution.py:1747
  437.2 58.1 %attend_back.1 = (bf16[2048,256]{1,0:T(8,128)(2,1)}, bf16[2048,256]{1,0:T(8,128)(2,1)}, bf16[2048,256]{1,0:T(8,128)(2,1)}, f32[256,2048]{1,0:T(8,128)}, bf16[256,2048]{1,0:T(8,128)(2,1)}) custom-call(bf16[2048,256]{1,0:T(8,128)(2,1)} %bitcast.68, bf16[2048,256]{1,0:T(8,128)(2,1)} %bitcast.70, bf16[2048,256]{1,0:T(8,128)(2,1)} %bitcast.72, ...), custom_call_target="tpu_custom_call" | custom-call | flops 5368709120 | bytes 7340032 | tf_op jit(solution)/shard_map/attend_back/pallas_call | solution.py:1974
  495.3 79.0 %sum_one.1 = (f32[256,2048]{1,0:T(8,128)}, f32[256,2048]{1,0:T(8,128)}, f32[64,2048]{1,0:T(8,128)}, f32[64,2048]{1,0:T(8,128)}, f32[64,2048]{1,0:T(8,128)}) custom-call(bf16[2048,256]{1,0:T(8,128)(2,1)} %get-tuple-element.92.refs_0_, bf16[2048,256]{1,0:T(8,128)(2,1)} %get-tuple-element.93.refs_1_, bf16[2048,256]{1,0:T(8,128)(2,1)} %get-tuple-element.94.refs_2_, ...), custom_call_target="tpu_custom_call" | custom-call | flops 6442450944 | bytes 8388608 | tf_op jit(solution)/shard_map/sum_one/pallas_call | solution.py:1607
  574.3 2.2 fusion.10
  577.3 14.5 %small_sum.1 = f32[8,128]{1,0:T(8,128)} custom-call(f32[4,8,8,128]{3,2,1,0:T(8,128)} %pad.6.value_ref), custom_call_target="tpu_custom_call" | custom-call | tf_op jit(solution)/shard_map/small_sum/pallas_call | solution.py:459
  591.9 2.3 fusion.15
  594.1 3.0 collective-permute-start.1
  598.3 2.3 collective-permute-start
  600.6 14.8 %multiply_subtract_fusion = (f32[256,3,2048]{2,0,1:T(8,128)}, f32[256,3,2048]{2,0,1:T(8,128)}, f32[256,3,2048]{2,0,1:T(8,128)}) fusion(f32[256,3,2048]{2,0,1:T(8,128)} %param.25, f32[3]{0:T(128)S(1)} %copy-done.23, f32[256,1,2048]{2,0,1:T(8,128)} %bitcast.64, f32[256,1,2048]{2,0,1:T(8,128)} %bitcast.66, f32[256,1,2048]{2,0,1:T(8,128)} %bitcast.65, ...), kind=kLoop, calls=%fused_computation.3 | loop fusion | flops 26738688 | bytes 44040204 | tf_op jit(solution)/shard_map/sub | solution.py:102
  616.8 26.0 %collective-permute-done.2 = bf16[64,2048]{1,0:T(8,128)(2,1)} collective-permute-done((bf16[64,2048]{1,0:T(8,128)(2,1)}, bf16[64,2048]{1,0:T(8,128)(2,1)}, u32[]{:S(2)}, u32[]{:S(2)}) %collective-permute-start.2) | collective-permute-done | bytes 262176 | tf_op jit(solution)/shard_map/ppermute | solution.py:2041
  642.8 1.4 fusion.14
  644.2 7.1 %multiply_subtract_fusion.1 = (f32[64,4,2048]{2,0,1:T(8,128)S(1)}, f32[64,4,2048]{2,0,1:T(8,128)S(1)}, f32[64,4,2048]{2,0,1:T(8,128)S(1)}) fusion(f32[64,4,2048]{2,1,0:T(4,128)} %param.22, f32[4]{0:T(128)S(1)} %copy-done.22, f32[64,1,2048]{2,0,1:T(8,128)S(1)} %fusion.14, f32[64,1,2048]{2,0,1:T(8,128)S(1)} %bitcast.80, f32[64,1,2048]{2,0,1:T(8,128)S(1)} %bitcast.79, ...), kind=kLoop, calls=%fused_computation.24 | loop fusion | flops 9437184 | bytes 14680080 | tf_op jit(solution)/shard_map/sub | solution.py:102
  651.3 2.7 copy.52
  654.0 2.7 copy.53
  659.7 4.5 fusion.9
  (75 shorter events, 14.0 us)
Async XLA Ops:
  0.6 4.5 copy-start.17
  0.7 4.5 copy-start.3
  3.5 2.5 copy-start.21
  87.0 2.9 copy-start.16
  291.4 82.9 %copy-start = (f32[256,2048]{1,0:T(8,128)S(1)}, f32[256,2048]{1,0:T(8,128)}, u32[]{:S(2)}) copy-start(f32[256,2048]{1,0:T(8,128)} %get-tuple-element.76) | copy-start | bytes 6291460
  291.4 82.9 %copy-start.15 = (f32[1,4,4,128]{3,0,2,1:T(1,128)S(1)}, f32[1,4,4,128]{3,0,2,1:T(1,128)}, u32[]{:S(2)}) copy-start(f32[1,4,4,128]{3,0,2,1:T(1,128)} %get-tuple-element.168) | copy-start | bytes 24580
  374.3 2.5 copy-start.6
  495.3 79.0 %copy-start.4 = (bf16[256,2048]{1,0:T(8,128)(2,1)S(1)}, bf16[256,2048]{1,0:T(8,128)(2,1)}, u32[]{:S(2)}) copy-start(bf16[256,2048]{1,0:T(8,128)(2,1)} %refs_0_.1) | copy-start | bytes 3145732
  574.3 26.3 %copy-start.23 = (f32[3]{0:T(128)S(1)}, f32[3]{0:T(128)}, u32[]{:S(2)}) copy-start(f32[3]{0:T(128)} %constant.141) | copy-start | bytes 40
  594.1 22.7 %collective-permute-start.1 = (bf16[64,2048]{1,0:T(8,128)(2,1)}, bf16[64,2048]{1,0:T(8,128)(2,1)}, u32[]{:S(2)}, u32[]{:S(2)}) collective-permute-start(bf16[64,2048]{1,0:T(8,128)(2,1)} %get-tuple-element.162), channel_id=1, source_target_pairs={{0,1},{1,2},{2,3},{3,0},{4,5},{5,6},{6,7},{7,4},{8,9},{9,10},{10,1... | collective-permute-start | bytes 786440 | tf_op jit(solution)/shard_map/ppermute | solution.py:2041
  597.1 45.7 %collective-permute-start.2 = (bf16[64,2048]{1,0:T(8,128)(2,1)}, bf16[64,2048]{1,0:T(8,128)(2,1)}, u32[]{:S(2)}, u32[]{:S(2)}) collective-permute-start(bf16[64,2048]{1,0:T(8,128)(2,1)} %get-tuple-element.164), channel_id=1, source_target_pairs={{0,2},{1,3},{2,0},{3,1},{4,6},{5,7},{6,4},{7,5},{8,10},{9,11},{10,... | collective-permute-start | bytes 786440 | tf_op jit(solution)/shard_map/ppermute | solution.py:2041
  597.1 45.7 %collective-permute-start.3 = (bf16[64,2048]{1,0:T(8,128)(2,1)S(1)}, bf16[64,2048]{1,0:T(8,128)(2,1)}, u32[]{:S(2)}, u32[]{:S(2)}) collective-permute-start(bf16[64,2048]{1,0:T(8,128)(2,1)S(1)} %get-tuple-element.163), channel_id=1, source_target_pairs={{0,3},{1,0},{2,1},{3,2},{4,7},{5,4},{6,5},{7,6},{8,11},{9,8},{10,9... | collective-permute-start | bytes 786440 | tf_op jit(solution)/shard_map/ppermute | solution.py:2041
  598.3 60.5 %collective-permute-start = (bf16[256,2048]{1,0:T(8,128)(2,1)}, bf16[256,2048]{1,0:T(8,128)(2,1)}, u32[]{:S(2)}, u32[]{:S(2)}) collective-permute-start(bf16[256,2048]{1,0:T(8,128)(2,1)} %get-tuple-element.101), channel_id=1, source_target_pairs={{0,3},{1,0},{2,1},{3,2},{4,7},{5,4},{6,5},{7,6},{8,11},{9,8},{10,9... | collective-permute-start | bytes 3145736 | tf_op jit(solution)/shard_map/ppermute | solution.py:2041
  600.6 14.8 %copy-start.19 = (f32[2,64]{1,0:T(2,128)S(1)}, f32[2,64]{1,0:T(2,128)}, u32[]{:S(2)}) copy-start(f32[2,64]{1,0:T(2,128)} %param.30) | copy-start | bytes 1540
  600.6 14.8 %copy-start.20 = (f32[2,64]{1,0:T(2,128)S(1)}, f32[2,64]{1,0:T(2,128)}, u32[]{:S(2)}) copy-start(f32[2,64]{1,0:T(2,128)} %param.29) | copy-start | bytes 1540
  600.6 43.6 %copy-start.22 = (f32[4]{0:T(128)S(1)}, f32[4]{0:T(128)}, u32[]{:S(2)}) copy-start(f32[4]{0:T(128)} %constant.140) | copy-start | bytes 52
  615.4 28.8 %copy-start.12 = (f32[64,2048]{1,0:T(8,128)S(1)}, f32[64,2048]{1,0:T(8,128)}, u32[]{:S(2)}) copy-start(f32[64,2048]{1,0:T(8,128)} %get-tuple-element.102) | copy-start | bytes 1572868
  615.4 28.8 %copy-start.13 = (f32[64,2048]{1,0:T(8,128)S(1)}, f32[64,2048]{1,0:T(8,128)}, u32[]{:S(2)}) copy-start(f32[64,2048]{1,0:T(8,128)} %get-tuple-element.103) | copy-start | bytes 1572868
  615.4 28.8 %copy-start.14 = (f32[64,2048]{1,0:T(8,128)S(1)}, f32[64,2048]{1,0:T(8,128)}, u32[]{:S(2)}) copy-start(f32[64,2048]{1,0:T(8,128)} %get-tuple-element.104) | copy-start | bytes 1572868
  654.0 4.8 copy-start.7
  654.0 4.8 copy-start.9
  654.0 4.8 copy-start.10
  654.0 4.8 copy-start.11
  656.7 3.0 copy-start.5
  (4 other events, 7.3 us)
